TPU v7x, 128 devices: a whole 4x4x4 slice. The times are simulated.
128 devices in a mesh: row: 8 (over z, core), col: 16 (over x, y).
Axes of the slice: x: 4, y: 4, z: 4, core: 2. Of those that a mesh axis runs over, the one named last changes fastest.
Arguments:
- layer_input: bfloat16 [1536, 6144], P('col', 'row'), may hold values from -6 to 6
- out_grad: bfloat16 [1536, 6144], P('col', 'row'), may hold values from -6 to 6
- preactivation: bfloat16 [1536, 24576], P('row', 'col'), may hold values from -8 to 8
- weight_in: bfloat16 [6144, 24576], P('row', 'col'), may hold values from -0.078125 to 0.078125
- weight_out: bfloat16 [24576, 6144], P('col', 'row'), may hold values from -0.0390625 to 0.0390625
Outputs:
- input_grad: bfloat16 [1536, 6144], P('col', 'row')
- weight_in_grad: float32 [6144, 24576], P('row', 'col')
- weight_out_grad: float32 [24576, 6144], P('col', 'row')
All inputs are finite; a program needn't handle non-finite values.
Results may differ from a plain program's by a relative error of at most 0.0049.
Values may be sent and summed in bfloat16 or wider, within the bound.
No kernel may reach another device: no remote copies, remote signals or barrier semaphores. Data moves between devices by JAX's collectives and lax.ppermute only.
A program may use at most 128 MiB of HBM per device.

v0:
```python
import jax
import jax.numpy as jnp
from jax import lax
from jax.sharding import PartitionSpec as P

coeff = 0.7978845608
cubic = 0.044715


def gelu_parts(before):
    inner = coeff * (before + cubic * before * before * before)
    tanh_value = jnp.tanh(inner)
    value = 0.5 * before * (1.0 + tanh_value)
    slope = 0.5 * (1.0 + tanh_value) + 0.5 * before * (1.0 - tanh_value * tanh_value) * coeff * (
        1.0 + 3.0 * cubic * before * before
    )
    return (value, slope)


def on_device(layer_input, out_grad, preactivation, weight_in, weight_out):
    inputs_all, grads_all = (
        lax.all_gather(layer_input, "col", axis=0, tiled=True),
        lax.all_gather(out_grad, "col", axis=0, tiled=True),
    )
    block = grads_all
    act_grad = lax.psum_scatter(
        lax.dot_general(
            block, weight_out, (((1,), (1,)), ((), ())), preferred_element_type=jnp.float32
        ),
        "row",
        scatter_dimension=0,
        tiled=True,
    )
    value, slope = gelu_parts(preactivation.astype(jnp.float32))
    activation = value.astype(jnp.bfloat16)
    hidden_grad = (act_grad * slope).astype(jnp.bfloat16)
    act_all, hidden_all = (
        lax.all_gather(activation, "row", axis=0, tiled=True),
        lax.all_gather(hidden_grad, "row", axis=0, tiled=True),
    )
    weight_out_grad = lax.dot_general(
        act_all, grads_all, (((0,), (0,)), ((), ())), preferred_element_type=jnp.float32
    )
    weight_in_grad = lax.dot_general(
        inputs_all, hidden_all, (((0,), (0,)), ((), ())), preferred_element_type=jnp.float32
    )
    block = hidden_all
    input_grad = lax.psum_scatter(
        lax.dot_general(
            block, weight_in, (((1,), (1,)), ((), ())), preferred_element_type=jnp.float32
        ),
        "col",
        scatter_dimension=0,
        tiled=True,
    ).astype(jnp.bfloat16)
    return (input_grad, weight_in_grad, weight_out_grad)


def solution(mesh):
    placed = (P("col", "row"), P("col", "row"), P("row", "col"), P("row", "col"), P("col", "row"))
    return jax.shard_map(
        on_device,
        mesh=mesh,
        in_specs=placed,
        out_specs=(P("col", "row"), P("row", "col"), P("col", "row")),
        check_vma=False,
    )
```

profile of v0, /device:TPU:1, one launch (start us, length us, event | category | flops | bytes accessed | tf_op | source)
XLA Modules:
  0.0 332.5 jit_solution(9921423647957840702)
XLA Ops:
  7.2 0.0 copy-start
  7.2 0.0 all-gather.5.cloned.1.call-start
  7.2 0.7 all-gather.5.cloned.1.call-update
  7.9 0.0 reduce-scatter.3.cloned.1.call-start
  8.0 50.1 %all-gather.5.cloned.1.call-done = bf16[1536,768]{1,0:T(8,128)(2,1)} async-done(((bf16[96,768]{1,0:T(8,128)(2,1)}), bf16[1536,768]{1,0:T(8,128)(2,1)}) %all-gather.5.cloned.1.call-update) | async-done | bytes 2359312 | tf_op jit(solution)/shard_map/all_gather | solution.py:23
  58.1 0.0 copy-done
  58.1 8.1 %fusion.11 = f32[1536,1536]{1,0:T(8,128)} fusion(bf16[1536,768]{1,0:T(8,128)(2,1)} %all-gather.5.cloned.1.call-done, bf16[1536,768]{1,0:T(8,128)(2,1)S(1)} %copy-done), kind=kOutput, calls=%fused_computation.19 | convolution fusion | flops 3623878656 | bytes 14155776 | tf_op jit(solution)/shard_map/dot_general | solution.py:27
  66.1 0.0 copy-start.1
  66.2 0.0 reduce-scatter.3.cloned.1.call-update
  66.2 0.0 all-gather.7.cloned.1.call-start
  66.2 57.3 %reduce-scatter.3.cloned.1.call-done = f32[192,1536]{1,0:T(8,128)} async-done(((f32[1536,1536]{1,0:T(8,128)}), f32[192,1536]{1,0:T(8,128)}) %reduce-scatter.3.cloned.1.call-update) | async-done | bytes 1179664 | tf_op jit(solution)/shard_map/reduce_scatter | solution.py:26
  123.5 0.0 copy-done.1
  123.5 3.1 fusion.7
  126.7 0.0 all-gather.7.cloned.1.call-update
  126.7 0.0 all-gather.9.cloned.1.call-start
  126.7 0.5 all-gather.9.cloned.1.call-update
  127.3 0.0 all-gather.11.cloned.1.call-start
  127.3 0.5 all-gather.11.cloned.1.call-update
  127.9 0.2 reduce-scatter.5.cloned.1.call-start
  128.1 33.9 %all-gather.7.cloned.1.call-done = bf16[1536,1536]{1,0:T(8,128)(2,1)} async-done(((bf16[192,1536]{1,0:T(8,128)(2,1)}), bf16[1536,1536]{1,0:T(8,128)(2,1)}) %all-gather.7.cloned.1.call-update) | async-done | bytes 4718608 | tf_op jit(solution)/shard_map/all_gather | solution.py:39
  162.0 9.2 %fusion.12 = f32[1536,768]{1,0:T(8,128)} fusion(bf16[1536,1536]{1,0:T(8,128)(2,1)} %all-gather.7.cloned.1.call-done, bf16[768,1536]{1,0:T(8,128)(2,1)} %param.8), kind=kOutput, calls=%fused_computation.20 | convolution fusion | flops 3623878656 | bytes 11796480 | tf_op jit(solution)/shard_map/dot_general | solution.py:49
  171.1 0.0 reduce-scatter.5.cloned.1.call-update
  171.1 37.0 %all-gather.9.cloned.1.call-done = bf16[1536,768]{1,0:T(8,128)(2,1)} async-done(((bf16[96,768]{1,0:T(8,128)(2,1)}), bf16[1536,768]{1,0:T(8,128)(2,1)}) %all-gather.9.cloned.1.call-update) | async-done | bytes 2359312 | tf_op jit(solution)/shard_map/all_gather | solution.py:22
  208.1 9.2 %convolution_bitcast_fusion = f32[768,1536]{0,1:T(8,128)} fusion(bf16[1536,1536]{1,0:T(8,128)(2,1)} %all-gather.7.cloned.1.call-done, bf16[1536,768]{1,0:T(8,128)(2,1)} %all-gather.9.cloned.1.call-done), kind=kOutput, calls=%fused_computation | convolution fusion | flops 3623878656 | bytes 11796480 | tf_op jit(solution)/shard_map/dot_general | solution.py:44
  217.3 6.2 %copy.8 = f32[768,1536]{1,0:T(8,128)} copy(f32[768,1536]{0,1:T(8,128)} %convolution_bitcast_fusion) | data formatting | bytes 9437184
  223.5 21.5 %all-gather.11.cloned.1.call-done = bf16[1536,1536]{1,0:T(8,128)(2,1)} async-done(((bf16[192,1536]{1,0:T(8,128)(2,1)}), bf16[1536,1536]{1,0:T(8,128)(2,1)}) %all-gather.11.cloned.1.call-update) | async-done | bytes 4718608 | tf_op jit(solution)/shard_map/all_gather | solution.py:38
  244.9 9.2 %fusion.13 = f32[1536,768]{1,0:T(8,128)} fusion(bf16[1536,1536]{1,0:T(8,128)(2,1)} %all-gather.11.cloned.1.call-done, bf16[1536,768]{1,0:T(8,128)(2,1)} %all-gather.5.cloned.1.call-done), kind=kOutput, calls=%fused_computation.21 | convolution fusion | flops 3623878656 | bytes 11796480 | tf_op jit(solution)/shard_map/dot_general | solution.py:41
  254.1 69.9 %reduce-scatter.5.cloned.1.call-done = f32[96,768]{1,0:T(8,128)} async-done(((f32[1536,768]{1,0:T(8,128)}), f32[96,768]{1,0:T(8,128)}) %reduce-scatter.5.cloned.1.call-update) | async-done | bytes 294928 | tf_op jit(solution)/shard_map/reduce_scatter | solution.py:48
  324.0 1.6 convert_element_type.14
Async XLA Ops:
  7.2 50.9 %copy-start = (bf16[1536,768]{1,0:T(8,128)(2,1)S(1)}, bf16[1536,768]{1,0:T(8,128)(2,1)}, u32[]{:S(2)}) copy-start(bf16[1536,768]{1,0:T(8,128)(2,1)} %param.9) | copy-start | bytes 7077892
  7.2 50.9 %all-gather.5.cloned.1.call-start = ((), (), s32[]{:S(2)}) async-start(), calls=%async_computation.2 | async-start | bytes 2506752 | tf_op jit(solution)/shard_map/all_gather | solution.py:23
  7.9 115.6 %reduce-scatter.3.cloned.1.call-start = ((), (), s32[]{:S(2)}) async-start(), calls=%async_computation.3 | async-start | bytes 10616832 | tf_op jit(solution)/shard_map/reduce_scatter | solution.py:26
  66.1 57.4 %copy-start.1 = (bf16[192,1536]{1,0:T(8,128)(2,1)S(1)}, bf16[192,1536]{1,0:T(8,128)(2,1)}, u32[]{:S(2)}) copy-start(bf16[192,1536]{1,0:T(8,128)(2,1)} %param.7) | copy-start | bytes 1769476
  66.2 95.8 %all-gather.7.cloned.1.call-start = ((), (), s32[]{:S(2)}) async-start(), calls=%async_computation.4 | async-start | bytes 5308416 | tf_op jit(solution)/shard_map/all_gather | solution.py:39
  126.7 81.4 %all-gather.9.cloned.1.call-start = ((), (), s32[]{:S(2)}) async-start(), calls=%async_computation.6 | async-start | bytes 2506752 | tf_op jit(solution)/shard_map/all_gather | solution.py:22
  127.3 117.6 %all-gather.11.cloned.1.call-start = ((), (), s32[]{:S(2)}) async-start(), calls=%async_computation.7 | async-start | bytes 5308416 | tf_op jit(solution)/shard_map/all_gather | solution.py:38
  127.9 196.2 %reduce-scatter.5.cloned.1.call-start = ((), (), s32[]{:S(2)}) async-start(), calls=%async_computation.5 | async-start | bytes 5013504 | tf_op jit(solution)/shard_map/reduce_scatter | solution.py:48
Sparse Core Ops, SparseCore 0:
  10.2 47.8 all-gather.4
  66.3 57.1 reduce-scatter.2
  126.8 35.1 all-gather.6
  164.0 44.0 all-gather.8
  209.6 35.2 all-gather.10
  248.1 75.8 reduce-scatter.4
where the time goes:
time: 334 us; the launch traced here: 333 us
  waiting for transfers between devices  271 us (81%)
  matrix products  35.6 us (11%)
  between operations  14.1 us (4%)
  local copies, waits for them, and re-layouts  6.18 us (2%)
  other arithmetic  4.76 us (1%)
    reduce_scatter x1, waiting for transfers between devices, on_device(): lax.psum_scatter(lax.dot_general(block, weight_in, (((1,), (1,)), ((), ()...  69.9 us
    reduce_scatter x1, waiting for transfers between devices, on_device(): lax.psum_scatter(lax.dot_general(block, weight_out, (((1,), (1,)), ((), (...  57.3 us
    all_gather x1, waiting for transfers between devices, on_device(): lax.all_gather(out_grad, 'col', axis=0, tiled=True)  50.1 us
    all_gather x1, waiting for transfers between devices, on_device(): lax.all_gather(layer_input, 'col', axis=0, tiled=True)  37 us
    all_gather x1, waiting for transfers between devices, on_device(): lax.all_gather(hidden_grad, 'row', axis=0, tiled=True)  33.9 us
    all_gather x1, waiting for transfers between devices, on_device(): lax.all_gather(activation, 'row', axis=0, tiled=True)  21.5 us
    dot_general x1, matrix products, on_device(): lax.dot_general(act_all, grads_all, (((0,), (0,)), ((), ())), preferred_e...  9.19 us
    dot_general x1, matrix products, on_device(): lax.dot_general(inputs_all, hidden_all, (((0,), (0,)), ((), ())), preferr...  9.19 us
  transfers between devices with their start and end apart: 6, of which 6 were waited for; matrix products, arithmetic and copies ran while one was open for 10% of the time, Pallas kernels for 0%

commit v1 on v0

v1 whole, which is shorter than its diff:
```python
import jax
import jax.numpy as jnp
from jax import lax
from jax.experimental import pallas as pl
from jax.experimental.pallas import tpu as pltpu
from jax.sharding import PartitionSpec as P

coeff = 0.7978845608
cubic = 0.044715

N = 4
K = 48
VMEM = 56 * 2**20
LIGHT = pl.CostEstimate(flops=1024, bytes_accessed=1024, transcendentals=0)
AXES = ("row", "col")
BF = jnp.bfloat16
F32 = jnp.float32


def permute(array, target):
    pairs = []
    for z in range(N):
        for c in range(2):
            for x in range(N):
                for y in range(N):
                    tz, tc, tx, ty = target(z, c, x, y)
                    to = (((tz % N) * 2 + tc) * N + tx % N) * N + ty % N
                    pairs.append((((z * 2 + c) * N + x) * N + y, to))
    return lax.ppermute(array, AXES, pairs)


def swap(array):
    return permute(array, lambda z, c, x, y: (z, 1 - c, x, y))


def along_z(array, by):
    return permute(array, lambda z, c, x, y: (z + by, c, x, y))


def first_ring(array, by):
    return permute(array, lambda z, c, x, y: (z, c, x, y + by) if c else (z, c, x + by, y))


def second_ring(array, by):
    return permute(array, lambda z, c, x, y: (z, c, x + by, y) if c else (z, c, x, y + by))


def gelu_parts(before):
    inner = coeff * (before + cubic * before * before * before)
    tanh_value = jnp.tanh(inner)
    value = 0.5 * before * (1.0 + tanh_value)
    slope = 0.5 * (1.0 + tanh_value) + 0.5 * before * (1.0 - tanh_value * tanh_value) * coeff * (
        1.0 + 3.0 * cubic * before * before
    )
    return (value, slope)


def gather_z(block):
    below = along_z(block, 1)
    above = along_z(block, -1)
    far_a = along_z(below[:2], 1)
    far_b = along_z(above[2:], -1)
    return [block, above, far_a, far_b, below]


def place_xy(where, core, q, r):
    dx = jnp.where(core == 0, r, q)
    dy = jnp.where(core == 0, q, r)
    return ((where[2] + dx) % N, (where[3] + dy) % N)


def dot_nt(a, b):
    return lax.dot_general(a, b, (((1,), (1,)), ((), ())), preferred_element_type=F32)


def dot_tn(a, b):
    return lax.dot_general(a, b, (((0,), (0,)), ((), ())), preferred_element_type=F32)


ANY = pl.BlockSpec(memory_space=pl.ANY)
STEPS = 3


def act_grad_kernel(where, *refs):
    own, other, weights = refs[0:4], refs[4:8], refs[8:10]
    outs = refs[10:14]
    lhs, w, p0, p1, in_sems, w_sems, out_sems = refs[14:]
    rows = w.shape[1] // STEPS
    loads = []
    for j in range(STEPS):
        part = pl.ds(j * rows, rows)
        for half in range(2):
            loads.append(pltpu.make_async_copy(weights[half].at[part], w.at[half, part], w_sems.at[j, half]))
    fills = []
    mine = pl.ds(pl.multiple_of(where[1] * K, 16), K)
    for half, stacks in enumerate((own, other)):
        for q, stack in enumerate(stacks):
            for r in range(N):
                x, y = place_xy(where, where[1] if half == 0 else 1 - where[1], q, r)
                to = lhs.at[half, (x + N - where[0]) % N, y]
                fills.append(pltpu.make_async_copy(stack.at[r, mine], to, in_sems.at[half, q, r]))
    for copy in loads[:2] + fills + loads[2:]:
        copy.start()
    for copy in fills:
        copy.wait()
    stores = []
    for j in range(STEPS):
        loads[2 * j].wait()
        loads[2 * j + 1].wait()
        part = pl.ds(j * rows, rows)
        total = dot_nt(lhs[0].reshape(16 * K, -1), w[0, part]) + dot_nt(lhs[1].reshape(16 * K, -1), w[1, part])
        p0[:, part] = total[: N * K]
        for r in (1, 2, 3):
            p1[r - 1, :, part] = total[r * N * K : (r + 1) * N * K].astype(BF)
        for r in range(N):
            source = p0.at[:, part] if r == 0 else p1.at[r - 1, :, part]
            stores.append(pltpu.make_async_copy(source, outs[r].at[:, part], out_sems.at[j, r]))
            stores[-1].start()
    for copy in stores:
        copy.wait()


def act_grad_parts(where, stacks, others, w_own, w_other):
    hidden, half = w_own.shape
    return pl.pallas_call(
        act_grad_kernel,
        out_shape=[jax.ShapeDtypeStruct((N * K, hidden), t) for t in (F32, BF, BF, BF)],
        grid_spec=pltpu.PrefetchScalarGridSpec(
            num_scalar_prefetch=1,
            grid=(),
            in_specs=[ANY] * 10,
            out_specs=[ANY] * 4,
            scratch_shapes=[
                pltpu.VMEM((2, N, N, K, half), BF),
                pltpu.VMEM((2, hidden, half), BF),
                pltpu.VMEM((N * K, hidden), F32),
                pltpu.VMEM((3, N * K, hidden), BF),
                pltpu.SemaphoreType.DMA((2, N, N)),
                pltpu.SemaphoreType.DMA((STEPS, 2)),
                pltpu.SemaphoreType.DMA((STEPS, N)),
            ],
        ),
        compiler_params=pltpu.CompilerParams(vmem_limit_bytes=VMEM),
        cost_estimate=LIGHT,
        name="act_grad",
    )(where, *stacks, *others, w_own, w_other)


def input_grad_kernel(where, h0, h1, h2a, h2b, h3, w_own, w_other, *refs):
    outs, (rows_out, lhs, w, near, far, in_sems, w_sems, out_sems) = refs[:4], refs[4:]
    n = h0.shape[1]
    half = w_own.shape[0]
    rows = half // STEPS
    loads = []
    for j in range(2 * STEPS):
        weight = (w_own, w_other)[j // STEPS]
        loads.append(
            pltpu.make_async_copy(
                weight.at[pl.ds(j % STEPS * rows, rows)], w.at[pl.ds(j * rows, rows)], w_sems.at[j]
            )
        )
    fills = []
    for zr in range(N):
        for y in range(N):
            if zr == 2:
                piece = (h2a, h2b)[y // 2].at[y % 2]
            else:
                piece = (h0, h1, None, h3)[zr].at[y]
            dx = (where[0] + zr + N - where[2]) % N
            dy = (y + N - where[3]) % N
            r = jnp.where(where[1] == 0, dx, dy)
            q = jnp.where(where[1] == 0, dy, dx)
            fills.append(pltpu.make_async_copy(piece, lhs.at[r, q], in_sems.at[zr, y]))
    for copy in loads[:1] + fills + loads[1:]:
        copy.start()
    for copy in fills:
        copy.wait()
    stores = [pltpu.make_async_copy(lhs, rows_out, out_sems.at[2 * STEPS, 0])]
    stores[0].start()
    for j in range(2 * STEPS):
        loads[j].wait()
        part = pl.ds(j * rows, rows)
        total = dot_nt(lhs[...].reshape(16 * n, -1), w[part]).reshape(N, N, n, -1)
        near[:, :, part] = total[0]
        for r in (1, 2, 3):
            far[r - 1, :, :, part] = total[r].astype(BF)
        for r in range(N):
            source = near.at[:, :, part] if r == 0 else far.at[r - 1, :, :, part]
            stores.append(pltpu.make_async_copy(source, outs[r].at[:, :, part], out_sems.at[j, r]))
            stores[-1].start()
    for copy in stores:
        copy.wait()


def input_grad_parts(where, pieces, w_own, w_other):
    half, hidden = w_own.shape
    n = pieces[0].shape[1]
    return pl.pallas_call(
        input_grad_kernel,
        out_shape=[jax.ShapeDtypeStruct((N, n, 2 * half), t) for t in (F32, BF, BF, BF)]
        + [jax.ShapeDtypeStruct((N, N, n, hidden), BF)],
        grid_spec=pltpu.PrefetchScalarGridSpec(
            num_scalar_prefetch=1,
            grid=(),
            in_specs=[ANY] * 7,
            out_specs=[ANY] * 5,
            scratch_shapes=[
                pltpu.VMEM((N, N, n, hidden), BF),
                pltpu.VMEM((2 * half, hidden), BF),
                pltpu.VMEM((N, n, 2 * half), F32),
                pltpu.VMEM((3, N, n, 2 * half), BF),
                pltpu.SemaphoreType.DMA((N, N)),
                pltpu.SemaphoreType.DMA((2 * STEPS,)),
                pltpu.SemaphoreType.DMA((2 * STEPS + 1, N)),
            ],
        ),
        compiler_params=pltpu.CompilerParams(vmem_limit_bytes=VMEM),
        cost_estimate=LIGHT,
        name="input_grad",
    )(where, *pieces, w_own, w_other)


def weight_out_grad_kernel(where, act, g0, g1, g2, g3, out, rhs, sems):
    @pl.when(pl.program_id(0) == 0)
    def _():
        work = []
        for q, stack in enumerate((g0, g1, g2, g3)):
            for r in range(N):
                x, y = place_xy(where, where[1], q, r)
                work.append(pltpu.make_async_copy(stack.at[r], rhs.at[x, y], sems.at[q, r]))
        for copy in work:
            copy.start()
        for copy in work:
            copy.wait()

    out[...] = dot_tn(act[...], rhs[...].reshape(32 * K, -1))


def weight_out_grad_of(where, act, stacks):
    tokens, hidden = act.shape
    width = stacks[0].shape[-1]
    block = 512
    return pl.pallas_call(
        weight_out_grad_kernel,
        out_shape=jax.ShapeDtypeStruct((hidden, width), F32),
        grid_spec=pltpu.PrefetchScalarGridSpec(
            num_scalar_prefetch=1,
            grid=(hidden // block,),
            in_specs=[pl.BlockSpec((tokens, block), lambda i, s: (0, i))] + [ANY] * 4,
            out_specs=pl.BlockSpec((block, width), lambda i, s: (i, 0)),
            scratch_shapes=[pltpu.VMEM((N, N, 2 * K, width), BF), pltpu.SemaphoreType.DMA((N, N))],
        ),
        compiler_params=pltpu.CompilerParams(vmem_limit_bytes=VMEM),
        cost_estimate=LIGHT,
        name="weight_out_grad",
    )(where, act, *stacks)


def weight_in_grad_kernel(where, inputs, hid_own, hid_other, out, lhs):
    @pl.when(pl.program_id(0) == 0)
    def _():
        for s in range(2):
            core = where[1] if s == 0 else 1 - where[1]
            for r in range(N):
                for q in range(N):
                    x, y = place_xy(where, core, q, r)
                    lhs[s, r, q] = inputs[x * N + y, core]

    rows = lhs[...].reshape(2, 16 * K, -1)
    out[...] = dot_tn(rows[0], hid_own[...]) + dot_tn(rows[1], hid_other[...])


def weight_in_grad_of(where, inputs, hid_own, hid_other):
    hidden = hid_own.shape[-1]
    width = inputs.shape[1]
    block = 512
    b = pl.BlockSpec((16 * K, block), lambda i, s: (0, i))
    return pl.pallas_call(
        weight_in_grad_kernel,
        out_shape=jax.ShapeDtypeStruct((width, hidden), F32),
        grid_spec=pltpu.PrefetchScalarGridSpec(
            num_scalar_prefetch=1,
            grid=(hidden // block,),
            in_specs=[pl.BlockSpec((16, 2, K, width), lambda i, s: (0, 0, 0, 0)), b, b],
            out_specs=pl.BlockSpec((width, block), lambda i, s: (0, i)),
            scratch_shapes=[pltpu.VMEM((2, N, N, K, width), BF)],
        ),
        compiler_params=pltpu.CompilerParams(vmem_limit_bytes=VMEM),
        cost_estimate=LIGHT,
        name="weight_in_grad",
    )(where, inputs.reshape(16, 2, K, width), hid_own.reshape(-1, hidden), hid_other.reshape(-1, hidden))


def on_device(layer_input, out_grad, preactivation, weight_in, weight_out):
    row, col = lax.axis_index("row"), lax.axis_index("col")
    core = row % 2
    where = jnp.stack([row // 2, core, col // N, col % N]).astype(jnp.int32)
    width = layer_input.shape[1]
    hidden = preactivation.shape[1]

    def mine_and_other(array, axis):
        mine = lax.dynamic_index_in_dim(array, core, axis, keepdims=False)
        other = lax.dynamic_index_in_dim(array, 1 - core, axis, keepdims=False)
        return mine, swap(other)

    def in_core_order(mine, received, axis):
        return jnp.where(
            core == 0,
            jnp.concatenate([mine, received], axis),
            jnp.concatenate([received, mine], axis),
        )

    hold = lax.optimization_barrier
    w_out_other, w_in_other = swap(weight_out), swap(weight_in)
    g_near = [first_ring(out_grad, -r) for r in (1, 3, 2)]
    w_out_other, preact = hold((w_out_other, preactivation))
    act = gelu_parts(preact.astype(F32))[0].astype(BF)
    act_all = lax.all_gather(act, "row", axis=0, tiled=True)

    g_near, w_out_other, w_in_other, preact = hold((g_near, w_out_other, w_in_other, preact))
    g_stack = jnp.stack([out_grad, g_near[0], g_near[2], g_near[1]])
    g_far = [second_ring(g_stack, -q) for q in (1, 3, 2)]
    h_set = in_core_order(*mine_and_other(preact.reshape(2, 2, K, hidden), 1), 0)
    slope = gelu_parts(h_set.astype(F32))[1]
    g_far, slope = hold((g_far, slope))
    g_stacks = [g_stack, g_far[0], g_far[2], g_far[1]]
    g_others = [swap(g) for g in g_stacks]

    p0, p1, p2, p3 = act_grad_parts(where, g_stacks, g_others, weight_out, w_out_other)
    x_late, g_stacks = hold((layer_input, g_stacks))
    x_all = lax.all_gather(x_late, "col", axis=0, tiled=True)
    weight_out_grad = weight_out_grad_of(where, act_all, g_stacks)
    s1, s3, s2, weight_out_grad = hold((along_z(p1, 1), along_z(p3, -1), along_z(p2, 2), weight_out_grad))

    act_grad = (p0 + s1.astype(F32) + s2.astype(F32) + s3.astype(F32)).reshape(N, K, hidden)
    pieces = gather_z((act_grad * slope).astype(BF))
    d0, d1, d2, d3, hid_own = input_grad_parts(where, pieces, weight_in, w_in_other)
    got = [first_ring(d, r) for r, d in ((1, d1), (3, d3), (2, d2))]
    weight_in_grad = weight_in_grad_of(where, x_all, hid_own, swap(hid_own))
    got, weight_in_grad = hold((got, weight_in_grad))

    e = d0 + got[0].astype(F32) + got[1].astype(F32) + got[2].astype(F32)
    total = e[0]
    for q in (1, 3, 2):
        total = total + second_ring(e[q].astype(BF), q).astype(F32)
    total = total.astype(BF)
    input_grad = in_core_order(total[:, :width], swap(total[:, width:]), 0)
    return (input_grad, weight_in_grad, weight_out_grad)


def solution(mesh):
    placed = (P("col", "row"), P("col", "row"), P("row", "col"), P("row", "col"), P("col", "row"))
    return jax.shard_map(
        on_device,
        mesh=mesh,
        in_specs=placed,
        out_specs=(P("col", "row"), P("row", "col"), P("col", "row")),
        check_vma=False,
    )
```

time: 334 us -> 173 us (0.52)
  waiting for transfers between devices: 271 us -> 62.6 us
  Pallas kernels: 0 us -> 41.8 us
  starting transfers between devices: 0.42 us -> 38.8 us
  matrix products: 35.6 us -> 0 us
  other arithmetic: 4.76 us -> 8.6 us
    all_gather x4 -> x2, waiting for transfers between devices: 142 us -> 0.02 us  [the longest x1 0.02 us: on_device(): act_all = lax.all_gather(act, 'row', axis=0, tiled=True)]
    reduce_scatter x2 -> x0, waiting for transfers between devices: 127 us -> none  [the longest x1 69.9 us: on_device(): lax.psum_scatter(lax.dot_general(block, weight_in, (((1,), (1,)), ((), ()...]
    ppermute x0 -> x28, waiting for transfers between devices: none -> 62.5 us  [permute(): return lax.ppermute(array, AXES, pairs)]
    pallas_call x0 -> x4, Pallas kernels: none -> 41.8 us  [the longest x1 13.4 us: input_grad_parts(): pl.pallas_call(input_grad_kernel, out_shape=[jax.ShapeDtypeStruct((N, n,...]
    ppermute x0 -> x28, starting transfers between devices: none -> 38.7 us  [permute(): return lax.ppermute(array, AXES, pairs)]
    dot_general x4 -> x0, matrix products: 35.6 us -> none  [the longest x1 9.19 us: on_device(): lax.dot_general(act_all, grads_all, (((0,), (0,)), ((), ())), preferred_e...]
    add x0 -> x2, other arithmetic: none -> 3.45 us  [the longest x1 2.12 us: gelu_parts(): 0.5 * (1.0 + tanh_value)]
  transfers between devices with their start and end apart: 6 -> 30, of which waited for: 6 -> 19; matrix products, arithmetic and copies ran while one was open for 10% -> 4% of each run, Pallas kernels for 0% -> 24%
where the time goes in v1:
time: 173 us
  waiting for transfers between devices  62.6 us (36%)
  Pallas kernels  41.8 us (24%)
  starting transfers between devices  38.8 us (22%)
  between operations  14.3 us (8%)
  other arithmetic  8.6 us (5%)
  local copies, waits for them, and re-layouts  6.99 us (4%)
    ppermute x28, waiting for transfers between devices, permute(): return lax.ppermute(array, AXES, pairs)  62.5 us
    ppermute x28, starting transfers between devices, permute(): return lax.ppermute(array, AXES, pairs)  38.7 us
    pallas_call x1, Pallas kernels, input_grad_parts(): pl.pallas_call(input_grad_kernel, out_shape=[jax.ShapeDtypeStruct((N, n,...  13.4 us
    pallas_call x1, Pallas kernels, weight_out_grad_of(): pl.pallas_call(weight_out_grad_kernel, out_shape=jax.ShapeDtypeStruct((hi...  10.1 us
    pallas_call x1, Pallas kernels, act_grad_parts(): pl.pallas_call(act_grad_kernel, out_shape=[jax.ShapeDtypeStruct((N * K, h...  9.2 us
    pallas_call x1, Pallas kernels, weight_in_grad_of(): pl.pallas_call(weight_in_grad_kernel, out_shape=jax.ShapeDtypeStruct((wid...  9.15 us
    unnamed x30, local copies, waits for them, and re-layouts  5.09 us
  transfers between devices with their start and end apart: 30, of which 19 were waited for; matrix products, arithmetic and copies ran while one was open for 4% of the time, Pallas kernels for 24%

profile of v1, /device:TPU:1, one launch (start us, length us, event | category | flops | bytes accessed | tf_op | source)
XLA Modules:
  0.0 173.0 jit_solution(3200801372699127433)
XLA Ops:
  7.2 0.0 all-gather.3.cloned.1.call-start
  7.2 1.5 collective-permute-start.3
  8.7 4.5 %collective-permute-done.3.refs_9_ = bf16[1536,768]{1,0:T(8,128)(2,1)} collective-permute-done((bf16[1536,768]{1,0:T(8,128)(2,1)}, bf16[1536,768]{1,0:T(8,128)(2,1)}, u32[]{:S(2)}, u32[]{:S(2)}) %collective-permute-start.3) | collective-permute-done | bytes 2359328 | tf_op jit(solution)/shard_map/ppermute | solution.py:29
  13.2 2.3 %fusion.1 = bf16[192,1536]{1,0:T(8,128)(2,1)} fusion(bf16[192,1536]{1,0:T(8,128)(2,1)} %param.7), kind=kLoop, calls=%fused_computation.13 | loop fusion | flops 2949120 | bytes 1179648 | tf_op jit(solution)/shard_map/convert_element_type | solution.py:317
  15.5 0.0 all-gather.5.cloned.1.call-start
  15.6 0.5 collective-permute-start.4
  16.0 2.8 %collective-permute-start = (bf16[96,768]{1,0:T(8,128)(2,1)S(1)}, bf16[96,768]{1,0:T(8,128)(2,1)S(1)}, u32[]{:S(2)}, u32[]{:S(2)}) collective-permute-start(bf16[96,768]{1,0:T(8,128)(2,1)S(1)} %copy-done.14), channel_id=1, source_target_pairs={{0,12},{1,13},{2,14},{3,15},{4,0},{5,1},{6,2},{7,3},{8,4},{9,5},{1... | collective-permute-start | bytes 442376 | tf_op jit(solution)/shard_map/ppermute | solution.py:29
  18.9 1.6 collective-permute-start.2
  20.5 0.5 collective-permute-done
  21.0 5.0 %collective-permute-done.1 = bf16[96,768]{1,0:T(8,128)(2,1)S(1)} collective-permute-done((bf16[96,768]{1,0:T(8,128)(2,1)S(1)}, bf16[96,768]{1,0:T(8,128)(2,1)S(1)}, u32[]{:S(2)}, u32[]{:S(2)}) %collective-permute-start.1) | collective-permute-done | bytes 147488 | tf_op jit(solution)/shard_map/ppermute | solution.py:29
  25.9 1.4 copy-done.4
  27.3 0.1 pad_maximum_fusion.refs_0_.g0
  27.4 2.4 %collective-permute-start.5 = (bf16[4,96,768]{2,1,0:T(8,128)(2,1)S(1)}, bf16[4,96,768]{2,1,0:T(8,128)(2,1)S(1)}, u32[]{:S(2)}, u32[]{:S(2)}) collective-permute-start(bf16[4,96,768]{2,1,0:T(8,128)(2,1)S(1)} %pad_maximum_fusion.refs_0_.g0), channel_id=1, source_target_pairs={{0,3},{1,0},{2,1},{3,2},{4,7},{5,4},{6,5},{7,6},{8,11},{9,8},{10,9... | collective-permute-start | bytes 1769480 | tf_op jit(solution)/shard_map/ppermute | solution.py:29
  29.8 1.6 collective-permute-start.7
  31.4 1.8 %dynamic-slice_bitcast_fusion.1 = (bf16[2,48,1536]{2,1,0:T(8,128)(2,1)}, bf16[2,48,1536]{2,1,0:T(8,128)(2,1)S(1)}) fusion(bf16[2,2,48,1536]{3,2,1,0:T(8,128)(2,1)} %bitcast.38, s32[]{:T(128)S(6)} %select_n.47, s32[]{:T(128)S(6)} %select_n.48), kind=kLoop, calls=%fused_computation.35 | loop fusion | bytes 1179656 | tf_op jit(solution)/shard_map/jit(dynamic_index_in_dim)/squeeze | solution.py:302
  33.2 2.3 %collective-permute-start.8 = (bf16[2,48,1536]{2,1,0:T(8,128)(2,1)S(1)}, bf16[2,48,1536]{2,1,0:T(8,128)(2,1)S(1)}, u32[]{:S(2)}, u32[]{:S(2)}) collective-permute-start(bf16[2,48,1536]{2,1,0:T(8,128)(2,1)S(1)} %get-tuple-element.77), channel_id=1, source_target_pairs={{0,16},{1,17},{2,18},{3,19},{4,20},{5,21},{6,22},{7,23},{8,24},{9,... | collective-permute-start | bytes 884744 | tf_op jit(solution)/shard_map/ppermute | solution.py:29
  35.6 1.6 collective-permute-done.8
  37.2 0.8 copy-done.13
  37.9 2.1 %fusion.10 = f32[4,48,1536]{2,1,0:T(8,128)S(1)} fusion(bf16[2,48,1536]{2,1,0:T(8,128)(2,1)} %copy-done.13, bf16[2,48,1536]{2,1,0:T(8,128)(2,1)} %get-tuple-element.76, pred[]{:T(512)S(6)} %eq.7), kind=kLoop, calls=%fused_computation.22 | loop fusion | flops 6193152 | bytes 1769473 | tf_op jit(solution)/shard_map/add | solution.py:52
  40.1 2.9 %collective-permute-done.5.refs_1_.g1 = bf16[4,96,768]{2,1,0:T(8,128)(2,1)S(1)} collective-permute-done((bf16[4,96,768]{2,1,0:T(8,128)(2,1)S(1)}, bf16[4,96,768]{2,1,0:T(8,128)(2,1)S(1)}, u32[]{:S(2)}, u32[]{:S(2)}) %collective-permute-start.5) | collective-permute-done | bytes 589856 | tf_op jit(solution)/shard_map/ppermute | solution.py:29
  43.0 3.5 %collective-permute-done.6.refs_3_.g3 = bf16[4,96,768]{2,1,0:T(8,128)(2,1)S(1)} collective-permute-done((bf16[4,96,768]{2,1,0:T(8,128)(2,1)S(1)}, bf16[4,96,768]{2,1,0:T(8,128)(2,1)S(1)}, u32[]{:S(2)}, u32[]{:S(2)}) %collective-permute-start.6) | collective-permute-done | bytes 589856 | tf_op jit(solution)/shard_map/ppermute | solution.py:29
  46.5 2.6 %collective-permute-start.10 = (bf16[4,96,768]{2,1,0:T(8,128)(2,1)S(1)}, bf16[4,96,768]{2,1,0:T(8,128)(2,1)}, u32[]{:S(2)}, u32[]{:S(2)}) collective-permute-start(bf16[4,96,768]{2,1,0:T(8,128)(2,1)S(1)} %collective-permute-done.5.refs_1_.g1), channel_id=1, source_target_pairs={{0,16},{1,17},{2,18},{3,19},{4,20},{5,21},{6,22},{7,23},{8,24},{9,... | collective-permute-start | bytes 1769480 | tf_op jit(solution)/shard_map/ppermute | solution.py:29
  49.0 0.1 collective-permute-start.11
  49.1 0.4 collective-permute-start.12
  49.5 0.6 pad_add_fusion.where
  50.1 0.7 collective-permute-done.10.refs_5_
  50.8 1.1 collective-permute-done.11.refs_6_
  51.9 0.8 collective-permute-done.12.refs_7_
  52.7 9.2 %act_grad.1 = (f32[192,1536]{1,0:T(8,128)}, bf16[192,1536]{1,0:T(8,128)(2,1)}, bf16[192,1536]{1,0:T(8,128)(2,1)}, bf16[192,1536]{1,0:T(8,128)(2,1)}) custom-call(s32[4]{0:T(128)} %pad_add_fusion.where, bf16[4,96,768]{2,1,0:T(8,128)(2,1)} %copy-done, bf16[4,96,768]{2,1,0:T(8,128)(2,1)} %copy-done.1, bf16[4,96,768]{2,1,0:T(8,128)(2,1)} %copy-done.3, ...), custom_call_target="tpu_custom_call" | custom-call | flops 1024 | bytes 1024 | tf_op jit(solution)/shard_map/act_grad/pallas_call | solution.py:125
  61.9 1.7 collective-permute-start.13
  63.6 2.0 %collective-permute-start.14 = (bf16[192,1536]{1,0:T(8,128)(2,1)}, bf16[192,1536]{1,0:T(8,128)(2,1)S(1)}, u32[]{:S(2)}, u32[]{:S(2)}) collective-permute-start(bf16[192,1536]{1,0:T(8,128)(2,1)} %get-tuple-element.49), channel_id=1, source_target_pairs={{0,96},{1,97},{2,98},{3,99},{4,100},{5,101},{6,102},{7,103},{8,104... | collective-permute-start | bytes 1769480 | tf_op jit(solution)/shard_map/ppermute | solution.py:29
  65.6 1.3 collective-permute-start.15
  67.0 0.0 all-gather.3.cloned.1.call-done.act
  67.0 10.1 %weight_out_grad.1 = f32[1536,768]{1,0:T(8,128)} custom-call(s32[4]{0:T(128)} %pad_add_fusion.where, bf16[1536,1536]{1,0:T(8,128)(2,1)} %all-gather.3.cloned.1.call-done.act, bf16[4,96,768]{2,1,0:T(8,128)(2,1)} %copy-done, bf16[4,96,768]{2,1,0:T(8,128)(2,1)} %copy-done.1, bf16[4,96,768]{2,1,0:T(8,128)(2,1)} %copy-done.3, bf16[4,96,768]{2,1,0:T(8,128)(2,1)} %copy-done.2), custom_call_target="tpu_custom_call" | custom-call | flops 1024 | bytes 1024 | tf_op jit(solution)/shard_map/weight_out_grad/pallas_call | solution.py:243
  77.1 2.0 %collective-permute-done.13 = bf16[192,1536]{1,0:T(8,128)(2,1)S(1)} collective-permute-done((bf16[192,1536]{1,0:T(8,128)(2,1)}, bf16[192,1536]{1,0:T(8,128)(2,1)S(1)}, u32[]{:S(2)}, u32[]{:S(2)}) %collective-permute-start.13) | collective-permute-done | bytes 589856 | tf_op jit(solution)/shard_map/ppermute | solution.py:29
  79.1 13.6 %collective-permute-done.15 = bf16[192,1536]{1,0:T(8,128)(2,1)} collective-permute-done((bf16[192,1536]{1,0:T(8,128)(2,1)}, bf16[192,1536]{1,0:T(8,128)(2,1)}, u32[]{:S(2)}, u32[]{:S(2)}) %collective-permute-start.15) | collective-permute-done | bytes 589856 | tf_op jit(solution)/shard_map/ppermute | solution.py:29
  92.7 1.3 convert_add_fusion.3
  94.1 0.1 multiply_convert_fusion.h0
  94.2 0.6 collective-permute-start.17
  94.8 2.1 %collective-permute-start.16 = (bf16[4,48,1536]{2,1,0:T(8,128)(2,1)S(1)}, bf16[4,48,1536]{2,1,0:T(8,128)(2,1)S(1)}, u32[]{:S(2)}, u32[]{:S(2)}) collective-permute-start(bf16[4,48,1536]{2,1,0:T(8,128)(2,1)S(1)} %multiply_convert_fusion.h0), channel_id=1, source_target_pairs={{0,96},{1,97},{2,98},{3,99},{4,100},{5,101},{6,102},{7,103},{8,104... | collective-permute-start | bytes 1769480 | tf_op jit(solution)/shard_map/ppermute | solution.py:29
  97.0 12.1 %collective-permute-done.17.h3 = bf16[4,48,1536]{2,1,0:T(8,128)(2,1)S(1)} collective-permute-done((bf16[4,48,1536]{2,1,0:T(8,128)(2,1)S(1)}, bf16[4,48,1536]{2,1,0:T(8,128)(2,1)S(1)}, u32[]{:S(2)}, u32[]{:S(2)}) %collective-permute-start.17) | collective-permute-done | bytes 589856 | tf_op jit(solution)/shard_map/ppermute | solution.py:29
  109.1 0.1 collective-permute-start.18
  109.2 2.7 %collective-permute-start.19 = (bf16[2,48,1536]{2,1,0:T(8,128)(2,1)S(1)}, bf16[2,48,1536]{2,1,0:T(8,128)(2,1)S(1)}, u32[]{:S(2)}, u32[]{:S(2)}) collective-permute-start(bf16[2,48,1536]{2,1,0:T(8,128)(2,1)S(1)} %slice.36), channel_id=1, source_target_pairs={{0,96},{1,97},{2,98},{3,99},{4,100},{5,101},{6,102},{7,103},{8,104... | collective-permute-start | bytes 884744 | tf_op jit(solution)/shard_map/ppermute | solution.py:29
  111.9 4.7 %collective-permute-done.18.h2a = bf16[2,48,1536]{2,1,0:T(8,128)(2,1)S(1)} collective-permute-done((bf16[2,48,1536]{2,1,0:T(8,128)(2,1)S(1)}, bf16[2,48,1536]{2,1,0:T(8,128)(2,1)S(1)}, u32[]{:S(2)}, u32[]{:S(2)}) %collective-permute-start.18) | collective-permute-done | bytes 294944 | tf_op jit(solution)/shard_map/ppermute | solution.py:29
  116.7 0.7 copy-done.11
  117.4 0.7 copy-done.12
  118.1 13.4 %input_grad.1 = (f32[4,48,1536]{2,1,0:T(8,128)}, bf16[4,48,1536]{2,1,0:T(8,128)(2,1)}, bf16[4,48,1536]{2,1,0:T(8,128)(2,1)}, bf16[4,48,1536]{2,1,0:T(8,128)(2,1)}, bf16[4,4,48,1536]{3,2,1,0:T(8,128)(2,1)}) custom-call(s32[4]{0:T(128)} %pad_add_fusion.where, bf16[4,48,1536]{2,1,0:T(8,128)(2,1)} %copy-done.5, bf16[4,48,1536]{2,1,0:T(8,128)(2,1)} %copy-done.8, ...), custom_call_target="tpu_custom_call" | custom-call | flops 1024 | bytes 1024 | tf_op jit(solution)/shard_map/input_grad/pallas_call | solution.py:198
  131.5 3.2 %collective-permute-start.23 = (bf16[4,4,48,1536]{3,2,1,0:T(8,128)(2,1)}, bf16[4,4,48,1536]{3,2,1,0:T(8,128)(2,1)S(1)}, u32[]{:S(2)}, u32[]{:S(2)}) collective-permute-start(bf16[4,4,48,1536]{3,2,1,0:T(8,128)(2,1)} %get-tuple-element.65), channel_id=1, source_target_pairs={{0,16},{1,17},{2,18},{3,19},{4,20},{5,21},{6,22},{7,23},{8,24},{9,... | collective-permute-start | bytes 7077896 | tf_op jit(solution)/shard_map/ppermute | solution.py:29
  134.7 2.7 %collective-permute-start.21 = (bf16[4,48,1536]{2,1,0:T(8,128)(2,1)}, bf16[4,48,1536]{2,1,0:T(8,128)(2,1)S(1)}, u32[]{:S(2)}, u32[]{:S(2)}) collective-permute-start(bf16[4,48,1536]{2,1,0:T(8,128)(2,1)} %get-tuple-element.62), channel_id=1, source_target_pairs={{0,12},{1,13},{2,14},{3,15},{4,0},{5,1},{6,2},{7,3},{8,4},{9,5},{1... | collective-permute-start | bytes 1769480 | tf_op jit(solution)/shard_map/ppermute | solution.py:29
  137.4 1.7 collective-permute-done.23
  139.1 1.4 copy-done.6
  140.5 9.2 %weight_in_grad.1 = f32[768,1536]{1,0:T(8,128)} custom-call(s32[4]{0:T(128)} %pad_add_fusion.where, bf16[16,2,48,768]{3,2,1,0:T(8,128)(2,1)} %bitcast.39, bf16[768,1536]{1,0:T(8,128)(2,1)} %bitcast.40, bf16[768,1536]{1,0:T(8,128)(2,1)} %bitcast.41), custom_call_target="tpu_custom_call" | custom-call | flops 1024 | bytes 1024 | tf_op jit(solution)/shard_map/weight_in_grad/pallas_call | solution.py:278
  149.7 1.9 %collective-permute-done.20 = bf16[4,48,1536]{2,1,0:T(8,128)(2,1)S(1)} collective-permute-done((bf16[4,48,1536]{2,1,0:T(8,128)(2,1)}, bf16[4,48,1536]{2,1,0:T(8,128)(2,1)S(1)}, u32[]{:S(2)}, u32[]{:S(2)}) %collective-permute-start.20) | collective-permute-done | bytes 589856 | tf_op jit(solution)/shard_map/ppermute | solution.py:29
  151.6 1.3 fusion.16
  153.0 0.1 collective-permute-start.24
  153.0 2.7 %collective-permute-start.25 = (bf16[48,1536]{1,0:T(8,128)(2,1)S(1)}, bf16[48,1536]{1,0:T(8,128)(2,1)S(1)}, u32[]{:S(2)}, u32[]{:S(2)}) collective-permute-start(bf16[48,1536]{1,0:T(8,128)(2,1)S(1)} %get-tuple-element.75), channel_id=1, source_target_pairs={{0,3},{1,0},{2,1},{3,2},{4,7},{5,4},{6,5},{7,6},{8,11},{9,8},{10,9... | collective-permute-start | bytes 442376 | tf_op jit(solution)/shard_map/ppermute | solution.py:29
  155.7 0.4 collective-permute-start.26
  156.1 2.1 %collective-permute-done.24 = bf16[48,1536]{1,0:T(8,128)(2,1)S(1)} collective-permute-done((bf16[48,1536]{1,0:T(8,128)(2,1)S(1)}, bf16[48,1536]{1,0:T(8,128)(2,1)S(1)}, u32[]{:S(2)}, u32[]{:S(2)}) %collective-permute-start.24) | collective-permute-done | bytes 147488 | tf_op jit(solution)/shard_map/ppermute | solution.py:29
  158.2 1.1 collective-permute-done.25
  159.4 1.8 %collective-permute-done.26 = bf16[48,1536]{1,0:T(8,128)(2,1)S(1)} collective-permute-done((bf16[48,1536]{1,0:T(8,128)(2,1)S(1)}, bf16[48,1536]{1,0:T(8,128)(2,1)S(1)}, u32[]{:S(2)}, u32[]{:S(2)}) %collective-permute-start.26) | collective-permute-done | bytes 147488 | tf_op jit(solution)/shard_map/ppermute | solution.py:29
  161.2 0.1 fusion.15
  161.3 3.3 %collective-permute-start.27 = (bf16[48,768]{1,0:T(8,128)(2,1)S(1)}, bf16[48,768]{1,0:T(8,128)(2,1)S(1)}, u32[]{:S(2)}, u32[]{:S(2)}) collective-permute-start(bf16[48,768]{1,0:T(8,128)(2,1)S(1)} %get-tuple-element.79), channel_id=1, source_target_pairs={{0,16},{1,17},{2,18},{3,19},{4,20},{5,21},{6,22},{7,23},{8,24},{9,... | collective-permute-start | bytes 221192 | tf_op jit(solution)/shard_map/ppermute | solution.py:29
  164.6 0.9 collective-permute-done.27
  165.5 0.7 maximum_select_fusion.1
  (46 shorter events, 0.2 us)
Async XLA Ops:
  7.2 8.9 %copy-start.14 = (bf16[96,768]{1,0:T(8,128)(2,1)S(1)}, bf16[96,768]{1,0:T(8,128)(2,1)}, u32[]{:S(2)}) copy-start(bf16[96,768]{1,0:T(8,128)(2,1)} %param.6) | copy-start | bytes 442372
  7.2 59.8 %all-gather.3.cloned.1.call-start = ((), (), s32[]{:S(2)}) async-start(), calls=%async_computation | async-start | bytes 5308416 | tf_op jit(solution)/shard_map/all_gather | solution.py:318
  7.2 6.0 %collective-permute-start.3 = (bf16[1536,768]{1,0:T(8,128)(2,1)}, bf16[1536,768]{1,0:T(8,128)(2,1)}, u32[]{:S(2)}, u32[]{:S(2)}) collective-permute-start(bf16[1536,768]{1,0:T(8,128)(2,1)} %refs_8_.1), channel_id=1, source_target_pairs={{0,16},{1,17},{2,18},{3,19},{4,20},{5,21},{6,22},{7,23},{8,24},{9,... | collective-permute-start | bytes 7077896 | tf_op jit(solution)/shard_map/ppermute | solution.py:29
  15.5 121.8 %all-gather.5.cloned.1.call-start = ((), (), s32[]{:S(2)}) async-start(), calls=%async_computation.1 | async-start | bytes 2506752 | tf_op jit(solution)/shard_map/all_gather | solution.py:331
  15.6 10.4 %collective-permute-start.4 = (bf16[768,1536]{1,0:T(8,128)(2,1)}, bf16[768,1536]{1,0:T(8,128)(2,1)S(1)}, u32[]{:S(2)}, u32[]{:S(2)}) collective-permute-start(bf16[768,1536]{1,0:T(8,128)(2,1)} %w_own.1), channel_id=1, source_target_pairs={{0,16},{1,17},{2,18},{3,19},{4,20},{5,21},{6,22},{7,23},{8,24},{9,... | collective-permute-start | bytes 7077896 | tf_op jit(solution)/shard_map/ppermute | solution.py:29
  16.0 4.9 %collective-permute-start = (bf16[96,768]{1,0:T(8,128)(2,1)S(1)}, bf16[96,768]{1,0:T(8,128)(2,1)S(1)}, u32[]{:S(2)}, u32[]{:S(2)}) collective-permute-start(bf16[96,768]{1,0:T(8,128)(2,1)S(1)} %copy-done.14), channel_id=1, source_target_pairs={{0,12},{1,13},{2,14},{3,15},{4,0},{5,1},{6,2},{7,3},{8,4},{9,5},{1... | collective-permute-start | bytes 442376 | tf_op jit(solution)/shard_map/ppermute | solution.py:29
  18.9 7.1 %collective-permute-start.1 = (bf16[96,768]{1,0:T(8,128)(2,1)S(1)}, bf16[96,768]{1,0:T(8,128)(2,1)S(1)}, u32[]{:S(2)}, u32[]{:S(2)}) collective-permute-start(bf16[96,768]{1,0:T(8,128)(2,1)S(1)} %copy-done.14), channel_id=1, source_target_pairs={{0,4},{1,5},{2,6},{3,7},{4,8},{5,9},{6,10},{7,11},{8,12},{9,13},{1... | collective-permute-start | bytes 442376 | tf_op jit(solution)/shard_map/ppermute | solution.py:29
  18.9 7.1 %collective-permute-start.2 = (bf16[96,768]{1,0:T(8,128)(2,1)S(1)}, bf16[96,768]{1,0:T(8,128)(2,1)S(1)}, u32[]{:S(2)}, u32[]{:S(2)}) collective-permute-start(bf16[96,768]{1,0:T(8,128)(2,1)S(1)} %copy-done.14), channel_id=1, source_target_pairs={{0,8},{1,9},{2,10},{3,11},{4,12},{5,13},{6,14},{7,15},{8,0},{9,1},... | collective-permute-start | bytes 442376 | tf_op jit(solution)/shard_map/ppermute | solution.py:29
  25.9 1.4 copy-start.4
  27.4 12.6 %copy-start = (bf16[4,96,768]{2,1,0:T(8,128)(2,1)}, bf16[4,96,768]{2,1,0:T(8,128)(2,1)S(1)}, u32[]{:S(2)}) copy-start(bf16[4,96,768]{2,1,0:T(8,128)(2,1)S(1)} %pad_maximum_fusion.refs_0_.g0) | copy-start | bytes 1769476
  27.4 15.5 %collective-permute-start.5 = (bf16[4,96,768]{2,1,0:T(8,128)(2,1)S(1)}, bf16[4,96,768]{2,1,0:T(8,128)(2,1)S(1)}, u32[]{:S(2)}, u32[]{:S(2)}) collective-permute-start(bf16[4,96,768]{2,1,0:T(8,128)(2,1)S(1)} %pad_maximum_fusion.refs_0_.g0), channel_id=1, source_target_pairs={{0,3},{1,0},{2,1},{3,2},{4,7},{5,4},{6,5},{7,6},{8,11},{9,8},{10,9... | collective-permute-start | bytes 1769480 | tf_op jit(solution)/shard_map/ppermute | solution.py:29
  29.8 16.7 %collective-permute-start.6 = (bf16[4,96,768]{2,1,0:T(8,128)(2,1)S(1)}, bf16[4,96,768]{2,1,0:T(8,128)(2,1)S(1)}, u32[]{:S(2)}, u32[]{:S(2)}) collective-permute-start(bf16[4,96,768]{2,1,0:T(8,128)(2,1)S(1)} %pad_maximum_fusion.refs_0_.g0), channel_id=1, source_target_pairs={{0,1},{1,2},{2,3},{3,0},{4,5},{5,6},{6,7},{7,4},{8,9},{9,10},{10,1... | collective-permute-start | bytes 1769480 | tf_op jit(solution)/shard_map/ppermute | solution.py:29
  29.8 16.7 %collective-permute-start.7 = (bf16[4,96,768]{2,1,0:T(8,128)(2,1)S(1)}, bf16[4,96,768]{2,1,0:T(8,128)(2,1)S(1)}, u32[]{:S(2)}, u32[]{:S(2)}) collective-permute-start(bf16[4,96,768]{2,1,0:T(8,128)(2,1)S(1)} %pad_maximum_fusion.refs_0_.g0), channel_id=1, source_target_pairs={{0,2},{1,3},{2,0},{3,1},{4,6},{5,7},{6,4},{7,5},{8,10},{9,11},{10,... | collective-permute-start | bytes 1769480 | tf_op jit(solution)/shard_map/ppermute | solution.py:29
  33.2 3.9 %collective-permute-start.8 = (bf16[2,48,1536]{2,1,0:T(8,128)(2,1)S(1)}, bf16[2,48,1536]{2,1,0:T(8,128)(2,1)S(1)}, u32[]{:S(2)}, u32[]{:S(2)}) collective-permute-start(bf16[2,48,1536]{2,1,0:T(8,128)(2,1)S(1)} %get-tuple-element.77), channel_id=1, source_target_pairs={{0,16},{1,17},{2,18},{3,19},{4,20},{5,21},{6,22},{7,23},{8,24},{9,... | collective-permute-start | bytes 884744 | tf_op jit(solution)/shard_map/ppermute | solution.py:29
  35.6 14.6 %collective-permute-start.9 = (bf16[4,96,768]{2,1,0:T(8,128)(2,1)S(1)}, bf16[4,96,768]{2,1,0:T(8,128)(2,1)}, u32[]{:S(2)}, u32[]{:S(2)}) collective-permute-start(bf16[4,96,768]{2,1,0:T(8,128)(2,1)S(1)} %pad_maximum_fusion.refs_0_.g0), channel_id=1, source_target_pairs={{0,16},{1,17},{2,18},{3,19},{4,20},{5,21},{6,22},{7,23},{8,24},{9,... | collective-permute-start | bytes 1769480 | tf_op jit(solution)/shard_map/ppermute | solution.py:29
  37.2 0.8 copy-start.13
  42.9 9.7 %copy-start.1 = (bf16[4,96,768]{2,1,0:T(8,128)(2,1)}, bf16[4,96,768]{2,1,0:T(8,128)(2,1)S(1)}, u32[]{:S(2)}) copy-start(bf16[4,96,768]{2,1,0:T(8,128)(2,1)S(1)} %collective-permute-done.5.refs_1_.g1) | copy-start | bytes 1769476
  46.5 6.2 %copy-start.2 = (bf16[4,96,768]{2,1,0:T(8,128)(2,1)}, bf16[4,96,768]{2,1,0:T(8,128)(2,1)S(1)}, u32[]{:S(2)}) copy-start(bf16[4,96,768]{2,1,0:T(8,128)(2,1)S(1)} %collective-permute-done.6.refs_3_.g3) | copy-start | bytes 1769476
  46.5 6.2 %copy-start.3 = (bf16[4,96,768]{2,1,0:T(8,128)(2,1)}, bf16[4,96,768]{2,1,0:T(8,128)(2,1)S(1)}, u32[]{:S(2)}) copy-start(bf16[4,96,768]{2,1,0:T(8,128)(2,1)S(1)} %collective-permute-done.7.refs_2_.g2) | copy-start | bytes 1769476
  46.5 4.3 %collective-permute-start.10 = (bf16[4,96,768]{2,1,0:T(8,128)(2,1)S(1)}, bf16[4,96,768]{2,1,0:T(8,128)(2,1)}, u32[]{:S(2)}, u32[]{:S(2)}) collective-permute-start(bf16[4,96,768]{2,1,0:T(8,128)(2,1)S(1)} %collective-permute-done.5.refs_1_.g1), channel_id=1, source_target_pairs={{0,16},{1,17},{2,18},{3,19},{4,20},{5,21},{6,22},{7,23},{8,24},{9,... | collective-permute-start | bytes 1769480 | tf_op jit(solution)/shard_map/ppermute | solution.py:29
  49.0 2.8 %collective-permute-start.11 = (bf16[4,96,768]{2,1,0:T(8,128)(2,1)S(1)}, bf16[4,96,768]{2,1,0:T(8,128)(2,1)}, u32[]{:S(2)}, u32[]{:S(2)}) collective-permute-start(bf16[4,96,768]{2,1,0:T(8,128)(2,1)S(1)} %collective-permute-done.7.refs_2_.g2), channel_id=1, source_target_pairs={{0,16},{1,17},{2,18},{3,19},{4,20},{5,21},{6,22},{7,23},{8,24},{9,... | collective-permute-start | bytes 1769480 | tf_op jit(solution)/shard_map/ppermute | solution.py:29
  49.1 3.6 %collective-permute-start.12 = (bf16[4,96,768]{2,1,0:T(8,128)(2,1)S(1)}, bf16[4,96,768]{2,1,0:T(8,128)(2,1)}, u32[]{:S(2)}, u32[]{:S(2)}) collective-permute-start(bf16[4,96,768]{2,1,0:T(8,128)(2,1)S(1)} %collective-permute-done.6.refs_3_.g3), channel_id=1, source_target_pairs={{0,16},{1,17},{2,18},{3,19},{4,20},{5,21},{6,22},{7,23},{8,24},{9,... | collective-permute-start | bytes 1769480 | tf_op jit(solution)/shard_map/ppermute | solution.py:29
  61.9 17.2 %collective-permute-start.13 = (bf16[192,1536]{1,0:T(8,128)(2,1)}, bf16[192,1536]{1,0:T(8,128)(2,1)S(1)}, u32[]{:S(2)}, u32[]{:S(2)}) collective-permute-start(bf16[192,1536]{1,0:T(8,128)(2,1)} %get-tuple-element.48), channel_id=1, source_target_pairs={{0,32},{1,33},{2,34},{3,35},{4,36},{5,37},{6,38},{7,39},{8,40},{9,... | collective-permute-start | bytes 1769480 | tf_op jit(solution)/shard_map/ppermute | solution.py:29
  63.6 15.5 %collective-permute-start.14 = (bf16[192,1536]{1,0:T(8,128)(2,1)}, bf16[192,1536]{1,0:T(8,128)(2,1)S(1)}, u32[]{:S(2)}, u32[]{:S(2)}) collective-permute-start(bf16[192,1536]{1,0:T(8,128)(2,1)} %get-tuple-element.49), channel_id=1, source_target_pairs={{0,96},{1,97},{2,98},{3,99},{4,100},{5,101},{6,102},{7,103},{8,104... | collective-permute-start | bytes 1769480 | tf_op jit(solution)/shard_map/ppermute | solution.py:29
  65.6 27.1 %collective-permute-start.15 = (bf16[192,1536]{1,0:T(8,128)(2,1)}, bf16[192,1536]{1,0:T(8,128)(2,1)}, u32[]{:S(2)}, u32[]{:S(2)}) collective-permute-start(bf16[192,1536]{1,0:T(8,128)(2,1)} %get-tuple-element.50), channel_id=1, source_target_pairs={{0,64},{1,65},{2,66},{3,67},{4,68},{5,69},{6,70},{7,71},{8,72},{9,... | collective-permute-start | bytes 1769480 | tf_op jit(solution)/shard_map/ppermute | solution.py:29
  67.0 25.8 %copy-start.10 = (f32[192,1536]{1,0:T(8,128)S(1)}, f32[192,1536]{1,0:T(8,128)}, u32[]{:S(2)}) copy-start(f32[192,1536]{1,0:T(8,128)} %get-tuple-element.47) | copy-start | bytes 3538948
  94.2 22.4 %copy-start.5 = (bf16[4,48,1536]{2,1,0:T(8,128)(2,1)}, bf16[4,48,1536]{2,1,0:T(8,128)(2,1)S(1)}, u32[]{:S(2)}) copy-start(bf16[4,48,1536]{2,1,0:T(8,128)(2,1)S(1)} %multiply_convert_fusion.h0) | copy-start | bytes 1769476
  94.2 14.8 %collective-permute-start.17 = (bf16[4,48,1536]{2,1,0:T(8,128)(2,1)S(1)}, bf16[4,48,1536]{2,1,0:T(8,128)(2,1)S(1)}, u32[]{:S(2)}, u32[]{:S(2)}) collective-permute-start(bf16[4,48,1536]{2,1,0:T(8,128)(2,1)S(1)} %multiply_convert_fusion.h0), channel_id=1, source_target_pairs={{0,32},{1,33},{2,34},{3,35},{4,36},{5,37},{6,38},{7,39},{8,40},{9,... | collective-permute-start | bytes 1769480 | tf_op jit(solution)/shard_map/ppermute | solution.py:29
  94.8 14.3 %collective-permute-start.16 = (bf16[4,48,1536]{2,1,0:T(8,128)(2,1)S(1)}, bf16[4,48,1536]{2,1,0:T(8,128)(2,1)S(1)}, u32[]{:S(2)}, u32[]{:S(2)}) collective-permute-start(bf16[4,48,1536]{2,1,0:T(8,128)(2,1)S(1)} %multiply_convert_fusion.h0), channel_id=1, source_target_pairs={{0,96},{1,97},{2,98},{3,99},{4,100},{5,101},{6,102},{7,103},{8,104... | collective-permute-start | bytes 1769480 | tf_op jit(solution)/shard_map/ppermute | solution.py:29
  109.0 7.6 %copy-start.7 = (bf16[4,48,1536]{2,1,0:T(8,128)(2,1)}, bf16[4,48,1536]{2,1,0:T(8,128)(2,1)S(1)}, u32[]{:S(2)}) copy-start(bf16[4,48,1536]{2,1,0:T(8,128)(2,1)S(1)} %collective-permute-done.17.h3) | copy-start | bytes 1769476
  109.1 7.6 %collective-permute-start.18 = (bf16[2,48,1536]{2,1,0:T(8,128)(2,1)S(1)}, bf16[2,48,1536]{2,1,0:T(8,128)(2,1)S(1)}, u32[]{:S(2)}, u32[]{:S(2)}) collective-permute-start(bf16[2,48,1536]{2,1,0:T(8,128)(2,1)S(1)} %slice.35), channel_id=1, source_target_pairs={{0,32},{1,33},{2,34},{3,35},{4,36},{5,37},{6,38},{7,39},{8,40},{9,... | collective-permute-start | bytes 884744 | tf_op jit(solution)/shard_map/ppermute | solution.py:29
  109.1 7.5 %copy-start.8 = (bf16[4,48,1536]{2,1,0:T(8,128)(2,1)}, bf16[4,48,1536]{2,1,0:T(8,128)(2,1)S(1)}, u32[]{:S(2)}) copy-start(bf16[4,48,1536]{2,1,0:T(8,128)(2,1)S(1)} %collective-permute-done.16.h1) | copy-start | bytes 1769476
  109.2 7.4 %collective-permute-start.19 = (bf16[2,48,1536]{2,1,0:T(8,128)(2,1)S(1)}, bf16[2,48,1536]{2,1,0:T(8,128)(2,1)S(1)}, u32[]{:S(2)}, u32[]{:S(2)}) collective-permute-start(bf16[2,48,1536]{2,1,0:T(8,128)(2,1)S(1)} %slice.36), channel_id=1, source_target_pairs={{0,96},{1,97},{2,98},{3,99},{4,100},{5,101},{6,102},{7,103},{8,104... | collective-permute-start | bytes 884744 | tf_op jit(solution)/shard_map/ppermute | solution.py:29
  116.6 0.7 copy-start.11
  117.4 0.7 copy-start.12
  131.5 7.6 %collective-permute-start.23 = (bf16[4,4,48,1536]{3,2,1,0:T(8,128)(2,1)}, bf16[4,4,48,1536]{3,2,1,0:T(8,128)(2,1)S(1)}, u32[]{:S(2)}, u32[]{:S(2)}) collective-permute-start(bf16[4,4,48,1536]{3,2,1,0:T(8,128)(2,1)} %get-tuple-element.65), channel_id=1, source_target_pairs={{0,16},{1,17},{2,18},{3,19},{4,20},{5,21},{6,22},{7,23},{8,24},{9,... | collective-permute-start | bytes 7077896 | tf_op jit(solution)/shard_map/ppermute | solution.py:29
  134.7 16.9 %collective-permute-start.20 = (bf16[4,48,1536]{2,1,0:T(8,128)(2,1)}, bf16[4,48,1536]{2,1,0:T(8,128)(2,1)S(1)}, u32[]{:S(2)}, u32[]{:S(2)}) collective-permute-start(bf16[4,48,1536]{2,1,0:T(8,128)(2,1)} %get-tuple-element.61), channel_id=1, source_target_pairs={{0,4},{1,5},{2,6},{3,7},{4,8},{5,9},{6,10},{7,11},{8,12},{9,13},{1... | collective-permute-start | bytes 1769480 | tf_op jit(solution)/shard_map/ppermute | solution.py:29
  134.7 16.9 %collective-permute-start.21 = (bf16[4,48,1536]{2,1,0:T(8,128)(2,1)}, bf16[4,48,1536]{2,1,0:T(8,128)(2,1)S(1)}, u32[]{:S(2)}, u32[]{:S(2)}) collective-permute-start(bf16[4,48,1536]{2,1,0:T(8,128)(2,1)} %get-tuple-element.62), channel_id=1, source_target_pairs={{0,12},{1,13},{2,14},{3,15},{4,0},{5,1},{6,2},{7,3},{8,4},{9,5},{1... | collective-permute-start | bytes 1769480 | tf_op jit(solution)/shard_map/ppermute | solution.py:29
  137.4 14.2 %collective-permute-start.22 = (bf16[4,48,1536]{2,1,0:T(8,128)(2,1)}, bf16[4,48,1536]{2,1,0:T(8,128)(2,1)}, u32[]{:S(2)}, u32[]{:S(2)}) collective-permute-start(bf16[4,48,1536]{2,1,0:T(8,128)(2,1)} %get-tuple-element.63), channel_id=1, source_target_pairs={{0,8},{1,9},{2,10},{3,11},{4,12},{5,13},{6,14},{7,15},{8,0},{9,1},... | collective-permute-start | bytes 1769480 | tf_op jit(solution)/shard_map/ppermute | solution.py:29
  139.1 1.4 copy-start.6
  140.5 11.1 %copy-start.9 = (f32[4,48,1536]{2,1,0:T(8,128)S(1)}, f32[4,48,1536]{2,1,0:T(8,128)}, u32[]{:S(2)}) copy-start(f32[4,48,1536]{2,1,0:T(8,128)} %get-tuple-element.60) | copy-start | bytes 3538948
  153.0 5.3 %collective-permute-start.24 = (bf16[48,1536]{1,0:T(8,128)(2,1)S(1)}, bf16[48,1536]{1,0:T(8,128)(2,1)S(1)}, u32[]{:S(2)}, u32[]{:S(2)}) collective-permute-start(bf16[48,1536]{1,0:T(8,128)(2,1)S(1)} %get-tuple-element.73), channel_id=1, source_target_pairs={{0,1},{1,2},{2,3},{3,0},{4,5},{5,6},{6,7},{7,4},{8,9},{9,10},{10,1... | collective-permute-start | bytes 442376 | tf_op jit(solution)/shard_map/ppermute | solution.py:29
  153.0 6.3 %collective-permute-start.25 = (bf16[48,1536]{1,0:T(8,128)(2,1)S(1)}, bf16[48,1536]{1,0:T(8,128)(2,1)S(1)}, u32[]{:S(2)}, u32[]{:S(2)}) collective-permute-start(bf16[48,1536]{1,0:T(8,128)(2,1)S(1)} %get-tuple-element.75), channel_id=1, source_target_pairs={{0,3},{1,0},{2,1},{3,2},{4,7},{5,4},{6,5},{7,6},{8,11},{9,8},{10,9... | collective-permute-start | bytes 442376 | tf_op jit(solution)/shard_map/ppermute | solution.py:29
  155.7 5.5 %collective-permute-start.26 = (bf16[48,1536]{1,0:T(8,128)(2,1)S(1)}, bf16[48,1536]{1,0:T(8,128)(2,1)S(1)}, u32[]{:S(2)}, u32[]{:S(2)}) collective-permute-start(bf16[48,1536]{1,0:T(8,128)(2,1)S(1)} %get-tuple-element.74), channel_id=1, source_target_pairs={{0,2},{1,3},{2,0},{3,1},{4,6},{5,7},{6,4},{7,5},{8,10},{9,11},{10,... | collective-permute-start | bytes 442376 | tf_op jit(solution)/shard_map/ppermute | solution.py:29
  161.3 4.2 %collective-permute-start.27 = (bf16[48,768]{1,0:T(8,128)(2,1)S(1)}, bf16[48,768]{1,0:T(8,128)(2,1)S(1)}, u32[]{:S(2)}, u32[]{:S(2)}) collective-permute-start(bf16[48,768]{1,0:T(8,128)(2,1)S(1)} %get-tuple-element.79), channel_id=1, source_target_pairs={{0,16},{1,17},{2,18},{3,19},{4,20},{5,21},{6,22},{7,23},{8,24},{9,... | collective-permute-start | bytes 221192 | tf_op jit(solution)/shard_map/ppermute | solution.py:29
Sparse Core Ops, SparseCore 0:
  15.7 37.3 all-gather.2
  67.1 41.4 all-gather.4

commit v2 on v1

--- a/solution.py
+++ b/solution.py
@@ -1,3 +1,5 @@
+import functools
+
 import jax
 import jax.numpy as jnp
 from jax import lax
@@ -11,7 +13,9 @@
 N = 4
 K = 48
 VMEM = 56 * 2**20
+SMALL = 48 * 2**20
 LIGHT = pl.CostEstimate(flops=1024, bytes_accessed=1024, transcendentals=0)
+HEAVY = pl.CostEstimate(flops=8 * 10**9, bytes_accessed=2**24, transcendentals=0)
 AXES = ("row", "col")
 BF = jnp.bfloat16
 F32 = jnp.float32
@@ -55,14 +59,6 @@
     return (value, slope)
 
 
-def gather_z(block):
-    below = along_z(block, 1)
-    above = along_z(block, -1)
-    far_a = along_z(below[:2], 1)
-    far_b = along_z(above[2:], -1)
-    return [block, above, far_a, far_b, below]
-
-
 def place_xy(where, core, q, r):
     dx = jnp.where(core == 0, r, q)
     dy = jnp.where(core == 0, q, r)
@@ -77,71 +73,82 @@
     return lax.dot_general(a, b, (((0,), (0,)), ((), ())), preferred_element_type=F32)
 
 
+HBM = pl.BlockSpec(memory_space=pltpu.HBM)
 ANY = pl.BlockSpec(memory_space=pl.ANY)
-STEPS = 3
-
-
-def act_grad_kernel(where, *refs):
-    own, other, weights = refs[0:4], refs[4:8], refs[8:10]
-    outs = refs[10:14]
-    lhs, w, p0, p1, in_sems, w_sems, out_sems = refs[14:]
-    rows = w.shape[1] // STEPS
-    loads = []
-    for j in range(STEPS):
-        part = pl.ds(j * rows, rows)
-        for half in range(2):
-            loads.append(pltpu.make_async_copy(weights[half].at[part], w.at[half, part], w_sems.at[j, half]))
+
+
+def relay_slot(zr, y):
+    low = y < 2
+    up = jnp.where(low, 12 + y, y)
+    far = jnp.where(low, y, 4 + y)
+    down = jnp.where(low, 4 + y, 12 + y)
+    return jnp.where(zr == 0, 8 + y, jnp.where(zr == 1, up, jnp.where(zr == 2, far, down)))
+
+
+def act_grad_kernel(part, where, *refs):
+    own, other, weights, outs = refs[0:4], refs[4:8], refs[8:10], refs[10:12]
+    lhs, w, staged, in_sems, w_sems, out_sems = refs[12:]
+    columns = w.shape[2]
+    loads = [
+        pltpu.make_async_copy(weights[half].at[pl.ds(f * columns, columns)], w.at[f, half], w_sems.at[f, half])
+        for f in range(2)
+        for half in range(2)
+    ]
     fills = []
     mine = pl.ds(pl.multiple_of(where[1] * K, 16), K)
     for half, stacks in enumerate((own, other)):
         for q, stack in enumerate(stacks):
             for r in range(N):
                 x, y = place_xy(where, where[1] if half == 0 else 1 - where[1], q, r)
-                to = lhs.at[half, (x + N - where[0]) % N, y]
-                fills.append(pltpu.make_async_copy(stack.at[r, mine], to, in_sems.at[half, q, r]))
-    for copy in loads[:2] + fills + loads[2:]:
+                slot = relay_slot((x + N - where[0]) % N, y) - 8 * part
+                to = lhs.at[half, jnp.clip(slot, 0, 7)]
+                copy = pltpu.make_async_copy(stack.at[r, mine], to, in_sems.at[half, q, r])
+                fills.append(((slot >= 0) & (slot < 8), copy))
+    for copy in loads[:2]:
         copy.start()
-    for copy in fills:
-        copy.wait()
+    for wanted, copy in fills:
+        pl.when(wanted)(copy.start)
+    for copy in loads[2:]:
+        copy.start()
+    for wanted, copy in fills:
+        pl.when(wanted)(copy.wait)
+    a, b = (lhs[half].reshape(8 * K, -1) for half in range(2))
     stores = []
-    for j in range(STEPS):
-        loads[2 * j].wait()
-        loads[2 * j + 1].wait()
-        part = pl.ds(j * rows, rows)
-        total = dot_nt(lhs[0].reshape(16 * K, -1), w[0, part]) + dot_nt(lhs[1].reshape(16 * K, -1), w[1, part])
-        p0[:, part] = total[: N * K]
-        for r in (1, 2, 3):
-            p1[r - 1, :, part] = total[r * N * K : (r + 1) * N * K].astype(BF)
-        for r in range(N):
-            source = p0.at[:, part] if r == 0 else p1.at[r - 1, :, part]
-            stores.append(pltpu.make_async_copy(source, outs[r].at[:, part], out_sems.at[j, r]))
+    for f in range(2):
+        loads[2 * f].wait()
+        loads[2 * f + 1].wait()
+        total = dot_nt(a, w[f, 0]) + dot_nt(b, w[f, 1])
+        at = pl.ds(f * columns, columns)
+        staged[:, :, at] = total.reshape(2, N * K, columns).astype(staged.dtype)
+        for i in range(2):
+            stores.append(pltpu.make_async_copy(staged.at[i, :, at], outs[i].at[:, at], out_sems.at[f, i]))
             stores[-1].start()
     for copy in stores:
         copy.wait()
 
 
-def act_grad_parts(where, stacks, others, w_own, w_other):
+def act_grad_parts(part, where, stacks, others, w_own, w_other):
     hidden, half = w_own.shape
+    kind = (BF, F32)[part]
     return pl.pallas_call(
-        act_grad_kernel,
-        out_shape=[jax.ShapeDtypeStruct((N * K, hidden), t) for t in (F32, BF, BF, BF)],
+        functools.partial(act_grad_kernel, part),
+        out_shape=[jax.ShapeDtypeStruct((N * K, hidden), kind)] * 2,
         grid_spec=pltpu.PrefetchScalarGridSpec(
             num_scalar_prefetch=1,
             grid=(),
-            in_specs=[ANY] * 10,
-            out_specs=[ANY] * 4,
+            in_specs=[ANY] * 8 + [HBM, ANY],
+            out_specs=[ANY] * 2,
             scratch_shapes=[
-                pltpu.VMEM((2, N, N, K, half), BF),
-                pltpu.VMEM((2, hidden, half), BF),
-                pltpu.VMEM((N * K, hidden), F32),
-                pltpu.VMEM((3, N * K, hidden), BF),
+                pltpu.VMEM((2, 8, K, half), BF),
+                pltpu.VMEM((2, 2, hidden // 2, half), BF),
+                pltpu.VMEM((2, N * K, hidden), kind),
                 pltpu.SemaphoreType.DMA((2, N, N)),
-                pltpu.SemaphoreType.DMA((STEPS, 2)),
-                pltpu.SemaphoreType.DMA((STEPS, N)),
+                pltpu.SemaphoreType.DMA((2, 2)),
+                pltpu.SemaphoreType.DMA((2, 2)),
             ],
         ),
-        compiler_params=pltpu.CompilerParams(vmem_limit_bytes=VMEM),
-        cost_estimate=LIGHT,
+        compiler_params=pltpu.CompilerParams(vmem_limit_bytes=SMALL),
+        cost_estimate=HEAVY if part else LIGHT,
         name="act_grad",
     )(where, *stacks, *others, w_own, w_other)
 
@@ -150,15 +157,11 @@
     outs, (rows_out, lhs, w, near, far, in_sems, w_sems, out_sems) = refs[:4], refs[4:]
     n = h0.shape[1]
     half = w_own.shape[0]
-    rows = half // STEPS
+    rows = half
     loads = []
-    for j in range(2 * STEPS):
-        weight = (w_own, w_other)[j // STEPS]
-        loads.append(
-            pltpu.make_async_copy(
-                weight.at[pl.ds(j % STEPS * rows, rows)], w.at[pl.ds(j * rows, rows)], w_sems.at[j]
-            )
-        )
+    for j in range(2):
+        weight = (w_own, w_other)[j]
+        loads.append(pltpu.make_async_copy(weight, w.at[pl.ds(j * rows, rows)], w_sems.at[j]))
     fills = []
     for zr in range(N):
         for y in range(N):
@@ -175,9 +178,9 @@
         copy.start()
     for copy in fills:
         copy.wait()
-    stores = [pltpu.make_async_copy(lhs, rows_out, out_sems.at[2 * STEPS, 0])]
+    stores = [pltpu.make_async_copy(lhs, rows_out, out_sems.at[2, 0])]
     stores[0].start()
-    for j in range(2 * STEPS):
+    for j in range(2):
         loads[j].wait()
         part = pl.ds(j * rows, rows)
         total = dot_nt(lhs[...].reshape(16 * n, -1), w[part]).reshape(N, N, n, -1)
@@ -202,19 +205,19 @@
         grid_spec=pltpu.PrefetchScalarGridSpec(
             num_scalar_prefetch=1,
             grid=(),
-            in_specs=[ANY] * 7,
-            out_specs=[ANY] * 5,
+            in_specs=[HBM] * 7,
+            out_specs=[HBM] * 5,
             scratch_shapes=[
                 pltpu.VMEM((N, N, n, hidden), BF),
                 pltpu.VMEM((2 * half, hidden), BF),
                 pltpu.VMEM((N, n, 2 * half), F32),
                 pltpu.VMEM((3, N, n, 2 * half), BF),
                 pltpu.SemaphoreType.DMA((N, N)),
-                pltpu.SemaphoreType.DMA((2 * STEPS,)),
-                pltpu.SemaphoreType.DMA((2 * STEPS + 1, N)),
+                pltpu.SemaphoreType.DMA((2,)),
+                pltpu.SemaphoreType.DMA((3, N)),
             ],
         ),
-        compiler_params=pltpu.CompilerParams(vmem_limit_bytes=VMEM),
+        compiler_params=pltpu.CompilerParams(vmem_limit_bytes=SMALL),
         cost_estimate=LIGHT,
         name="input_grad",
     )(where, *pieces, w_own, w_other)
@@ -246,12 +249,12 @@
         grid_spec=pltpu.PrefetchScalarGridSpec(
             num_scalar_prefetch=1,
             grid=(hidden // block,),
-            in_specs=[pl.BlockSpec((tokens, block), lambda i, s: (0, i))] + [ANY] * 4,
+            in_specs=[pl.BlockSpec((tokens, block), lambda i, s: (0, i))] + [HBM] * 4,
             out_specs=pl.BlockSpec((block, width), lambda i, s: (i, 0)),
             scratch_shapes=[pltpu.VMEM((N, N, 2 * K, width), BF), pltpu.SemaphoreType.DMA((N, N))],
         ),
         compiler_params=pltpu.CompilerParams(vmem_limit_bytes=VMEM),
-        cost_estimate=LIGHT,
+        cost_estimate=HEAVY,
         name="weight_out_grad",
     )(where, act, *stacks)
 
@@ -286,7 +289,7 @@
             scratch_shapes=[pltpu.VMEM((2, N, N, K, width), BF)],
         ),
         compiler_params=pltpu.CompilerParams(vmem_limit_bytes=VMEM),
-        cost_estimate=LIGHT,
+        cost_estimate=HEAVY,
         name="weight_in_grad",
     )(where, inputs.reshape(16, 2, K, width), hid_own.reshape(-1, hidden), hid_other.reshape(-1, hidden))
 
@@ -311,29 +314,40 @@
         )
 
     hold = lax.optimization_barrier
+    act = gelu_parts(preactivation.astype(F32))[0].astype(BF)
+    act_all = lax.all_gather(act, "row", axis=0, tiled=True)
+    g_near = [first_ring(out_grad, -r) for r in (1, 3, 2)]
     w_out_other, w_in_other = swap(weight_out), swap(weight_in)
-    g_near = [first_ring(out_grad, -r) for r in (1, 3, 2)]
-    w_out_other, preact = hold((w_out_other, preactivation))
-    act = gelu_parts(preact.astype(F32))[0].astype(BF)
-    act_all = lax.all_gather(act, "row", axis=0, tiled=True)
-
-    g_near, w_out_other, w_in_other, preact = hold((g_near, w_out_other, w_in_other, preact))
+    g_near, w_out_other, w_in_other, preact, where = hold(
+        (g_near, w_out_other, w_in_other, preactivation, where)
+    )
     g_stack = jnp.stack([out_grad, g_near[0], g_near[2], g_near[1]])
     g_far = [second_ring(g_stack, -q) for q in (1, 3, 2)]
     h_set = in_core_order(*mine_and_other(preact.reshape(2, 2, K, hidden), 1), 0)
     slope = gelu_parts(h_set.astype(F32))[1]
-    g_far, slope = hold((g_far, slope))
+    g_far[0], slope = hold((g_far[0], slope))
     g_stacks = [g_stack, g_far[0], g_far[2], g_far[1]]
     g_others = [swap(g) for g in g_stacks]
 
-    p0, p1, p2, p3 = act_grad_parts(where, g_stacks, g_others, weight_out, w_out_other)
-    x_late, g_stacks = hold((layer_input, g_stacks))
+    half = N * K // 2
+    to_up, to_down = act_grad_parts(0, where, g_stacks, g_others, weight_out, w_out_other)
+    from_down, from_up = along_z(to_up, 1), along_z(to_down, -1)
+    g_stacks, g_others, act_all, to_up, x_late = hold((g_stacks, g_others, act_all, to_up, layer_input))
     x_all = lax.all_gather(x_late, "col", axis=0, tiled=True)
-    weight_out_grad = weight_out_grad_of(where, act_all, g_stacks)
-    s1, s3, s2, weight_out_grad = hold((along_z(p1, 1), along_z(p3, -1), along_z(p2, 2), weight_out_grad))
-
-    act_grad = (p0 + s1.astype(F32) + s2.astype(F32) + s3.astype(F32)).reshape(N, K, hidden)
-    pieces = gather_z((act_grad * slope).astype(BF))
+    own, relay = act_grad_parts(1, where, g_stacks, g_others, weight_out, w_out_other)
+    from_down, from_up, own, relay = hold((from_down, from_up, own, relay))
+    relay_up = (relay[:half] + from_down[:half].astype(F32)).astype(BF)
+    relay_down = (relay[half:] + from_up[half:].astype(F32)).astype(BF)
+    sum_a, sum_b = along_z(relay_up, 1), along_z(relay_down, -1)
+    rest = jnp.concatenate([from_up[:half], from_down[half:]]).astype(F32)
+    act_grad = own + rest + jnp.concatenate([sum_a, sum_b]).astype(F32)
+    hid = (act_grad.reshape(N, K, hidden) * slope).astype(BF)
+
+    below, above = along_z(hid, 1), along_z(hid, -1)
+    act_late, hid = hold((act_all, hid))
+    weight_out_grad = weight_out_grad_of(where, act_late, g_stacks)
+    below, above, weight_out_grad = hold((below, above, weight_out_grad))
+    pieces = [hid, above, along_z(below[:2], 1), along_z(above[2:], -1), below]
     d0, d1, d2, d3, hid_own = input_grad_parts(where, pieces, weight_in, w_in_other)
     got = [first_ring(d, r) for r, d in ((1, d1), (3, d3), (2, d2))]
     weight_in_grad = weight_in_grad_of(where, x_all, hid_own, swap(hid_own))

time: 173 us -> 157 us (0.908)
  waiting for transfers between devices: 62.6 us -> 38.5 us
  starting transfers between devices: 38.8 us -> 44.3 us
    ppermute x28 -> x29, waiting for transfers between devices: 62.5 us -> 38.4 us  [permute(): return lax.ppermute(array, AXES, pairs)]
    ppermute x28 -> x29, starting transfers between devices: 38.7 us -> 44.2 us  [permute(): return lax.ppermute(array, AXES, pairs)]
    pallas_call x1 -> x2, Pallas kernels: 9.2 us -> 14.2 us  [act_grad_parts(): pl.pallas_call(functools.partial(act_grad_kernel, part), out_shape=[jax.S...]
    pallas_call x1, Pallas kernels: 13.4 us -> 9.74 us  [input_grad_parts(): pl.pallas_call(input_grad_kernel, out_shape=[jax.ShapeDtypeStruct((N, n,...]
    slice x2 -> x4, local copies, waits for them, and re-layouts: 0.04 us -> 2 us  [the longest x2 1.96 us: on_device(): rest = jnp.concatenate([from_up[:half], from_down[half:]]).astype(F32)]
    squeeze x1, local copies, waits for them, and re-layouts: 1.81 us -> 0.04 us  [mine_and_other(): mine = lax.dynamic_index_in_dim(array, core, axis, keepdims=False)]
    convert_element_type x2 -> x3, other arithmetic: 2.41 us -> 3.96 us  [the longest x1 2.32 us: on_device(): act = gelu_parts(preactivation.astype(F32))[0].astype(BF)]
    unnamed x30 -> x36, local copies, waits for them, and re-layouts: 5.09 us -> 5.7 us
  transfers between devices with their start and end apart: 30 -> 31, of which waited for: 19 -> 18; matrix products, arithmetic and copies ran while one was open for 4% -> 3% of each run, Pallas kernels for 24% -> 27%
where the time goes in v2:
time: 157 us; the launch traced here: 156 us
  starting transfers between devices  44.3 us (28%)
  Pallas kernels  42.9 us (27%)
  waiting for transfers between devices  38.5 us (25%)
  between operations  14.3 us (9%)
  other arithmetic  8.46 us (5%)
  local copies, waits for them, and re-layouts  7.79 us (5%)
    ppermute x29, starting transfers between devices, permute(): return lax.ppermute(array, AXES, pairs)  44.2 us
    ppermute x29, waiting for transfers between devices, permute(): return lax.ppermute(array, AXES, pairs)  38.4 us
    pallas_call x2, Pallas kernels, act_grad_parts(): pl.pallas_call(functools.partial(act_grad_kernel, part), out_shape=[jax.S...  14.2 us
    pallas_call x1, Pallas kernels, weight_out_grad_of(): pl.pallas_call(weight_out_grad_kernel, out_shape=jax.ShapeDtypeStruct((hi...  9.98 us
    pallas_call x1, Pallas kernels, input_grad_parts(): pl.pallas_call(input_grad_kernel, out_shape=[jax.ShapeDtypeStruct((N, n,...  9.74 us
    pallas_call x1, Pallas kernels, weight_in_grad_of(): pl.pallas_call(weight_in_grad_kernel, out_shape=jax.ShapeDtypeStruct((wid...  9.02 us
    unnamed x36, local copies, waits for them, and re-layouts  5.7 us
  transfers between devices with their start and end apart: 31, of which 18 were waited for; matrix products, arithmetic and copies ran while one was open for 3% of the time, Pallas kernels for 27%

profile of v2, /device:TPU:1, one launch (start us, length us, event | category | flops | bytes accessed | tf_op | source)
XLA Modules:
  0.0 156.2 jit_solution(9830821041880886488)
XLA Ops:
  7.2 2.3 %fusion.1 = bf16[192,1536]{1,0:T(8,128)(2,1)} fusion(bf16[192,1536]{1,0:T(8,128)(2,1)} %param.7), kind=kLoop, calls=%fused_computation.13 | loop fusion | flops 2949120 | bytes 1179648 | tf_op jit(solution)/shard_map/convert_element_type | solution.py:317
  9.6 1.5 collective-permute-start.4
  11.1 0.1 collective-permute-start.3
  11.2 1.4 collective-permute-start.1
  12.6 1.4 collective-permute-start
  14.0 1.6 %collective-permute-start.2 = (bf16[96,768]{1,0:T(8,128)(2,1)S(1)}, bf16[96,768]{1,0:T(8,128)(2,1)S(1)}, u32[]{:S(2)}, u32[]{:S(2)}) collective-permute-start(bf16[96,768]{1,0:T(8,128)(2,1)S(1)} %copy-done.17), channel_id=1, source_target_pairs={{0,8},{1,9},{2,10},{3,11},{4,12},{5,13},{6,14},{7,15},{8,0},{9,1},... | collective-permute-start | bytes 442376 | tf_op jit(solution)/shard_map/ppermute | solution.py:33
  15.7 0.1 pad_add_fusion.where
  15.8 1.1 collective-permute-done.1
  16.9 2.9 %collective-permute-done.2 = bf16[96,768]{1,0:T(8,128)(2,1)S(1)} collective-permute-done((bf16[96,768]{1,0:T(8,128)(2,1)S(1)}, bf16[96,768]{1,0:T(8,128)(2,1)S(1)}, u32[]{:S(2)}, u32[]{:S(2)}) %collective-permute-start.2) | collective-permute-done | bytes 147488 | tf_op jit(solution)/shard_map/ppermute | solution.py:33
  19.8 1.4 copy-done.15
  21.2 0.1 pad_maximum_fusion.refs_0_.g0
  21.3 1.0 collective-permute-start.8
  22.3 2.7 %collective-permute-start.7 = (bf16[4,96,768]{2,1,0:T(8,128)(2,1)S(1)}, bf16[4,96,768]{2,1,0:T(8,128)(2,1)S(1)}, u32[]{:S(2)}, u32[]{:S(2)}) collective-permute-start(bf16[4,96,768]{2,1,0:T(8,128)(2,1)S(1)} %pad_maximum_fusion.refs_0_.g0), channel_id=1, source_target_pairs={{0,2},{1,3},{2,0},{3,1},{4,6},{5,7},{6,4},{7,5},{8,10},{9,11},{10,... | collective-permute-start | bytes 1769480 | tf_op jit(solution)/shard_map/ppermute | solution.py:33
  25.1 0.9 collective-permute-start.5
  26.0 3.2 %collective-permute-start.6 = (bf16[2,48,1536]{2,1,0:T(8,128)(2,1)S(1)}, bf16[2,48,1536]{2,1,0:T(8,128)(2,1)S(1)}, u32[]{:S(2)}, u32[]{:S(2)}) collective-permute-start(bf16[2,48,1536]{2,1,0:T(8,128)(2,1)S(1)} %get-tuple-element.93), channel_id=1, source_target_pairs={{0,16},{1,17},{2,18},{3,19},{4,20},{5,21},{6,22},{7,23},{8,24},{9,... | collective-permute-start | bytes 884744 | tf_op jit(solution)/shard_map/ppermute | solution.py:33
  29.1 0.1 collective-permute-start.9
  29.2 1.1 collective-permute-done.6
  30.3 1.9 %fusion.10 = f32[4,48,1536]{2,1,0:T(8,128)} fusion(bf16[2,48,1536]{2,1,0:T(8,128)(2,1)S(1)} %collective-permute-done.6, bf16[2,48,1536]{2,1,0:T(8,128)(2,1)S(1)} %get-tuple-element.92, pred[]{:T(512)S(6)} %eq.7), kind=kLoop, calls=%fused_computation.22 | loop fusion | flops 6193152 | bytes 1769473 | tf_op jit(solution)/shard_map/add | solution.py:56
  32.2 6.5 %collective-permute-done.5.refs_1_.g1 = bf16[4,96,768]{2,1,0:T(8,128)(2,1)S(1)} collective-permute-done((bf16[4,96,768]{2,1,0:T(8,128)(2,1)S(1)}, bf16[4,96,768]{2,1,0:T(8,128)(2,1)S(1)}, u32[]{:S(2)}, u32[]{:S(2)}) %collective-permute-start.5) | collective-permute-done | bytes 589856 | tf_op jit(solution)/shard_map/ppermute | solution.py:33
  38.7 2.8 %collective-permute-start.12 = (bf16[4,96,768]{2,1,0:T(8,128)(2,1)S(1)}, bf16[4,96,768]{2,1,0:T(8,128)(2,1)S(1)}, u32[]{:S(2)}, u32[]{:S(2)}) collective-permute-start(bf16[4,96,768]{2,1,0:T(8,128)(2,1)S(1)} %collective-permute-done.8.refs_3_.g3), channel_id=1, source_target_pairs={{0,16},{1,17},{2,18},{3,19},{4,20},{5,21},{6,22},{7,23},{8,24},{9,... | collective-permute-start | bytes 1769480 | tf_op jit(solution)/shard_map/ppermute | solution.py:33
  41.5 0.3 collective-permute-start.11
  41.8 0.2 collective-permute-start.10
  42.0 1.3 collective-permute-done.12.refs_7_
  43.3 0.8 collective-permute-done.11.refs_6_
  44.1 1.1 collective-permute-done.10.refs_5_
  45.2 7.0 %act_grad.2 = (bf16[192,1536]{1,0:T(8,128)(2,1)}, bf16[192,1536]{1,0:T(8,128)(2,1)}) custom-call(s32[4]{0:T(128)S(1)} %pad_add_fusion.where, bf16[4,96,768]{2,1,0:T(8,128)(2,1)S(1)} %pad_maximum_fusion.refs_0_.g0, bf16[4,96,768]{2,1,0:T(8,128)(2,1)S(1)} %collective-permute-done.5.refs_1_.g1, bf16[4,96,768]{2,1,0:T(8,128)(2,1)S(1)} %collective-permute-done.7.refs_2_.g2, ...), custom_call_target="tpu_custom_call" | custom-call | flops 1024 | bytes 1024 | tf_op jit(solution)/shard_map/act_grad/pallas_call | solution.py:133
  52.2 3.7 %collective-permute-start.14 = (bf16[192,1536]{1,0:T(8,128)(2,1)}, bf16[192,1536]{1,0:T(8,128)(2,1)}, u32[]{:S(2)}, u32[]{:S(2)}) collective-permute-start(bf16[192,1536]{1,0:T(8,128)(2,1)} %get-tuple-element.53), channel_id=1, source_target_pairs={{0,96},{1,97},{2,98},{3,99},{4,100},{5,101},{6,102},{7,103},{8,104... | collective-permute-start | bytes 1769480 | tf_op jit(solution)/shard_map/ppermute | solution.py:33
  56.0 1.1 copy-done.5
  57.1 1.1 copy-done.7
  58.1 1.1 copy-done.9
  59.2 1.1 copy-done.11
  60.2 7.2 %act_grad.3 = (f32[192,1536]{1,0:T(8,128)S(1)}, f32[192,1536]{1,0:T(8,128)}) custom-call(s32[4]{0:T(128)S(1)} %pad_add_fusion.where, bf16[4,96,768]{2,1,0:T(8,128)(2,1)S(1)} %pad_maximum_fusion.refs_0_.g0, bf16[4,96,768]{2,1,0:T(8,128)(2,1)S(1)} %collective-permute-done.5.refs_1_.g1, bf16[4,96,768]{2,1,0:T(8,128)(2,1)S(1)} %collective-permute-done.7.refs_2_.g2, ...), custom_call_target="tpu_custom_call" | custom-call | flops 8000000000 | bytes 16777216 | tf_op jit(solution)/shard_map/act_grad/pallas_call | solution.py:133
  67.4 1.1 collective-permute-done.14
  68.6 3.1 %collective-permute-done.13 = bf16[192,1536]{1,0:T(8,128)(2,1)} collective-permute-done((bf16[192,1536]{1,0:T(8,128)(2,1)}, bf16[192,1536]{1,0:T(8,128)(2,1)}, u32[]{:S(2)}, u32[]{:S(2)}) %collective-permute-start.13) | collective-permute-done | bytes 589856 | tf_op jit(solution)/shard_map/ppermute | solution.py:33
  71.7 1.5 add_convert_fusion.1
  73.3 2.7 %collective-permute-start.16 = (bf16[96,1536]{1,0:T(8,128)(2,1)S(1)}, bf16[96,1536]{1,0:T(8,128)(2,1)S(1)}, u32[]{:S(2)}, u32[]{:S(2)}) collective-permute-start(bf16[96,1536]{1,0:T(8,128)(2,1)S(1)} %get-tuple-element.88), channel_id=1, source_target_pairs={{0,96},{1,97},{2,98},{3,99},{4,100},{5,101},{6,102},{7,103},{8,104... | collective-permute-start | bytes 884744 | tf_op jit(solution)/shard_map/ppermute | solution.py:33
  75.9 1.0 slice.45
  76.9 1.0 slice.46
  78.0 3.5 %collective-permute-done.15 = bf16[96,1536]{1,0:T(8,128)(2,1)S(1)} collective-permute-done((bf16[96,1536]{1,0:T(8,128)(2,1)S(1)}, bf16[96,1536]{1,0:T(8,128)(2,1)S(1)}, u32[]{:S(2)}, u32[]{:S(2)}) %collective-permute-start.15) | collective-permute-done | bytes 294944 | tf_op jit(solution)/shard_map/ppermute | solution.py:33
  81.5 0.2 convert_add_fusion.3
  81.7 0.1 multiply_convert_fusion.h0
  81.8 2.5 %collective-permute-start.18 = (bf16[4,48,1536]{2,1,0:T(8,128)(2,1)S(1)}, bf16[4,48,1536]{2,1,0:T(8,128)(2,1)S(1)}, u32[]{:S(2)}, u32[]{:S(2)}) collective-permute-start(bf16[4,48,1536]{2,1,0:T(8,128)(2,1)S(1)} %multiply_convert_fusion.h0), channel_id=1, source_target_pairs={{0,96},{1,97},{2,98},{3,99},{4,100},{5,101},{6,102},{7,103},{8,104... | collective-permute-start | bytes 1769480 | tf_op jit(solution)/shard_map/ppermute | solution.py:33
  84.3 10.0 %weight_out_grad.1 = f32[1536,768]{1,0:T(8,128)} custom-call(s32[4]{0:T(128)} %copy-done.12, bf16[1536,1536]{1,0:T(8,128)(2,1)} %all-gather.3.cloned.1.call-done.act, bf16[4,96,768]{2,1,0:T(8,128)(2,1)} %copy-done, bf16[4,96,768]{2,1,0:T(8,128)(2,1)} %copy-done.3, bf16[4,96,768]{2,1,0:T(8,128)(2,1)} %copy-done.2, bf16[4,96,768]{2,1,0:T(8,128)(2,1)} %copy-done.1), custom_call_target="tpu_custom_call" | custom-call | flops 8000000000 | bytes 16777216 | tf_op jit(solution)/shard_map/weight_out_grad/pallas_call | solution.py:246
  94.3 0.1 collective-permute-done.18.h1
  94.4 2.9 %collective-permute-done.17.h3 = bf16[4,48,1536]{2,1,0:T(8,128)(2,1)S(1)} collective-permute-done((bf16[4,48,1536]{2,1,0:T(8,128)(2,1)S(1)}, bf16[4,48,1536]{2,1,0:T(8,128)(2,1)S(1)}, u32[]{:S(2)}, u32[]{:S(2)}) %collective-permute-start.17) | collective-permute-done | bytes 589856 | tf_op jit(solution)/shard_map/ppermute | solution.py:33
  97.4 2.7 %collective-permute-start.20 = (bf16[2,48,1536]{2,1,0:T(8,128)(2,1)S(1)}, bf16[2,48,1536]{2,1,0:T(8,128)(2,1)S(1)}, u32[]{:S(2)}, u32[]{:S(2)}) collective-permute-start(bf16[2,48,1536]{2,1,0:T(8,128)(2,1)S(1)} %slice.52), channel_id=1, source_target_pairs={{0,96},{1,97},{2,98},{3,99},{4,100},{5,101},{6,102},{7,103},{8,104... | collective-permute-start | bytes 884744 | tf_op jit(solution)/shard_map/ppermute | solution.py:33
  100.1 4.1 %collective-permute-done.19.h2a = bf16[2,48,1536]{2,1,0:T(8,128)(2,1)S(1)} collective-permute-done((bf16[2,48,1536]{2,1,0:T(8,128)(2,1)S(1)}, bf16[2,48,1536]{2,1,0:T(8,128)(2,1)S(1)}, u32[]{:S(2)}, u32[]{:S(2)}) %collective-permute-start.19) | collective-permute-done | bytes 294944 | tf_op jit(solution)/shard_map/ppermute | solution.py:33
  104.2 9.7 %input_grad.1 = (f32[4,48,1536]{2,1,0:T(8,128)S(1)}, bf16[4,48,1536]{2,1,0:T(8,128)(2,1)S(1)}, bf16[4,48,1536]{2,1,0:T(8,128)(2,1)S(1)}, bf16[4,48,1536]{2,1,0:T(8,128)(2,1)S(1)}, bf16[4,4,48,1536]{3,2,1,0:T(8,128)(2,1)}) custom-call(s32[4]{0:T(128)S(1)} %copy-done.13, bf16[4,48,1536]{2,1,0:T(8,128)(2,1)S(1)} %multiply_convert_fusion.h0, ...), custom_call_target="tpu_custom_call" | custom-call | flops 1024 | bytes 1024 | tf_op jit(solution)/shard_map/input_grad/pallas_call | solution.py:201
  113.9 5.2 %collective-permute-start.24 = (bf16[4,4,48,1536]{3,2,1,0:T(8,128)(2,1)}, bf16[4,4,48,1536]{3,2,1,0:T(8,128)(2,1)}, u32[]{:S(2)}, u32[]{:S(2)}) collective-permute-start(bf16[4,4,48,1536]{3,2,1,0:T(8,128)(2,1)} %get-tuple-element.79), channel_id=1, source_target_pairs={{0,16},{1,17},{2,18},{3,19},{4,20},{5,21},{6,22},{7,23},{8,24},{9,... | collective-permute-start | bytes 7077896 | tf_op jit(solution)/shard_map/ppermute | solution.py:33
  119.1 2.0 %collective-permute-start.21 = (bf16[4,48,1536]{2,1,0:T(8,128)(2,1)S(1)}, bf16[4,48,1536]{2,1,0:T(8,128)(2,1)S(1)}, u32[]{:S(2)}, u32[]{:S(2)}) collective-permute-start(bf16[4,48,1536]{2,1,0:T(8,128)(2,1)S(1)} %get-tuple-element.75), channel_id=1, source_target_pairs={{0,4},{1,5},{2,6},{3,7},{4,8},{5,9},{6,10},{7,11},{8,12},{9,13},{1... | collective-permute-start | bytes 1769480 | tf_op jit(solution)/shard_map/ppermute | solution.py:33
  121.1 0.7 collective-permute-start.22
  121.8 2.0 %collective-permute-start.23 = (bf16[4,48,1536]{2,1,0:T(8,128)(2,1)S(1)}, bf16[4,48,1536]{2,1,0:T(8,128)(2,1)}, u32[]{:S(2)}, u32[]{:S(2)}) collective-permute-start(bf16[4,48,1536]{2,1,0:T(8,128)(2,1)S(1)} %get-tuple-element.77), channel_id=1, source_target_pairs={{0,8},{1,9},{2,10},{3,11},{4,12},{5,13},{6,14},{7,15},{8,0},{9,1},... | collective-permute-start | bytes 1769480 | tf_op jit(solution)/shard_map/ppermute | solution.py:33
  123.8 9.0 %weight_in_grad.1 = f32[768,1536]{1,0:T(8,128)} custom-call(s32[4]{0:T(128)} %copy-done.12, bf16[16,2,48,768]{3,2,1,0:T(8,128)(2,1)} %bitcast.43, bf16[768,1536]{1,0:T(8,128)(2,1)} %bitcast.44, bf16[768,1536]{1,0:T(8,128)(2,1)} %bitcast.14.hid_other), custom_call_target="tpu_custom_call" | custom-call | flops 8000000000 | bytes 16777216 | tf_op jit(solution)/shard_map/weight_in_grad/pallas_call | solution.py:281
  132.8 3.6 %collective-permute-done.23 = bf16[4,48,1536]{2,1,0:T(8,128)(2,1)} collective-permute-done((bf16[4,48,1536]{2,1,0:T(8,128)(2,1)S(1)}, bf16[4,48,1536]{2,1,0:T(8,128)(2,1)}, u32[]{:S(2)}, u32[]{:S(2)}) %collective-permute-start.23) | collective-permute-done | bytes 589856 | tf_op jit(solution)/shard_map/ppermute | solution.py:33
  136.4 1.5 fusion.16
  138.0 0.4 collective-permute-start.25
  138.4 2.3 %collective-permute-start.27 = (bf16[48,1536]{1,0:T(8,128)(2,1)S(1)}, bf16[48,1536]{1,0:T(8,128)(2,1)S(1)}, u32[]{:S(2)}, u32[]{:S(2)}) collective-permute-start(bf16[48,1536]{1,0:T(8,128)(2,1)S(1)} %get-tuple-element.90), channel_id=1, source_target_pairs={{0,2},{1,3},{2,0},{3,1},{4,6},{5,7},{6,4},{7,5},{8,10},{9,11},{10,... | collective-permute-start | bytes 442376 | tf_op jit(solution)/shard_map/ppermute | solution.py:33
  140.7 0.9 collective-permute-start.26
  141.6 2.0 %collective-permute-done.25 = bf16[48,1536]{1,0:T(8,128)(2,1)S(1)} collective-permute-done((bf16[48,1536]{1,0:T(8,128)(2,1)S(1)}, bf16[48,1536]{1,0:T(8,128)(2,1)S(1)}, u32[]{:S(2)}, u32[]{:S(2)}) %collective-permute-start.25) | collective-permute-done | bytes 147488 | tf_op jit(solution)/shard_map/ppermute | solution.py:33
  143.6 1.3 collective-permute-done.27
  144.9 0.9 collective-permute-done.26
  145.8 1.9 %collective-permute-start.28 = (bf16[48,768]{1,0:T(8,128)(2,1)S(1)}, bf16[48,768]{1,0:T(8,128)(2,1)S(1)}, u32[]{:S(2)}, u32[]{:S(2)}) collective-permute-start(bf16[48,768]{1,0:T(8,128)(2,1)S(1)} %get-tuple-element.95), channel_id=1, source_target_pairs={{0,16},{1,17},{2,18},{3,19},{4,20},{5,21},{6,22},{7,23},{8,24},{9,... | collective-permute-start | bytes 221192 | tf_op jit(solution)/shard_map/ppermute | solution.py:33
  147.8 0.9 collective-permute-done.28
  148.7 0.7 maximum_select_fusion.1
  (58 shorter events, 0.6 us)
Async XLA Ops:
  7.2 4.0 %copy-start.17 = (bf16[96,768]{1,0:T(8,128)(2,1)S(1)}, bf16[96,768]{1,0:T(8,128)(2,1)}, u32[]{:S(2)}) copy-start(bf16[96,768]{1,0:T(8,128)(2,1)} %param.6) | copy-start | bytes 442372
  7.2 48.8 %all-gather.3.cloned.1.call-start = ((), (), s32[]{:S(2)}) async-start(), calls=%async_computation | async-start | bytes 5308416 | tf_op jit(solution)/shard_map/all_gather | solution.py:318
  9.5 16.4 %copy-start.16 = (bf16[192,1536]{1,0:T(8,128)(2,1)S(1)}, bf16[192,1536]{1,0:T(8,128)(2,1)}, u32[]{:S(2)}) copy-start(bf16[192,1536]{1,0:T(8,128)(2,1)} %param.7) | copy-start | bytes 1769476
  9.6 114.2 %all-gather.5.cloned.1.call-start = ((), (), s32[]{:S(2)}) async-start(), calls=%async_computation.1 | async-start | bytes 2506752 | tf_op jit(solution)/shard_map/all_gather | solution.py:336
  9.6 10.2 %collective-permute-start.4 = (bf16[768,1536]{1,0:T(8,128)(2,1)}, bf16[768,1536]{1,0:T(8,128)(2,1)S(1)}, u32[]{:S(2)}, u32[]{:S(2)}) collective-permute-start(bf16[768,1536]{1,0:T(8,128)(2,1)} %w_own.1), channel_id=1, source_target_pairs={{0,16},{1,17},{2,18},{3,19},{4,20},{5,21},{6,22},{7,23},{8,24},{9,... | collective-permute-start | bytes 7077896 | tf_op jit(solution)/shard_map/ppermute | solution.py:33
  11.1 8.7 %collective-permute-start.3 = (bf16[1536,768]{1,0:T(8,128)(2,1)}, bf16[1536,768]{1,0:T(8,128)(2,1)}, u32[]{:S(2)}, u32[]{:S(2)}) collective-permute-start(bf16[1536,768]{1,0:T(8,128)(2,1)} %refs_8_.3), channel_id=1, source_target_pairs={{0,16},{1,17},{2,18},{3,19},{4,20},{5,21},{6,22},{7,23},{8,24},{9,... | collective-permute-start | bytes 7077896 | tf_op jit(solution)/shard_map/ppermute | solution.py:33
  11.2 5.6 %collective-permute-start.1 = (bf16[96,768]{1,0:T(8,128)(2,1)S(1)}, bf16[96,768]{1,0:T(8,128)(2,1)S(1)}, u32[]{:S(2)}, u32[]{:S(2)}) collective-permute-start(bf16[96,768]{1,0:T(8,128)(2,1)S(1)} %copy-done.17), channel_id=1, source_target_pairs={{0,4},{1,5},{2,6},{3,7},{4,8},{5,9},{6,10},{7,11},{8,12},{9,13},{1... | collective-permute-start | bytes 442376 | tf_op jit(solution)/shard_map/ppermute | solution.py:33
  12.6 4.3 %collective-permute-start = (bf16[96,768]{1,0:T(8,128)(2,1)S(1)}, bf16[96,768]{1,0:T(8,128)(2,1)S(1)}, u32[]{:S(2)}, u32[]{:S(2)}) collective-permute-start(bf16[96,768]{1,0:T(8,128)(2,1)S(1)} %copy-done.17), channel_id=1, source_target_pairs={{0,12},{1,13},{2,14},{3,15},{4,0},{5,1},{6,2},{7,3},{8,4},{9,5},{1... | collective-permute-start | bytes 442376 | tf_op jit(solution)/shard_map/ppermute | solution.py:33
  14.0 5.8 %collective-permute-start.2 = (bf16[96,768]{1,0:T(8,128)(2,1)S(1)}, bf16[96,768]{1,0:T(8,128)(2,1)S(1)}, u32[]{:S(2)}, u32[]{:S(2)}) collective-permute-start(bf16[96,768]{1,0:T(8,128)(2,1)S(1)} %copy-done.17), channel_id=1, source_target_pairs={{0,8},{1,9},{2,10},{3,11},{4,12},{5,13},{6,14},{7,15},{8,0},{9,1},... | collective-permute-start | bytes 442376 | tf_op jit(solution)/shard_map/ppermute | solution.py:33
  15.8 40.2 %copy-start.12 = (s32[4]{0:T(128)}, s32[4]{0:T(128)S(1)}, u32[]{:S(2)}) copy-start(s32[4]{0:T(128)S(1)} %pad_add_fusion.where) | copy-start | bytes 52
  19.8 1.4 copy-start.15
  21.3 34.6 %copy-start = (bf16[4,96,768]{2,1,0:T(8,128)(2,1)}, bf16[4,96,768]{2,1,0:T(8,128)(2,1)S(1)}, u32[]{:S(2)}) copy-start(bf16[4,96,768]{2,1,0:T(8,128)(2,1)S(1)} %pad_maximum_fusion.refs_0_.g0) | copy-start | bytes 1769476
  21.3 17.4 %collective-permute-start.8 = (bf16[4,96,768]{2,1,0:T(8,128)(2,1)S(1)}, bf16[4,96,768]{2,1,0:T(8,128)(2,1)S(1)}, u32[]{:S(2)}, u32[]{:S(2)}) collective-permute-start(bf16[4,96,768]{2,1,0:T(8,128)(2,1)S(1)} %pad_maximum_fusion.refs_0_.g0), channel_id=1, source_target_pairs={{0,1},{1,2},{2,3},{3,0},{4,5},{5,6},{6,7},{7,4},{8,9},{9,10},{10,1... | collective-permute-start | bytes 1769480 | tf_op jit(solution)/shard_map/ppermute | solution.py:33
  22.3 19.2 %collective-permute-start.7 = (bf16[4,96,768]{2,1,0:T(8,128)(2,1)S(1)}, bf16[4,96,768]{2,1,0:T(8,128)(2,1)S(1)}, u32[]{:S(2)}, u32[]{:S(2)}) collective-permute-start(bf16[4,96,768]{2,1,0:T(8,128)(2,1)S(1)} %pad_maximum_fusion.refs_0_.g0), channel_id=1, source_target_pairs={{0,2},{1,3},{2,0},{3,1},{4,6},{5,7},{6,4},{7,5},{8,10},{9,11},{10,... | collective-permute-start | bytes 1769480 | tf_op jit(solution)/shard_map/ppermute | solution.py:33
  25.1 13.6 %collective-permute-start.5 = (bf16[4,96,768]{2,1,0:T(8,128)(2,1)S(1)}, bf16[4,96,768]{2,1,0:T(8,128)(2,1)S(1)}, u32[]{:S(2)}, u32[]{:S(2)}) collective-permute-start(bf16[4,96,768]{2,1,0:T(8,128)(2,1)S(1)} %pad_maximum_fusion.refs_0_.g0), channel_id=1, source_target_pairs={{0,3},{1,0},{2,1},{3,2},{4,7},{5,4},{6,5},{7,6},{8,11},{9,8},{10,9... | collective-permute-start | bytes 1769480 | tf_op jit(solution)/shard_map/ppermute | solution.py:33
  26.0 4.4 %collective-permute-start.6 = (bf16[2,48,1536]{2,1,0:T(8,128)(2,1)S(1)}, bf16[2,48,1536]{2,1,0:T(8,128)(2,1)S(1)}, u32[]{:S(2)}, u32[]{:S(2)}) collective-permute-start(bf16[2,48,1536]{2,1,0:T(8,128)(2,1)S(1)} %get-tuple-element.93), channel_id=1, source_target_pairs={{0,16},{1,17},{2,18},{3,19},{4,20},{5,21},{6,22},{7,23},{8,24},{9,... | collective-permute-start | bytes 884744 | tf_op jit(solution)/shard_map/ppermute | solution.py:33
  29.1 12.9 %collective-permute-start.9 = (bf16[4,96,768]{2,1,0:T(8,128)(2,1)S(1)}, bf16[4,96,768]{2,1,0:T(8,128)(2,1)S(1)}, u32[]{:S(2)}, u32[]{:S(2)}) collective-permute-start(bf16[4,96,768]{2,1,0:T(8,128)(2,1)S(1)} %pad_maximum_fusion.refs_0_.g0), channel_id=1, source_target_pairs={{0,16},{1,17},{2,18},{3,19},{4,20},{5,21},{6,22},{7,23},{8,24},{9,... | collective-permute-start | bytes 1769480 | tf_op jit(solution)/shard_map/ppermute | solution.py:33
  38.7 17.3 %copy-start.3 = (bf16[4,96,768]{2,1,0:T(8,128)(2,1)}, bf16[4,96,768]{2,1,0:T(8,128)(2,1)S(1)}, u32[]{:S(2)}) copy-start(bf16[4,96,768]{2,1,0:T(8,128)(2,1)S(1)} %collective-permute-done.5.refs_1_.g1) | copy-start | bytes 1769476
  38.7 17.3 %copy-start.1 = (bf16[4,96,768]{2,1,0:T(8,128)(2,1)}, bf16[4,96,768]{2,1,0:T(8,128)(2,1)S(1)}, u32[]{:S(2)}) copy-start(bf16[4,96,768]{2,1,0:T(8,128)(2,1)S(1)} %collective-permute-done.8.refs_3_.g3) | copy-start | bytes 1769476
  38.7 4.6 %collective-permute-start.12 = (bf16[4,96,768]{2,1,0:T(8,128)(2,1)S(1)}, bf16[4,96,768]{2,1,0:T(8,128)(2,1)S(1)}, u32[]{:S(2)}, u32[]{:S(2)}) collective-permute-start(bf16[4,96,768]{2,1,0:T(8,128)(2,1)S(1)} %collective-permute-done.8.refs_3_.g3), channel_id=1, source_target_pairs={{0,16},{1,17},{2,18},{3,19},{4,20},{5,21},{6,22},{7,23},{8,24},{9,... | collective-permute-start | bytes 1769480 | tf_op jit(solution)/shard_map/ppermute | solution.py:33
  41.5 14.5 %copy-start.2 = (bf16[4,96,768]{2,1,0:T(8,128)(2,1)}, bf16[4,96,768]{2,1,0:T(8,128)(2,1)S(1)}, u32[]{:S(2)}) copy-start(bf16[4,96,768]{2,1,0:T(8,128)(2,1)S(1)} %collective-permute-done.7.refs_2_.g2) | copy-start | bytes 1769476
  41.5 2.7 %collective-permute-start.11 = (bf16[4,96,768]{2,1,0:T(8,128)(2,1)S(1)}, bf16[4,96,768]{2,1,0:T(8,128)(2,1)S(1)}, u32[]{:S(2)}, u32[]{:S(2)}) collective-permute-start(bf16[4,96,768]{2,1,0:T(8,128)(2,1)S(1)} %collective-permute-done.7.refs_2_.g2), channel_id=1, source_target_pairs={{0,16},{1,17},{2,18},{3,19},{4,20},{5,21},{6,22},{7,23},{8,24},{9,... | collective-permute-start | bytes 1769480 | tf_op jit(solution)/shard_map/ppermute | solution.py:33
  41.8 3.4 %collective-permute-start.10 = (bf16[4,96,768]{2,1,0:T(8,128)(2,1)S(1)}, bf16[4,96,768]{2,1,0:T(8,128)(2,1)S(1)}, u32[]{:S(2)}, u32[]{:S(2)}) collective-permute-start(bf16[4,96,768]{2,1,0:T(8,128)(2,1)S(1)} %collective-permute-done.5.refs_1_.g1), channel_id=1, source_target_pairs={{0,16},{1,17},{2,18},{3,19},{4,20},{5,21},{6,22},{7,23},{8,24},{9,... | collective-permute-start | bytes 1769480 | tf_op jit(solution)/shard_map/ppermute | solution.py:33
  42.0 10.2 %copy-start.4 = (bf16[4,96,768]{2,1,0:T(8,128)(2,1)}, bf16[4,96,768]{2,1,0:T(8,128)(2,1)S(1)}, u32[]{:S(2)}) copy-start(bf16[4,96,768]{2,1,0:T(8,128)(2,1)S(1)} %collective-permute-done.9.refs_4_) | copy-start | bytes 1769476
  43.3 8.9 %copy-start.6 = (bf16[4,96,768]{2,1,0:T(8,128)(2,1)}, bf16[4,96,768]{2,1,0:T(8,128)(2,1)S(1)}, u32[]{:S(2)}) copy-start(bf16[4,96,768]{2,1,0:T(8,128)(2,1)S(1)} %collective-permute-done.12.refs_7_) | copy-start | bytes 1769476
  44.1 8.1 %copy-start.8 = (bf16[4,96,768]{2,1,0:T(8,128)(2,1)}, bf16[4,96,768]{2,1,0:T(8,128)(2,1)S(1)}, u32[]{:S(2)}) copy-start(bf16[4,96,768]{2,1,0:T(8,128)(2,1)S(1)} %collective-permute-done.11.refs_6_) | copy-start | bytes 1769476
  45.2 7.0 %copy-start.10 = (bf16[4,96,768]{2,1,0:T(8,128)(2,1)}, bf16[4,96,768]{2,1,0:T(8,128)(2,1)S(1)}, u32[]{:S(2)}) copy-start(bf16[4,96,768]{2,1,0:T(8,128)(2,1)S(1)} %collective-permute-done.10.refs_5_) | copy-start | bytes 1769476
  52.2 16.4 %collective-permute-start.14 = (bf16[192,1536]{1,0:T(8,128)(2,1)}, bf16[192,1536]{1,0:T(8,128)(2,1)}, u32[]{:S(2)}, u32[]{:S(2)}) collective-permute-start(bf16[192,1536]{1,0:T(8,128)(2,1)} %get-tuple-element.53), channel_id=1, source_target_pairs={{0,96},{1,97},{2,98},{3,99},{4,100},{5,101},{6,102},{7,103},{8,104... | collective-permute-start | bytes 1769480 | tf_op jit(solution)/shard_map/ppermute | solution.py:33
  55.9 15.7 %collective-permute-start.13 = (bf16[192,1536]{1,0:T(8,128)(2,1)}, bf16[192,1536]{1,0:T(8,128)(2,1)}, u32[]{:S(2)}, u32[]{:S(2)}) collective-permute-start(bf16[192,1536]{1,0:T(8,128)(2,1)} %get-tuple-element.51), channel_id=1, source_target_pairs={{0,32},{1,33},{2,34},{3,35},{4,36},{5,37},{6,38},{7,39},{8,40},{9,... | collective-permute-start | bytes 1769480 | tf_op jit(solution)/shard_map/ppermute | solution.py:33
  56.0 1.1 copy-start.5
  57.1 1.1 copy-start.7
  58.1 1.1 copy-start.9
  59.2 1.1 copy-start.11
  73.2 8.3 %collective-permute-start.15 = (bf16[96,1536]{1,0:T(8,128)(2,1)S(1)}, bf16[96,1536]{1,0:T(8,128)(2,1)S(1)}, u32[]{:S(2)}, u32[]{:S(2)}) collective-permute-start(bf16[96,1536]{1,0:T(8,128)(2,1)S(1)} %get-tuple-element.87), channel_id=1, source_target_pairs={{0,32},{1,33},{2,34},{3,35},{4,36},{5,37},{6,38},{7,39},{8,40},{9,... | collective-permute-start | bytes 884744 | tf_op jit(solution)/shard_map/ppermute | solution.py:33
  73.3 8.2 %collective-permute-start.16 = (bf16[96,1536]{1,0:T(8,128)(2,1)S(1)}, bf16[96,1536]{1,0:T(8,128)(2,1)S(1)}, u32[]{:S(2)}, u32[]{:S(2)}) collective-permute-start(bf16[96,1536]{1,0:T(8,128)(2,1)S(1)} %get-tuple-element.88), channel_id=1, source_target_pairs={{0,96},{1,97},{2,98},{3,99},{4,100},{5,101},{6,102},{7,103},{8,104... | collective-permute-start | bytes 884744 | tf_op jit(solution)/shard_map/ppermute | solution.py:33
  77.9 3.7 %copy-start.14 = (f32[4,48,1536]{2,1,0:T(8,128)S(1)}, f32[4,48,1536]{2,1,0:T(8,128)}, u32[]{:S(2)}) copy-start(f32[4,48,1536]{2,1,0:T(8,128)} %fusion.10) | copy-start | bytes 3538948
  81.8 12.5 %collective-permute-start.18 = (bf16[4,48,1536]{2,1,0:T(8,128)(2,1)S(1)}, bf16[4,48,1536]{2,1,0:T(8,128)(2,1)S(1)}, u32[]{:S(2)}, u32[]{:S(2)}) collective-permute-start(bf16[4,48,1536]{2,1,0:T(8,128)(2,1)S(1)} %multiply_convert_fusion.h0), channel_id=1, source_target_pairs={{0,96},{1,97},{2,98},{3,99},{4,100},{5,101},{6,102},{7,103},{8,104... | collective-permute-start | bytes 1769480 | tf_op jit(solution)/shard_map/ppermute | solution.py:33
  84.3 13.0 %collective-permute-start.17 = (bf16[4,48,1536]{2,1,0:T(8,128)(2,1)S(1)}, bf16[4,48,1536]{2,1,0:T(8,128)(2,1)S(1)}, u32[]{:S(2)}, u32[]{:S(2)}) collective-permute-start(bf16[4,48,1536]{2,1,0:T(8,128)(2,1)S(1)} %multiply_convert_fusion.h0), channel_id=1, source_target_pairs={{0,32},{1,33},{2,34},{3,35},{4,36},{5,37},{6,38},{7,39},{8,40},{9,... | collective-permute-start | bytes 1769480 | tf_op jit(solution)/shard_map/ppermute | solution.py:33
  94.3 9.9 %copy-start.13 = (s32[4]{0:T(128)S(1)}, s32[4]{0:T(128)}, u32[]{:S(2)}) copy-start(s32[4]{0:T(128)} %copy-done.12) | copy-start | bytes 52
  97.3 6.9 %collective-permute-start.19 = (bf16[2,48,1536]{2,1,0:T(8,128)(2,1)S(1)}, bf16[2,48,1536]{2,1,0:T(8,128)(2,1)S(1)}, u32[]{:S(2)}, u32[]{:S(2)}) collective-permute-start(bf16[2,48,1536]{2,1,0:T(8,128)(2,1)S(1)} %slice.51), channel_id=1, source_target_pairs={{0,32},{1,33},{2,34},{3,35},{4,36},{5,37},{6,38},{7,39},{8,40},{9,... | collective-permute-start | bytes 884744 | tf_op jit(solution)/shard_map/ppermute | solution.py:33
  97.4 6.8 %collective-permute-start.20 = (bf16[2,48,1536]{2,1,0:T(8,128)(2,1)S(1)}, bf16[2,48,1536]{2,1,0:T(8,128)(2,1)S(1)}, u32[]{:S(2)}, u32[]{:S(2)}) collective-permute-start(bf16[2,48,1536]{2,1,0:T(8,128)(2,1)S(1)} %slice.52), channel_id=1, source_target_pairs={{0,96},{1,97},{2,98},{3,99},{4,100},{5,101},{6,102},{7,103},{8,104... | collective-permute-start | bytes 884744 | tf_op jit(solution)/shard_map/ppermute | solution.py:33
  113.9 9.8 %collective-permute-start.24 = (bf16[4,4,48,1536]{3,2,1,0:T(8,128)(2,1)}, bf16[4,4,48,1536]{3,2,1,0:T(8,128)(2,1)}, u32[]{:S(2)}, u32[]{:S(2)}) collective-permute-start(bf16[4,4,48,1536]{3,2,1,0:T(8,128)(2,1)} %get-tuple-element.79), channel_id=1, source_target_pairs={{0,16},{1,17},{2,18},{3,19},{4,20},{5,21},{6,22},{7,23},{8,24},{9,... | collective-permute-start | bytes 7077896 | tf_op jit(solution)/shard_map/ppermute | solution.py:33
  119.1 13.7 %collective-permute-start.21 = (bf16[4,48,1536]{2,1,0:T(8,128)(2,1)S(1)}, bf16[4,48,1536]{2,1,0:T(8,128)(2,1)S(1)}, u32[]{:S(2)}, u32[]{:S(2)}) collective-permute-start(bf16[4,48,1536]{2,1,0:T(8,128)(2,1)S(1)} %get-tuple-element.75), channel_id=1, source_target_pairs={{0,4},{1,5},{2,6},{3,7},{4,8},{5,9},{6,10},{7,11},{8,12},{9,13},{1... | collective-permute-start | bytes 1769480 | tf_op jit(solution)/shard_map/ppermute | solution.py:33
  121.1 11.7 %collective-permute-start.22 = (bf16[4,48,1536]{2,1,0:T(8,128)(2,1)S(1)}, bf16[4,48,1536]{2,1,0:T(8,128)(2,1)}, u32[]{:S(2)}, u32[]{:S(2)}) collective-permute-start(bf16[4,48,1536]{2,1,0:T(8,128)(2,1)S(1)} %get-tuple-element.76), channel_id=1, source_target_pairs={{0,12},{1,13},{2,14},{3,15},{4,0},{5,1},{6,2},{7,3},{8,4},{9,5},{1... | collective-permute-start | bytes 1769480 | tf_op jit(solution)/shard_map/ppermute | solution.py:33
  121.8 14.7 %collective-permute-start.23 = (bf16[4,48,1536]{2,1,0:T(8,128)(2,1)S(1)}, bf16[4,48,1536]{2,1,0:T(8,128)(2,1)}, u32[]{:S(2)}, u32[]{:S(2)}) collective-permute-start(bf16[4,48,1536]{2,1,0:T(8,128)(2,1)S(1)} %get-tuple-element.77), channel_id=1, source_target_pairs={{0,8},{1,9},{2,10},{3,11},{4,12},{5,13},{6,14},{7,15},{8,0},{9,1},... | collective-permute-start | bytes 1769480 | tf_op jit(solution)/shard_map/ppermute | solution.py:33
  138.0 5.6 %collective-permute-start.25 = (bf16[48,1536]{1,0:T(8,128)(2,1)S(1)}, bf16[48,1536]{1,0:T(8,128)(2,1)S(1)}, u32[]{:S(2)}, u32[]{:S(2)}) collective-permute-start(bf16[48,1536]{1,0:T(8,128)(2,1)S(1)} %get-tuple-element.89), channel_id=1, source_target_pairs={{0,1},{1,2},{2,3},{3,0},{4,5},{5,6},{6,7},{7,4},{8,9},{9,10},{10,1... | collective-permute-start | bytes 442376 | tf_op jit(solution)/shard_map/ppermute | solution.py:33
  138.4 6.4 %collective-permute-start.27 = (bf16[48,1536]{1,0:T(8,128)(2,1)S(1)}, bf16[48,1536]{1,0:T(8,128)(2,1)S(1)}, u32[]{:S(2)}, u32[]{:S(2)}) collective-permute-start(bf16[48,1536]{1,0:T(8,128)(2,1)S(1)} %get-tuple-element.90), channel_id=1, source_target_pairs={{0,2},{1,3},{2,0},{3,1},{4,6},{5,7},{6,4},{7,5},{8,10},{9,11},{10,... | collective-permute-start | bytes 442376 | tf_op jit(solution)/shard_map/ppermute | solution.py:33
  140.7 5.0 %collective-permute-start.26 = (bf16[48,1536]{1,0:T(8,128)(2,1)S(1)}, bf16[48,1536]{1,0:T(8,128)(2,1)S(1)}, u32[]{:S(2)}, u32[]{:S(2)}) collective-permute-start(bf16[48,1536]{1,0:T(8,128)(2,1)S(1)} %get-tuple-element.91), channel_id=1, source_target_pairs={{0,3},{1,0},{2,1},{3,2},{4,7},{5,4},{6,5},{7,6},{8,11},{9,8},{10,9... | collective-permute-start | bytes 442376 | tf_op jit(solution)/shard_map/ppermute | solution.py:33
  145.8 2.9 %collective-permute-start.28 = (bf16[48,768]{1,0:T(8,128)(2,1)S(1)}, bf16[48,768]{1,0:T(8,128)(2,1)S(1)}, u32[]{:S(2)}, u32[]{:S(2)}) collective-permute-start(bf16[48,768]{1,0:T(8,128)(2,1)S(1)} %get-tuple-element.95), channel_id=1, source_target_pairs={{0,16},{1,17},{2,18},{3,19},{4,20},{5,21},{6,22},{7,23},{8,24},{9,... | collective-permute-start | bytes 221192 | tf_op jit(solution)/shard_map/ppermute | solution.py:33
Sparse Core Ops, SparseCore 0:
  9.7 38.1 all-gather.2
  78.1 43.8 all-gather.4

commit v3 on v2

--- a/solution.py
+++ b/solution.py
@@ -332,7 +332,7 @@
     half = N * K // 2
     to_up, to_down = act_grad_parts(0, where, g_stacks, g_others, weight_out, w_out_other)
     from_down, from_up = along_z(to_up, 1), along_z(to_down, -1)
-    g_stacks, g_others, act_all, to_up, x_late = hold((g_stacks, g_others, act_all, to_up, layer_input))
+    g_stacks, g_others, to_up, x_late = hold((g_stacks, g_others, to_up, layer_input))
     x_all = lax.all_gather(x_late, "col", axis=0, tiled=True)
     own, relay = act_grad_parts(1, where, g_stacks, g_others, weight_out, w_out_other)
     from_down, from_up, own, relay = hold((from_down, from_up, own, relay))

time: 157 us -> 154 us (0.981)
  local copies, waits for them, and re-layouts: 7.79 us -> 1.58 us
  waiting for transfers between devices: 38.5 us -> 43.7 us
    ppermute x29, waiting for transfers between devices: 38.4 us -> 43.6 us  [permute(): return lax.ppermute(array, AXES, pairs)]
    unnamed x36 -> x24, local copies, waits for them, and re-layouts: 5.7 us -> 1.44 us
    slice x2 -> x4, local copies, waits for them, and re-layouts: 1.96 us -> 0.01 us  [on_device(): rest = jnp.concatenate([from_up[:half], from_down[half:]]).astype(F32)]
  transfers between devices with their start and end apart: 31 -> 31, of which waited for: 18 -> 18; matrix products, arithmetic and copies ran while one was open for 3% -> 3% of each run, Pallas kernels for 27% -> 28%
where the time goes in v3:
time: 154 us
  starting transfers between devices  44.3 us (29%)
  waiting for transfers between devices  43.7 us (28%)
  Pallas kernels  42.9 us (28%)
  between operations  14.3 us (9%)
  other arithmetic  7.3 us (5%)
  local copies, waits for them, and re-layouts  1.58 us (1%)
    ppermute x29, starting transfers between devices, permute(): return lax.ppermute(array, AXES, pairs)  44.2 us
    ppermute x29, waiting for transfers between devices, permute(): return lax.ppermute(array, AXES, pairs)  43.6 us
    pallas_call x2, Pallas kernels, act_grad_parts(): pl.pallas_call(functools.partial(act_grad_kernel, part), out_shape=[jax.S...  13.4 us
    pallas_call x1, Pallas kernels, input_grad_parts(): pl.pallas_call(input_grad_kernel, out_shape=[jax.ShapeDtypeStruct((N, n,...  10.5 us
    pallas_call x1, Pallas kernels, weight_out_grad_of(): pl.pallas_call(weight_out_grad_kernel, out_shape=jax.ShapeDtypeStruct((hi...  9.98 us
    pallas_call x1, Pallas kernels, weight_in_grad_of(): pl.pallas_call(weight_in_grad_kernel, out_shape=jax.ShapeDtypeStruct((wid...  9.02 us
  transfers between devices with their start and end apart: 31, of which 18 were waited for; matrix products, arithmetic and copies ran while one was open for 3% of the time, Pallas kernels for 28%

profile of v3, /device:TPU:1, one launch (start us, length us, event | category | flops | bytes accessed | tf_op | source)
XLA Modules:
  0.0 153.9 jit_solution(6362842472085253999)
XLA Ops:
  7.2 0.0 all-gather.3.cloned.1.call-start
  7.2 2.3 %fusion.1 = bf16[192,1536]{1,0:T(8,128)(2,1)} fusion(bf16[192,1536]{1,0:T(8,128)(2,1)} %param.7), kind=kLoop, calls=%fused_computation.13 | loop fusion | flops 2949120 | bytes 1179648 | tf_op jit(solution)/shard_map/convert_element_type | solution.py:317
  9.6 0.0 all-gather.5.cloned.1.call-start
  9.6 1.5 collective-permute-start.4
  11.1 0.1 collective-permute-start.3
  11.2 1.4 collective-permute-start.1
  12.6 1.4 collective-permute-start
  14.1 1.6 %collective-permute-start.2 = (bf16[96,768]{1,0:T(8,128)(2,1)S(1)}, bf16[96,768]{1,0:T(8,128)(2,1)S(1)}, u32[]{:S(2)}, u32[]{:S(2)}) collective-permute-start(bf16[96,768]{1,0:T(8,128)(2,1)S(1)} %copy-done.11), channel_id=1, source_target_pairs={{0,8},{1,9},{2,10},{3,11},{4,12},{5,13},{6,14},{7,15},{8,0},{9,1},... | collective-permute-start | bytes 442376 | tf_op jit(solution)/shard_map/ppermute | solution.py:33
  15.7 0.1 pad_add_fusion.where
  15.8 1.1 collective-permute-done.1
  16.9 2.9 %collective-permute-done.2 = bf16[96,768]{1,0:T(8,128)(2,1)S(1)} collective-permute-done((bf16[96,768]{1,0:T(8,128)(2,1)S(1)}, bf16[96,768]{1,0:T(8,128)(2,1)S(1)}, u32[]{:S(2)}, u32[]{:S(2)}) %collective-permute-start.2) | collective-permute-done | bytes 147488 | tf_op jit(solution)/shard_map/ppermute | solution.py:33
  19.9 1.4 copy-done.7
  21.3 0.1 pad_maximum_fusion.refs_0_.g0
  21.3 1.0 collective-permute-start.8
  22.3 2.7 %collective-permute-start.7 = (bf16[4,96,768]{2,1,0:T(8,128)(2,1)S(1)}, bf16[4,96,768]{2,1,0:T(8,128)(2,1)S(1)}, u32[]{:S(2)}, u32[]{:S(2)}) collective-permute-start(bf16[4,96,768]{2,1,0:T(8,128)(2,1)S(1)} %pad_maximum_fusion.refs_0_.g0), channel_id=1, source_target_pairs={{0,2},{1,3},{2,0},{3,1},{4,6},{5,7},{6,4},{7,5},{8,10},{9,11},{10,... | collective-permute-start | bytes 1769480 | tf_op jit(solution)/shard_map/ppermute | solution.py:33
  25.1 0.9 collective-permute-start.5
  26.0 3.2 %collective-permute-start.6 = (bf16[2,48,1536]{2,1,0:T(8,128)(2,1)S(1)}, bf16[2,48,1536]{2,1,0:T(8,128)(2,1)S(1)}, u32[]{:S(2)}, u32[]{:S(2)}) collective-permute-start(bf16[2,48,1536]{2,1,0:T(8,128)(2,1)S(1)} %get-tuple-element.91), channel_id=1, source_target_pairs={{0,16},{1,17},{2,18},{3,19},{4,20},{5,21},{6,22},{7,23},{8,24},{9,... | collective-permute-start | bytes 884744 | tf_op jit(solution)/shard_map/ppermute | solution.py:33
  29.1 0.1 collective-permute-start.9
  29.2 1.1 collective-permute-done.6
  30.3 1.9 %fusion.10 = f32[4,48,1536]{2,1,0:T(8,128)} fusion(bf16[2,48,1536]{2,1,0:T(8,128)(2,1)S(1)} %collective-permute-done.6, bf16[2,48,1536]{2,1,0:T(8,128)(2,1)S(1)} %get-tuple-element.90, pred[]{:T(512)S(6)} %eq.7), kind=kLoop, calls=%fused_computation.22 | loop fusion | flops 6193152 | bytes 1769473 | tf_op jit(solution)/shard_map/add | solution.py:56
  32.2 6.5 %collective-permute-done.5.refs_1_.g1 = bf16[4,96,768]{2,1,0:T(8,128)(2,1)S(1)} collective-permute-done((bf16[4,96,768]{2,1,0:T(8,128)(2,1)S(1)}, bf16[4,96,768]{2,1,0:T(8,128)(2,1)S(1)}, u32[]{:S(2)}, u32[]{:S(2)}) %collective-permute-start.5) | collective-permute-done | bytes 589856 | tf_op jit(solution)/shard_map/ppermute | solution.py:33
  38.7 2.8 %collective-permute-start.12 = (bf16[4,96,768]{2,1,0:T(8,128)(2,1)S(1)}, bf16[4,96,768]{2,1,0:T(8,128)(2,1)S(1)}, u32[]{:S(2)}, u32[]{:S(2)}) collective-permute-start(bf16[4,96,768]{2,1,0:T(8,128)(2,1)S(1)} %collective-permute-done.8.refs_3_.g3), channel_id=1, source_target_pairs={{0,16},{1,17},{2,18},{3,19},{4,20},{5,21},{6,22},{7,23},{8,24},{9,... | collective-permute-start | bytes 1769480 | tf_op jit(solution)/shard_map/ppermute | solution.py:33
  41.5 0.3 collective-permute-start.11
  41.8 0.2 collective-permute-start.10
  42.0 1.3 collective-permute-done.12.refs_7_
  43.3 0.8 collective-permute-done.11.refs_6_
  44.2 1.1 collective-permute-done.10.refs_5_
  45.2 6.2 %act_grad.2 = (bf16[192,1536]{1,0:T(8,128)(2,1)S(1)}, bf16[192,1536]{1,0:T(8,128)(2,1)S(1)}) custom-call(s32[4]{0:T(128)S(1)} %pad_add_fusion.where, bf16[4,96,768]{2,1,0:T(8,128)(2,1)S(1)} %pad_maximum_fusion.refs_0_.g0, bf16[4,96,768]{2,1,0:T(8,128)(2,1)S(1)} %collective-permute-done.5.refs_1_.g1, ...), custom_call_target="tpu_custom_call" | custom-call | flops 1024 | bytes 1024 | tf_op jit(solution)/shard_map/act_grad/pallas_call | solution.py:133
  51.4 1.8 %collective-permute-start.13 = (bf16[192,1536]{1,0:T(8,128)(2,1)S(1)}, bf16[192,1536]{1,0:T(8,128)(2,1)S(1)}, u32[]{:S(2)}, u32[]{:S(2)}) collective-permute-start(bf16[192,1536]{1,0:T(8,128)(2,1)S(1)} %get-tuple-element.50), channel_id=1, source_target_pairs={{0,32},{1,33},{2,34},{3,35},{4,36},{5,37},{6,38},{7,39},{8,40},{9,... | collective-permute-start | bytes 1769480 | tf_op jit(solution)/shard_map/ppermute | solution.py:33
  53.2 2.0 %collective-permute-start.14 = (bf16[192,1536]{1,0:T(8,128)(2,1)S(1)}, bf16[192,1536]{1,0:T(8,128)(2,1)S(1)}, u32[]{:S(2)}, u32[]{:S(2)}) collective-permute-start(bf16[192,1536]{1,0:T(8,128)(2,1)S(1)} %get-tuple-element.51), channel_id=1, source_target_pairs={{0,96},{1,97},{2,98},{3,99},{4,100},{5,101},{6,102},{7,103},{8,104... | collective-permute-start | bytes 1769480 | tf_op jit(solution)/shard_map/ppermute | solution.py:33
  55.2 7.2 %act_grad.3 = (f32[192,1536]{1,0:T(8,128)S(1)}, f32[192,1536]{1,0:T(8,128)}) custom-call(s32[4]{0:T(128)S(1)} %pad_add_fusion.where, bf16[4,96,768]{2,1,0:T(8,128)(2,1)S(1)} %pad_maximum_fusion.refs_0_.g0, bf16[4,96,768]{2,1,0:T(8,128)(2,1)S(1)} %collective-permute-done.5.refs_1_.g1, bf16[4,96,768]{2,1,0:T(8,128)(2,1)S(1)} %collective-permute-done.7.refs_2_.g2, ...), custom_call_target="tpu_custom_call" | custom-call | flops 8000000000 | bytes 16777216 | tf_op jit(solution)/shard_map/act_grad/pallas_call | solution.py:133
  62.5 5.1 %collective-permute-done.14 = bf16[192,1536]{1,0:T(8,128)(2,1)S(1)} collective-permute-done((bf16[192,1536]{1,0:T(8,128)(2,1)S(1)}, bf16[192,1536]{1,0:T(8,128)(2,1)S(1)}, u32[]{:S(2)}, u32[]{:S(2)}) %collective-permute-start.14) | collective-permute-done | bytes 589856 | tf_op jit(solution)/shard_map/ppermute | solution.py:33
  67.6 1.0 collective-permute-done.13
  68.5 1.6 %add_convert_fusion.1 = (bf16[96,1536]{1,0:T(8,128)(2,1)S(1)}, bf16[96,1536]{1,0:T(8,128)(2,1)S(1)}) fusion(f32[192,1536]{1,0:T(8,128)} %get-tuple-element.65, bf16[192,1536]{1,0:T(8,128)(2,1)S(1)} %collective-permute-done.13, bf16[192,1536]{1,0:T(8,128)(2,1)S(1)} %collective-permute-done.14), kind=kLoop, calls=%fused_computation.30 | loop fusion | flops 884736 | bytes 2359296 | tf_op jit(solution)/shard_map/convert_element_type | solution.py:339
  70.1 1.2 collective-permute-start.15
  71.3 2.0 %collective-permute-start.16 = (bf16[96,1536]{1,0:T(8,128)(2,1)S(1)}, bf16[96,1536]{1,0:T(8,128)(2,1)S(1)}, u32[]{:S(2)}, u32[]{:S(2)}) collective-permute-start(bf16[96,1536]{1,0:T(8,128)(2,1)S(1)} %get-tuple-element.86), channel_id=1, source_target_pairs={{0,96},{1,97},{2,98},{3,99},{4,100},{5,101},{6,102},{7,103},{8,104... | collective-permute-start | bytes 884744 | tf_op jit(solution)/shard_map/ppermute | solution.py:33
  73.4 6.0 %collective-permute-done.15 = bf16[96,1536]{1,0:T(8,128)(2,1)S(1)} collective-permute-done((bf16[96,1536]{1,0:T(8,128)(2,1)S(1)}, bf16[96,1536]{1,0:T(8,128)(2,1)S(1)}, u32[]{:S(2)}, u32[]{:S(2)}) %collective-permute-start.15) | collective-permute-done | bytes 294944 | tf_op jit(solution)/shard_map/ppermute | solution.py:33
  79.4 0.2 convert_add_fusion.3
  79.6 0.1 multiply_convert_fusion.h0
  79.8 2.5 %collective-permute-start.18 = (bf16[4,48,1536]{2,1,0:T(8,128)(2,1)S(1)}, bf16[4,48,1536]{2,1,0:T(8,128)(2,1)S(1)}, u32[]{:S(2)}, u32[]{:S(2)}) collective-permute-start(bf16[4,48,1536]{2,1,0:T(8,128)(2,1)S(1)} %multiply_convert_fusion.h0), channel_id=1, source_target_pairs={{0,96},{1,97},{2,98},{3,99},{4,100},{5,101},{6,102},{7,103},{8,104... | collective-permute-start | bytes 1769480 | tf_op jit(solution)/shard_map/ppermute | solution.py:33
  82.3 10.0 %weight_out_grad.1 = f32[1536,768]{1,0:T(8,128)} custom-call(s32[4]{0:T(128)} %copy-done.4, bf16[1536,1536]{1,0:T(8,128)(2,1)} %all-gather.3.cloned.1.call-done.act, bf16[4,96,768]{2,1,0:T(8,128)(2,1)} %copy-done, bf16[4,96,768]{2,1,0:T(8,128)(2,1)} %copy-done.3, bf16[4,96,768]{2,1,0:T(8,128)(2,1)} %copy-done.2, bf16[4,96,768]{2,1,0:T(8,128)(2,1)} %copy-done.1), custom_call_target="tpu_custom_call" | custom-call | flops 8000000000 | bytes 16777216 | tf_op jit(solution)/shard_map/weight_out_grad/pallas_call | solution.py:246
  92.3 0.6 collective-permute-done.18.h1
  92.9 3.1 %collective-permute-done.17.h3 = bf16[4,48,1536]{2,1,0:T(8,128)(2,1)S(1)} collective-permute-done((bf16[4,48,1536]{2,1,0:T(8,128)(2,1)S(1)}, bf16[4,48,1536]{2,1,0:T(8,128)(2,1)S(1)}, u32[]{:S(2)}, u32[]{:S(2)}) %collective-permute-start.17) | collective-permute-done | bytes 589856 | tf_op jit(solution)/shard_map/ppermute | solution.py:33
  96.1 0.1 collective-permute-start.19
  96.1 2.7 %collective-permute-start.20 = (bf16[2,48,1536]{2,1,0:T(8,128)(2,1)S(1)}, bf16[2,48,1536]{2,1,0:T(8,128)(2,1)S(1)}, u32[]{:S(2)}, u32[]{:S(2)}) collective-permute-start(bf16[2,48,1536]{2,1,0:T(8,128)(2,1)S(1)} %slice.52), channel_id=1, source_target_pairs={{0,96},{1,97},{2,98},{3,99},{4,100},{5,101},{6,102},{7,103},{8,104... | collective-permute-start | bytes 884744 | tf_op jit(solution)/shard_map/ppermute | solution.py:33
  98.8 4.1 %collective-permute-done.19.h2a = bf16[2,48,1536]{2,1,0:T(8,128)(2,1)S(1)} collective-permute-done((bf16[2,48,1536]{2,1,0:T(8,128)(2,1)S(1)}, bf16[2,48,1536]{2,1,0:T(8,128)(2,1)S(1)}, u32[]{:S(2)}, u32[]{:S(2)}) %collective-permute-start.19) | collective-permute-done | bytes 294944 | tf_op jit(solution)/shard_map/ppermute | solution.py:33
  102.9 10.5 %input_grad.1 = (f32[4,48,1536]{2,1,0:T(8,128)S(1)}, bf16[4,48,1536]{2,1,0:T(8,128)(2,1)}, bf16[4,48,1536]{2,1,0:T(8,128)(2,1)S(1)}, bf16[4,48,1536]{2,1,0:T(8,128)(2,1)}, bf16[4,4,48,1536]{3,2,1,0:T(8,128)(2,1)}) custom-call(s32[4]{0:T(128)S(1)} %copy-done.5, bf16[4,48,1536]{2,1,0:T(8,128)(2,1)S(1)} %multiply_convert_fusion.h0, ...), custom_call_target="tpu_custom_call" | custom-call | flops 1024 | bytes 1024 | tf_op jit(solution)/shard_map/input_grad/pallas_call | solution.py:201
  113.4 4.5 %collective-permute-start.24 = (bf16[4,4,48,1536]{3,2,1,0:T(8,128)(2,1)}, bf16[4,4,48,1536]{3,2,1,0:T(8,128)(2,1)}, u32[]{:S(2)}, u32[]{:S(2)}) collective-permute-start(bf16[4,4,48,1536]{3,2,1,0:T(8,128)(2,1)} %get-tuple-element.77), channel_id=1, source_target_pairs={{0,16},{1,17},{2,18},{3,19},{4,20},{5,21},{6,22},{7,23},{8,24},{9,... | collective-permute-start | bytes 7077896 | tf_op jit(solution)/shard_map/ppermute | solution.py:33
  117.9 2.0 %collective-permute-start.21 = (bf16[4,48,1536]{2,1,0:T(8,128)(2,1)}, bf16[4,48,1536]{2,1,0:T(8,128)(2,1)S(1)}, u32[]{:S(2)}, u32[]{:S(2)}) collective-permute-start(bf16[4,48,1536]{2,1,0:T(8,128)(2,1)} %get-tuple-element.73), channel_id=1, source_target_pairs={{0,4},{1,5},{2,6},{3,7},{4,8},{5,9},{6,10},{7,11},{8,12},{9,13},{1... | collective-permute-start | bytes 1769480 | tf_op jit(solution)/shard_map/ppermute | solution.py:33
  119.8 0.7 collective-permute-start.22
  120.5 2.0 %collective-permute-start.23 = (bf16[4,48,1536]{2,1,0:T(8,128)(2,1)S(1)}, bf16[4,48,1536]{2,1,0:T(8,128)(2,1)S(1)}, u32[]{:S(2)}, u32[]{:S(2)}) collective-permute-start(bf16[4,48,1536]{2,1,0:T(8,128)(2,1)S(1)} %get-tuple-element.75), channel_id=1, source_target_pairs={{0,8},{1,9},{2,10},{3,11},{4,12},{5,13},{6,14},{7,15},{8,0},{9,1},... | collective-permute-start | bytes 1769480 | tf_op jit(solution)/shard_map/ppermute | solution.py:33
  122.5 9.0 %weight_in_grad.1 = f32[768,1536]{1,0:T(8,128)} custom-call(s32[4]{0:T(128)} %copy-done.4, bf16[16,2,48,768]{3,2,1,0:T(8,128)(2,1)} %bitcast.43, bf16[768,1536]{1,0:T(8,128)(2,1)} %bitcast.44, bf16[768,1536]{1,0:T(8,128)(2,1)} %bitcast.14.hid_other), custom_call_target="tpu_custom_call" | custom-call | flops 8000000000 | bytes 16777216 | tf_op jit(solution)/shard_map/weight_in_grad/pallas_call | solution.py:281
  131.5 3.8 %collective-permute-done.23 = bf16[4,48,1536]{2,1,0:T(8,128)(2,1)S(1)} collective-permute-done((bf16[4,48,1536]{2,1,0:T(8,128)(2,1)S(1)}, bf16[4,48,1536]{2,1,0:T(8,128)(2,1)S(1)}, u32[]{:S(2)}, u32[]{:S(2)}) %collective-permute-start.23) | collective-permute-done | bytes 589856 | tf_op jit(solution)/shard_map/ppermute | solution.py:33
  135.3 0.3 fusion.16
  135.6 0.4 collective-permute-start.25
  136.0 2.3 %collective-permute-start.27 = (bf16[48,1536]{1,0:T(8,128)(2,1)S(1)}, bf16[48,1536]{1,0:T(8,128)(2,1)S(1)}, u32[]{:S(2)}, u32[]{:S(2)}) collective-permute-start(bf16[48,1536]{1,0:T(8,128)(2,1)S(1)} %get-tuple-element.88), channel_id=1, source_target_pairs={{0,2},{1,3},{2,0},{3,1},{4,6},{5,7},{6,4},{7,5},{8,10},{9,11},{10,... | collective-permute-start | bytes 442376 | tf_op jit(solution)/shard_map/ppermute | solution.py:33
  138.3 0.9 collective-permute-start.26
  139.2 2.0 %collective-permute-done.25 = bf16[48,1536]{1,0:T(8,128)(2,1)S(1)} collective-permute-done((bf16[48,1536]{1,0:T(8,128)(2,1)S(1)}, bf16[48,1536]{1,0:T(8,128)(2,1)S(1)}, u32[]{:S(2)}, u32[]{:S(2)}) %collective-permute-start.25) | collective-permute-done | bytes 147488 | tf_op jit(solution)/shard_map/ppermute | solution.py:33
  141.2 1.3 collective-permute-done.27
  142.5 0.9 collective-permute-done.26
  143.4 0.1 fusion.15
  143.5 2.0 %collective-permute-start.28 = (bf16[48,768]{1,0:T(8,128)(2,1)S(1)}, bf16[48,768]{1,0:T(8,128)(2,1)S(1)}, u32[]{:S(2)}, u32[]{:S(2)}) collective-permute-start(bf16[48,768]{1,0:T(8,128)(2,1)S(1)} %get-tuple-element.93), channel_id=1, source_target_pairs={{0,16},{1,17},{2,18},{3,19},{4,20},{5,21},{6,22},{7,23},{8,24},{9,... | collective-permute-start | bytes 221192 | tf_op jit(solution)/shard_map/ppermute | solution.py:33
  145.5 0.9 collective-permute-done.28
  146.4 0.7 maximum_select_fusion.1
  (48 shorter events, 0.3 us)
Async XLA Ops:
  7.2 4.1 %copy-start.11 = (bf16[96,768]{1,0:T(8,128)(2,1)S(1)}, bf16[96,768]{1,0:T(8,128)(2,1)}, u32[]{:S(2)}) copy-start(bf16[96,768]{1,0:T(8,128)(2,1)} %param.6) | copy-start | bytes 442372
  7.2 75.1 %all-gather.3.cloned.1.call-start = ((), (), s32[]{:S(2)}) async-start(), calls=%async_computation | async-start | bytes 5308416 | tf_op jit(solution)/shard_map/all_gather | solution.py:318
  9.6 16.4 %copy-start.8 = (bf16[192,1536]{1,0:T(8,128)(2,1)S(1)}, bf16[192,1536]{1,0:T(8,128)(2,1)}, u32[]{:S(2)}) copy-start(bf16[192,1536]{1,0:T(8,128)(2,1)} %param.7) | copy-start | bytes 1769476
  9.6 112.9 %all-gather.5.cloned.1.call-start = ((), (), s32[]{:S(2)}) async-start(), calls=%async_computation.1 | async-start | bytes 2506752 | tf_op jit(solution)/shard_map/all_gather | solution.py:336
  9.6 10.2 %collective-permute-start.4 = (bf16[768,1536]{1,0:T(8,128)(2,1)}, bf16[768,1536]{1,0:T(8,128)(2,1)S(1)}, u32[]{:S(2)}, u32[]{:S(2)}) collective-permute-start(bf16[768,1536]{1,0:T(8,128)(2,1)} %w_own.1), channel_id=1, source_target_pairs={{0,16},{1,17},{2,18},{3,19},{4,20},{5,21},{6,22},{7,23},{8,24},{9,... | collective-permute-start | bytes 7077896 | tf_op jit(solution)/shard_map/ppermute | solution.py:33
  11.1 8.7 %collective-permute-start.3 = (bf16[1536,768]{1,0:T(8,128)(2,1)}, bf16[1536,768]{1,0:T(8,128)(2,1)}, u32[]{:S(2)}, u32[]{:S(2)}) collective-permute-start(bf16[1536,768]{1,0:T(8,128)(2,1)} %refs_8_.3), channel_id=1, source_target_pairs={{0,16},{1,17},{2,18},{3,19},{4,20},{5,21},{6,22},{7,23},{8,24},{9,... | collective-permute-start | bytes 7077896 | tf_op jit(solution)/shard_map/ppermute | solution.py:33
  11.2 5.6 %collective-permute-start.1 = (bf16[96,768]{1,0:T(8,128)(2,1)S(1)}, bf16[96,768]{1,0:T(8,128)(2,1)S(1)}, u32[]{:S(2)}, u32[]{:S(2)}) collective-permute-start(bf16[96,768]{1,0:T(8,128)(2,1)S(1)} %copy-done.11), channel_id=1, source_target_pairs={{0,4},{1,5},{2,6},{3,7},{4,8},{5,9},{6,10},{7,11},{8,12},{9,13},{1... | collective-permute-start | bytes 442376 | tf_op jit(solution)/shard_map/ppermute | solution.py:33
  12.6 4.3 %collective-permute-start = (bf16[96,768]{1,0:T(8,128)(2,1)S(1)}, bf16[96,768]{1,0:T(8,128)(2,1)S(1)}, u32[]{:S(2)}, u32[]{:S(2)}) collective-permute-start(bf16[96,768]{1,0:T(8,128)(2,1)S(1)} %copy-done.11), channel_id=1, source_target_pairs={{0,12},{1,13},{2,14},{3,15},{4,0},{5,1},{6,2},{7,3},{8,4},{9,5},{1... | collective-permute-start | bytes 442376 | tf_op jit(solution)/shard_map/ppermute | solution.py:33
  14.1 5.8 %collective-permute-start.2 = (bf16[96,768]{1,0:T(8,128)(2,1)S(1)}, bf16[96,768]{1,0:T(8,128)(2,1)S(1)}, u32[]{:S(2)}, u32[]{:S(2)}) collective-permute-start(bf16[96,768]{1,0:T(8,128)(2,1)S(1)} %copy-done.11), channel_id=1, source_target_pairs={{0,8},{1,9},{2,10},{3,11},{4,12},{5,13},{6,14},{7,15},{8,0},{9,1},... | collective-permute-start | bytes 442376 | tf_op jit(solution)/shard_map/ppermute | solution.py:33
  15.8 39.4 %copy-start.4 = (s32[4]{0:T(128)}, s32[4]{0:T(128)S(1)}, u32[]{:S(2)}) copy-start(s32[4]{0:T(128)S(1)} %pad_add_fusion.where) | copy-start | bytes 52
  19.9 1.4 copy-start.7
  21.3 33.9 %copy-start = (bf16[4,96,768]{2,1,0:T(8,128)(2,1)}, bf16[4,96,768]{2,1,0:T(8,128)(2,1)S(1)}, u32[]{:S(2)}) copy-start(bf16[4,96,768]{2,1,0:T(8,128)(2,1)S(1)} %pad_maximum_fusion.refs_0_.g0) | copy-start | bytes 1769476
  21.3 17.4 %collective-permute-start.8 = (bf16[4,96,768]{2,1,0:T(8,128)(2,1)S(1)}, bf16[4,96,768]{2,1,0:T(8,128)(2,1)S(1)}, u32[]{:S(2)}, u32[]{:S(2)}) collective-permute-start(bf16[4,96,768]{2,1,0:T(8,128)(2,1)S(1)} %pad_maximum_fusion.refs_0_.g0), channel_id=1, source_target_pairs={{0,1},{1,2},{2,3},{3,0},{4,5},{5,6},{6,7},{7,4},{8,9},{9,10},{10,1... | collective-permute-start | bytes 1769480 | tf_op jit(solution)/shard_map/ppermute | solution.py:33
  22.3 19.2 %collective-permute-start.7 = (bf16[4,96,768]{2,1,0:T(8,128)(2,1)S(1)}, bf16[4,96,768]{2,1,0:T(8,128)(2,1)S(1)}, u32[]{:S(2)}, u32[]{:S(2)}) collective-permute-start(bf16[4,96,768]{2,1,0:T(8,128)(2,1)S(1)} %pad_maximum_fusion.refs_0_.g0), channel_id=1, source_target_pairs={{0,2},{1,3},{2,0},{3,1},{4,6},{5,7},{6,4},{7,5},{8,10},{9,11},{10,... | collective-permute-start | bytes 1769480 | tf_op jit(solution)/shard_map/ppermute | solution.py:33
  25.1 13.6 %collective-permute-start.5 = (bf16[4,96,768]{2,1,0:T(8,128)(2,1)S(1)}, bf16[4,96,768]{2,1,0:T(8,128)(2,1)S(1)}, u32[]{:S(2)}, u32[]{:S(2)}) collective-permute-start(bf16[4,96,768]{2,1,0:T(8,128)(2,1)S(1)} %pad_maximum_fusion.refs_0_.g0), channel_id=1, source_target_pairs={{0,3},{1,0},{2,1},{3,2},{4,7},{5,4},{6,5},{7,6},{8,11},{9,8},{10,9... | collective-permute-start | bytes 1769480 | tf_op jit(solution)/shard_map/ppermute | solution.py:33
  26.0 4.4 %collective-permute-start.6 = (bf16[2,48,1536]{2,1,0:T(8,128)(2,1)S(1)}, bf16[2,48,1536]{2,1,0:T(8,128)(2,1)S(1)}, u32[]{:S(2)}, u32[]{:S(2)}) collective-permute-start(bf16[2,48,1536]{2,1,0:T(8,128)(2,1)S(1)} %get-tuple-element.91), channel_id=1, source_target_pairs={{0,16},{1,17},{2,18},{3,19},{4,20},{5,21},{6,22},{7,23},{8,24},{9,... | collective-permute-start | bytes 884744 | tf_op jit(solution)/shard_map/ppermute | solution.py:33
  29.1 12.9 %collective-permute-start.9 = (bf16[4,96,768]{2,1,0:T(8,128)(2,1)S(1)}, bf16[4,96,768]{2,1,0:T(8,128)(2,1)S(1)}, u32[]{:S(2)}, u32[]{:S(2)}) collective-permute-start(bf16[4,96,768]{2,1,0:T(8,128)(2,1)S(1)} %pad_maximum_fusion.refs_0_.g0), channel_id=1, source_target_pairs={{0,16},{1,17},{2,18},{3,19},{4,20},{5,21},{6,22},{7,23},{8,24},{9,... | collective-permute-start | bytes 1769480 | tf_op jit(solution)/shard_map/ppermute | solution.py:33
  38.7 16.5 %copy-start.3 = (bf16[4,96,768]{2,1,0:T(8,128)(2,1)}, bf16[4,96,768]{2,1,0:T(8,128)(2,1)S(1)}, u32[]{:S(2)}) copy-start(bf16[4,96,768]{2,1,0:T(8,128)(2,1)S(1)} %collective-permute-done.5.refs_1_.g1) | copy-start | bytes 1769476
  38.7 16.5 %copy-start.1 = (bf16[4,96,768]{2,1,0:T(8,128)(2,1)}, bf16[4,96,768]{2,1,0:T(8,128)(2,1)S(1)}, u32[]{:S(2)}) copy-start(bf16[4,96,768]{2,1,0:T(8,128)(2,1)S(1)} %collective-permute-done.8.refs_3_.g3) | copy-start | bytes 1769476
  38.7 4.6 %collective-permute-start.12 = (bf16[4,96,768]{2,1,0:T(8,128)(2,1)S(1)}, bf16[4,96,768]{2,1,0:T(8,128)(2,1)S(1)}, u32[]{:S(2)}, u32[]{:S(2)}) collective-permute-start(bf16[4,96,768]{2,1,0:T(8,128)(2,1)S(1)} %collective-permute-done.8.refs_3_.g3), channel_id=1, source_target_pairs={{0,16},{1,17},{2,18},{3,19},{4,20},{5,21},{6,22},{7,23},{8,24},{9,... | collective-permute-start | bytes 1769480 | tf_op jit(solution)/shard_map/ppermute | solution.py:33
  41.5 13.7 %copy-start.2 = (bf16[4,96,768]{2,1,0:T(8,128)(2,1)}, bf16[4,96,768]{2,1,0:T(8,128)(2,1)S(1)}, u32[]{:S(2)}) copy-start(bf16[4,96,768]{2,1,0:T(8,128)(2,1)S(1)} %collective-permute-done.7.refs_2_.g2) | copy-start | bytes 1769476
  41.5 2.7 %collective-permute-start.11 = (bf16[4,96,768]{2,1,0:T(8,128)(2,1)S(1)}, bf16[4,96,768]{2,1,0:T(8,128)(2,1)S(1)}, u32[]{:S(2)}, u32[]{:S(2)}) collective-permute-start(bf16[4,96,768]{2,1,0:T(8,128)(2,1)S(1)} %collective-permute-done.7.refs_2_.g2), channel_id=1, source_target_pairs={{0,16},{1,17},{2,18},{3,19},{4,20},{5,21},{6,22},{7,23},{8,24},{9,... | collective-permute-start | bytes 1769480 | tf_op jit(solution)/shard_map/ppermute | solution.py:33
  41.8 3.4 %collective-permute-start.10 = (bf16[4,96,768]{2,1,0:T(8,128)(2,1)S(1)}, bf16[4,96,768]{2,1,0:T(8,128)(2,1)S(1)}, u32[]{:S(2)}, u32[]{:S(2)}) collective-permute-start(bf16[4,96,768]{2,1,0:T(8,128)(2,1)S(1)} %collective-permute-done.5.refs_1_.g1), channel_id=1, source_target_pairs={{0,16},{1,17},{2,18},{3,19},{4,20},{5,21},{6,22},{7,23},{8,24},{9,... | collective-permute-start | bytes 1769480 | tf_op jit(solution)/shard_map/ppermute | solution.py:33
  51.4 17.1 %collective-permute-start.13 = (bf16[192,1536]{1,0:T(8,128)(2,1)S(1)}, bf16[192,1536]{1,0:T(8,128)(2,1)S(1)}, u32[]{:S(2)}, u32[]{:S(2)}) collective-permute-start(bf16[192,1536]{1,0:T(8,128)(2,1)S(1)} %get-tuple-element.50), channel_id=1, source_target_pairs={{0,32},{1,33},{2,34},{3,35},{4,36},{5,37},{6,38},{7,39},{8,40},{9,... | collective-permute-start | bytes 1769480 | tf_op jit(solution)/shard_map/ppermute | solution.py:33
  53.2 14.3 %collective-permute-start.14 = (bf16[192,1536]{1,0:T(8,128)(2,1)S(1)}, bf16[192,1536]{1,0:T(8,128)(2,1)S(1)}, u32[]{:S(2)}, u32[]{:S(2)}) collective-permute-start(bf16[192,1536]{1,0:T(8,128)(2,1)S(1)} %get-tuple-element.51), channel_id=1, source_target_pairs={{0,96},{1,97},{2,98},{3,99},{4,100},{5,101},{6,102},{7,103},{8,104... | collective-permute-start | bytes 1769480 | tf_op jit(solution)/shard_map/ppermute | solution.py:33
  67.6 1.0 copy-start.9
  68.5 1.6 %copy-start.10 = (bf16[192,1536]{1,0:T(8,128)(2,1)}, bf16[192,1536]{1,0:T(8,128)(2,1)S(1)}, u32[]{:S(2)}) copy-start(bf16[192,1536]{1,0:T(8,128)(2,1)S(1)} %collective-permute-done.13) | copy-start | bytes 1769476
  70.1 9.3 %slice-start = ((bf16[192,1536]{1,0:T(8,128)(2,1)}), bf16[96,1536]{1,0:T(8,128)(2,1)S(1)}, s32[]{:S(2)}) async-start(bf16[192,1536]{1,0:T(8,128)(2,1)} %copy-done.9), calls=%async_computation.2 | async-start | bytes 589824 | tf_op jit(solution)/shard_map/slice | solution.py:342
  70.1 9.3 %slice-start.1 = ((bf16[192,1536]{1,0:T(8,128)(2,1)}), bf16[96,1536]{1,0:T(8,128)(2,1)S(1)}, s32[]{:S(2)}) async-start(bf16[192,1536]{1,0:T(8,128)(2,1)} %copy-done.10), calls=%async_computation.3 | async-start | bytes 589824 | tf_op jit(solution)/shard_map/slice | solution.py:342
  70.1 9.3 %collective-permute-start.15 = (bf16[96,1536]{1,0:T(8,128)(2,1)S(1)}, bf16[96,1536]{1,0:T(8,128)(2,1)S(1)}, u32[]{:S(2)}, u32[]{:S(2)}) collective-permute-start(bf16[96,1536]{1,0:T(8,128)(2,1)S(1)} %get-tuple-element.85), channel_id=1, source_target_pairs={{0,32},{1,33},{2,34},{3,35},{4,36},{5,37},{6,38},{7,39},{8,40},{9,... | collective-permute-start | bytes 884744 | tf_op jit(solution)/shard_map/ppermute | solution.py:33
  71.3 8.0 %collective-permute-start.16 = (bf16[96,1536]{1,0:T(8,128)(2,1)S(1)}, bf16[96,1536]{1,0:T(8,128)(2,1)S(1)}, u32[]{:S(2)}, u32[]{:S(2)}) collective-permute-start(bf16[96,1536]{1,0:T(8,128)(2,1)S(1)} %get-tuple-element.86), channel_id=1, source_target_pairs={{0,96},{1,97},{2,98},{3,99},{4,100},{5,101},{6,102},{7,103},{8,104... | collective-permute-start | bytes 884744 | tf_op jit(solution)/shard_map/ppermute | solution.py:33
  73.4 6.2 %copy-start.6 = (f32[4,48,1536]{2,1,0:T(8,128)S(1)}, f32[4,48,1536]{2,1,0:T(8,128)}, u32[]{:S(2)}) copy-start(f32[4,48,1536]{2,1,0:T(8,128)} %fusion.10) | copy-start | bytes 3538948
  79.8 13.2 %collective-permute-start.18 = (bf16[4,48,1536]{2,1,0:T(8,128)(2,1)S(1)}, bf16[4,48,1536]{2,1,0:T(8,128)(2,1)S(1)}, u32[]{:S(2)}, u32[]{:S(2)}) collective-permute-start(bf16[4,48,1536]{2,1,0:T(8,128)(2,1)S(1)} %multiply_convert_fusion.h0), channel_id=1, source_target_pairs={{0,96},{1,97},{2,98},{3,99},{4,100},{5,101},{6,102},{7,103},{8,104... | collective-permute-start | bytes 1769480 | tf_op jit(solution)/shard_map/ppermute | solution.py:33
  82.3 13.7 %collective-permute-start.17 = (bf16[4,48,1536]{2,1,0:T(8,128)(2,1)S(1)}, bf16[4,48,1536]{2,1,0:T(8,128)(2,1)S(1)}, u32[]{:S(2)}, u32[]{:S(2)}) collective-permute-start(bf16[4,48,1536]{2,1,0:T(8,128)(2,1)S(1)} %multiply_convert_fusion.h0), channel_id=1, source_target_pairs={{0,32},{1,33},{2,34},{3,35},{4,36},{5,37},{6,38},{7,39},{8,40},{9,... | collective-permute-start | bytes 1769480 | tf_op jit(solution)/shard_map/ppermute | solution.py:33
  92.3 10.7 %copy-start.5 = (s32[4]{0:T(128)S(1)}, s32[4]{0:T(128)}, u32[]{:S(2)}) copy-start(s32[4]{0:T(128)} %copy-done.4) | copy-start | bytes 52
  96.1 6.9 %collective-permute-start.19 = (bf16[2,48,1536]{2,1,0:T(8,128)(2,1)S(1)}, bf16[2,48,1536]{2,1,0:T(8,128)(2,1)S(1)}, u32[]{:S(2)}, u32[]{:S(2)}) collective-permute-start(bf16[2,48,1536]{2,1,0:T(8,128)(2,1)S(1)} %slice.51), channel_id=1, source_target_pairs={{0,32},{1,33},{2,34},{3,35},{4,36},{5,37},{6,38},{7,39},{8,40},{9,... | collective-permute-start | bytes 884744 | tf_op jit(solution)/shard_map/ppermute | solution.py:33
  96.1 6.8 %collective-permute-start.20 = (bf16[2,48,1536]{2,1,0:T(8,128)(2,1)S(1)}, bf16[2,48,1536]{2,1,0:T(8,128)(2,1)S(1)}, u32[]{:S(2)}, u32[]{:S(2)}) collective-permute-start(bf16[2,48,1536]{2,1,0:T(8,128)(2,1)S(1)} %slice.52), channel_id=1, source_target_pairs={{0,96},{1,97},{2,98},{3,99},{4,100},{5,101},{6,102},{7,103},{8,104... | collective-permute-start | bytes 884744 | tf_op jit(solution)/shard_map/ppermute | solution.py:33
  113.4 9.1 %collective-permute-start.24 = (bf16[4,4,48,1536]{3,2,1,0:T(8,128)(2,1)}, bf16[4,4,48,1536]{3,2,1,0:T(8,128)(2,1)}, u32[]{:S(2)}, u32[]{:S(2)}) collective-permute-start(bf16[4,4,48,1536]{3,2,1,0:T(8,128)(2,1)} %get-tuple-element.77), channel_id=1, source_target_pairs={{0,16},{1,17},{2,18},{3,19},{4,20},{5,21},{6,22},{7,23},{8,24},{9,... | collective-permute-start | bytes 7077896 | tf_op jit(solution)/shard_map/ppermute | solution.py:33
  117.9 13.7 %collective-permute-start.21 = (bf16[4,48,1536]{2,1,0:T(8,128)(2,1)}, bf16[4,48,1536]{2,1,0:T(8,128)(2,1)S(1)}, u32[]{:S(2)}, u32[]{:S(2)}) collective-permute-start(bf16[4,48,1536]{2,1,0:T(8,128)(2,1)} %get-tuple-element.73), channel_id=1, source_target_pairs={{0,4},{1,5},{2,6},{3,7},{4,8},{5,9},{6,10},{7,11},{8,12},{9,13},{1... | collective-permute-start | bytes 1769480 | tf_op jit(solution)/shard_map/ppermute | solution.py:33
  119.8 11.7 %collective-permute-start.22 = (bf16[4,48,1536]{2,1,0:T(8,128)(2,1)}, bf16[4,48,1536]{2,1,0:T(8,128)(2,1)S(1)}, u32[]{:S(2)}, u32[]{:S(2)}) collective-permute-start(bf16[4,48,1536]{2,1,0:T(8,128)(2,1)} %get-tuple-element.74), channel_id=1, source_target_pairs={{0,12},{1,13},{2,14},{3,15},{4,0},{5,1},{6,2},{7,3},{8,4},{9,5},{1... | collective-permute-start | bytes 1769480 | tf_op jit(solution)/shard_map/ppermute | solution.py:33
  120.5 14.8 %collective-permute-start.23 = (bf16[4,48,1536]{2,1,0:T(8,128)(2,1)S(1)}, bf16[4,48,1536]{2,1,0:T(8,128)(2,1)S(1)}, u32[]{:S(2)}, u32[]{:S(2)}) collective-permute-start(bf16[4,48,1536]{2,1,0:T(8,128)(2,1)S(1)} %get-tuple-element.75), channel_id=1, source_target_pairs={{0,8},{1,9},{2,10},{3,11},{4,12},{5,13},{6,14},{7,15},{8,0},{9,1},... | collective-permute-start | bytes 1769480 | tf_op jit(solution)/shard_map/ppermute | solution.py:33
  135.6 5.6 %collective-permute-start.25 = (bf16[48,1536]{1,0:T(8,128)(2,1)S(1)}, bf16[48,1536]{1,0:T(8,128)(2,1)S(1)}, u32[]{:S(2)}, u32[]{:S(2)}) collective-permute-start(bf16[48,1536]{1,0:T(8,128)(2,1)S(1)} %get-tuple-element.87), channel_id=1, source_target_pairs={{0,1},{1,2},{2,3},{3,0},{4,5},{5,6},{6,7},{7,4},{8,9},{9,10},{10,1... | collective-permute-start | bytes 442376 | tf_op jit(solution)/shard_map/ppermute | solution.py:33
  136.0 6.5 %collective-permute-start.27 = (bf16[48,1536]{1,0:T(8,128)(2,1)S(1)}, bf16[48,1536]{1,0:T(8,128)(2,1)S(1)}, u32[]{:S(2)}, u32[]{:S(2)}) collective-permute-start(bf16[48,1536]{1,0:T(8,128)(2,1)S(1)} %get-tuple-element.88), channel_id=1, source_target_pairs={{0,2},{1,3},{2,0},{3,1},{4,6},{5,7},{6,4},{7,5},{8,10},{9,11},{10,... | collective-permute-start | bytes 442376 | tf_op jit(solution)/shard_map/ppermute | solution.py:33
  138.3 5.0 %collective-permute-start.26 = (bf16[48,1536]{1,0:T(8,128)(2,1)S(1)}, bf16[48,1536]{1,0:T(8,128)(2,1)S(1)}, u32[]{:S(2)}, u32[]{:S(2)}) collective-permute-start(bf16[48,1536]{1,0:T(8,128)(2,1)S(1)} %get-tuple-element.89), channel_id=1, source_target_pairs={{0,3},{1,0},{2,1},{3,2},{4,7},{5,4},{6,5},{7,6},{8,11},{9,8},{10,9... | collective-permute-start | bytes 442376 | tf_op jit(solution)/shard_map/ppermute | solution.py:33
  143.5 3.0 %collective-permute-start.28 = (bf16[48,768]{1,0:T(8,128)(2,1)S(1)}, bf16[48,768]{1,0:T(8,128)(2,1)S(1)}, u32[]{:S(2)}, u32[]{:S(2)}) collective-permute-start(bf16[48,768]{1,0:T(8,128)(2,1)S(1)} %get-tuple-element.93), channel_id=1, source_target_pairs={{0,16},{1,17},{2,18},{3,19},{4,20},{5,21},{6,22},{7,23},{8,24},{9,... | collective-permute-start | bytes 221192 | tf_op jit(solution)/shard_map/ppermute | solution.py:33
Sparse Core Ops, SparseCore 0:
  9.7 38.1 all-gather.2
  73.5 44.5 all-gather.4

commit v4 on v3

--- a/solution.py
+++ b/solution.py
@@ -13,7 +13,8 @@
 N = 4
 K = 48
 VMEM = 56 * 2**20
-SMALL = 48 * 2**20
+SMALL = 46 * 2**20
+MEDIUM = 52 * 2**20
 LIGHT = pl.CostEstimate(flops=1024, bytes_accessed=1024, transcendentals=0)
 HEAVY = pl.CostEstimate(flops=8 * 10**9, bytes_accessed=2**24, transcendentals=0)
 AXES = ("row", "col")
@@ -217,7 +218,7 @@
                 pltpu.SemaphoreType.DMA((3, N)),
             ],
         ),
-        compiler_params=pltpu.CompilerParams(vmem_limit_bytes=SMALL),
+        compiler_params=pltpu.CompilerParams(vmem_limit_bytes=MEDIUM),
         cost_estimate=LIGHT,
         name="input_grad",
     )(where, *pieces, w_own, w_other)

time: 154 us -> 151 us (0.981)
  waiting for transfers between devices: 43.7 us -> 39.4 us
  local copies, waits for them, and re-layouts: 1.58 us -> 3.62 us
  Pallas kernels: 42.9 us -> 40.9 us
    ppermute x29, waiting for transfers between devices: 43.6 us -> 39.4 us  [permute(): return lax.ppermute(array, AXES, pairs)]
    squeeze x1, local copies, waits for them, and re-layouts: 0.04 us -> 2.05 us  [mine_and_other(): mine = lax.dynamic_index_in_dim(array, core, axis, keepdims=False)]
  transfers between devices with their start and end apart: 31 -> 31, of which waited for: 18 -> 18; matrix products, arithmetic and copies ran while one was open for 3% -> 4% of each run, Pallas kernels for 28% -> 27%
where the time goes in v4:
time: 151 us; the launch traced here: 150 us
  starting transfers between devices  45.1 us (30%)
  Pallas kernels  40.9 us (27%)
  waiting for transfers between devices  39.4 us (26%)
  between operations  14.3 us (9%)
  other arithmetic  7.14 us (5%)
  local copies, waits for them, and re-layouts  3.62 us (2%)
    ppermute x29, starting transfers between devices, permute(): return lax.ppermute(array, AXES, pairs)  45 us
    ppermute x29, waiting for transfers between devices, permute(): return lax.ppermute(array, AXES, pairs)  39.4 us
    pallas_call x2, Pallas kernels, act_grad_parts(): pl.pallas_call(functools.partial(act_grad_kernel, part), out_shape=[jax.S...  12.3 us
    pallas_call x1, Pallas kernels, weight_out_grad_of(): pl.pallas_call(weight_out_grad_kernel, out_shape=jax.ShapeDtypeStruct((hi...  10 us
    pallas_call x1, Pallas kernels, input_grad_parts(): pl.pallas_call(input_grad_kernel, out_shape=[jax.ShapeDtypeStruct((N, n,...  9.45 us
    pallas_call x1, Pallas kernels, weight_in_grad_of(): pl.pallas_call(weight_in_grad_kernel, out_shape=jax.ShapeDtypeStruct((wid...  9.15 us
    add x1, other arithmetic, gelu_parts(): 0.5 * (1.0 + tanh_value)  3.05 us
  transfers between devices with their start and end apart: 31, of which 18 were waited for; matrix products, arithmetic and copies ran while one was open for 4% of the time, Pallas kernels for 27%

profile of v4, /device:TPU:1, one launch (start us, length us, event | category | flops | bytes accessed | tf_op | source)
XLA Modules:
  0.0 150.5 jit_solution(4627363154104110460)
XLA Ops:
  7.2 0.0 all-gather.3.cloned.1.call-start
  7.2 2.4 %fusion.1 = bf16[192,1536]{1,0:T(8,128)(2,1)} fusion(bf16[192,1536]{1,0:T(8,128)(2,1)} %param.7), kind=kLoop, calls=%fused_computation.13 | loop fusion | flops 2949120 | bytes 1179648 | tf_op jit(solution)/shard_map/convert_element_type | solution.py:318
  9.6 0.0 all-gather.5.cloned.1.call-start
  9.7 1.5 collective-permute-start.4
  11.2 0.1 collective-permute-start.3
  11.3 1.4 collective-permute-start.1
  12.6 1.4 collective-permute-start
  14.1 1.6 %collective-permute-start.2 = (bf16[96,768]{1,0:T(8,128)(2,1)S(1)}, bf16[96,768]{1,0:T(8,128)(2,1)S(1)}, u32[]{:S(2)}, u32[]{:S(2)}) collective-permute-start(bf16[96,768]{1,0:T(8,128)(2,1)S(1)} %copy-done.11), channel_id=1, source_target_pairs={{0,8},{1,9},{2,10},{3,11},{4,12},{5,13},{6,14},{7,15},{8,0},{9,1},... | collective-permute-start | bytes 442376 | tf_op jit(solution)/shard_map/ppermute | solution.py:34
  15.7 0.1 pad_add_fusion.where
  15.8 1.1 collective-permute-done.1
  16.9 2.9 %collective-permute-done.2 = bf16[96,768]{1,0:T(8,128)(2,1)S(1)} collective-permute-done((bf16[96,768]{1,0:T(8,128)(2,1)S(1)}, bf16[96,768]{1,0:T(8,128)(2,1)S(1)}, u32[]{:S(2)}, u32[]{:S(2)}) %collective-permute-start.2) | collective-permute-done | bytes 147488 | tf_op jit(solution)/shard_map/ppermute | solution.py:34
  19.9 1.4 copy-done.6
  21.3 0.1 pad_maximum_fusion.refs_0_.g0
  21.4 1.0 collective-permute-start.8
  22.4 2.7 %collective-permute-start.7 = (bf16[4,96,768]{2,1,0:T(8,128)(2,1)S(1)}, bf16[4,96,768]{2,1,0:T(8,128)(2,1)}, u32[]{:S(2)}, u32[]{:S(2)}) collective-permute-start(bf16[4,96,768]{2,1,0:T(8,128)(2,1)S(1)} %pad_maximum_fusion.refs_0_.g0), channel_id=1, source_target_pairs={{0,2},{1,3},{2,0},{3,1},{4,6},{5,7},{6,4},{7,5},{8,10},{9,11},{10,... | collective-permute-start | bytes 1769480 | tf_op jit(solution)/shard_map/ppermute | solution.py:34
  25.1 0.9 collective-permute-start.5
  26.0 2.0 %dynamic-slice_bitcast_fusion.1 = (bf16[2,48,1536]{2,1,0:T(8,128)(2,1)}, bf16[2,48,1536]{2,1,0:T(8,128)(2,1)}) fusion(bf16[2,2,48,1536]{3,2,1,0:T(8,128)(2,1)} %bitcast.38, s32[]{:T(128)S(6)} %select_n.47, s32[]{:T(128)S(6)} %select_n.48), kind=kLoop, calls=%fused_computation.37 | loop fusion | bytes 1179656 | tf_op jit(solution)/shard_map/jit(dynamic_index_in_dim)/squeeze | solution.py:306
  28.0 3.1 %collective-permute-start.6 = (bf16[2,48,1536]{2,1,0:T(8,128)(2,1)}, bf16[2,48,1536]{2,1,0:T(8,128)(2,1)}, u32[]{:S(2)}, u32[]{:S(2)}) collective-permute-start(bf16[2,48,1536]{2,1,0:T(8,128)(2,1)} %get-tuple-element.91), channel_id=1, source_target_pairs={{0,16},{1,17},{2,18},{3,19},{4,20},{5,21},{6,22},{7,23},{8,24},{9,... | collective-permute-start | bytes 884744 | tf_op jit(solution)/shard_map/ppermute | solution.py:34
  31.1 1.9 %collective-permute-done.6 = bf16[2,48,1536]{2,1,0:T(8,128)(2,1)} collective-permute-done((bf16[2,48,1536]{2,1,0:T(8,128)(2,1)}, bf16[2,48,1536]{2,1,0:T(8,128)(2,1)}, u32[]{:S(2)}, u32[]{:S(2)}) %collective-permute-start.6) | collective-permute-done | bytes 294944 | tf_op jit(solution)/shard_map/ppermute | solution.py:34
  33.0 3.0 %fusion.10 = f32[4,48,1536]{2,1,0:T(8,128)} fusion(bf16[2,48,1536]{2,1,0:T(8,128)(2,1)} %collective-permute-done.6, bf16[2,48,1536]{2,1,0:T(8,128)(2,1)} %get-tuple-element.90, pred[]{:T(512)S(6)} %eq.7), kind=kLoop, calls=%fused_computation.22 | loop fusion | flops 6193152 | bytes 1769473 | tf_op jit(solution)/shard_map/add | solution.py:57
  36.1 2.6 %collective-permute-done.5.refs_1_.g1 = bf16[4,96,768]{2,1,0:T(8,128)(2,1)} collective-permute-done((bf16[4,96,768]{2,1,0:T(8,128)(2,1)S(1)}, bf16[4,96,768]{2,1,0:T(8,128)(2,1)}, u32[]{:S(2)}, u32[]{:S(2)}) %collective-permute-start.5) | collective-permute-done | bytes 589856 | tf_op jit(solution)/shard_map/ppermute | solution.py:34
  38.7 2.8 %collective-permute-start.12 = (bf16[4,96,768]{2,1,0:T(8,128)(2,1)S(1)}, bf16[4,96,768]{2,1,0:T(8,128)(2,1)S(1)}, u32[]{:S(2)}, u32[]{:S(2)}) collective-permute-start(bf16[4,96,768]{2,1,0:T(8,128)(2,1)S(1)} %collective-permute-done.8.refs_3_.g3), channel_id=1, source_target_pairs={{0,16},{1,17},{2,18},{3,19},{4,20},{5,21},{6,22},{7,23},{8,24},{9,... | collective-permute-start | bytes 1769480 | tf_op jit(solution)/shard_map/ppermute | solution.py:34
  41.6 0.4 collective-permute-start.11
  42.0 0.1 collective-permute-start.10
  42.1 1.3 collective-permute-done.12.refs_7_
  43.4 1.1 collective-permute-done.11.refs_6_
  44.4 1.1 collective-permute-done.10.refs_5_
  45.5 6.1 %act_grad.2 = (bf16[192,1536]{1,0:T(8,128)(2,1)S(1)}, bf16[192,1536]{1,0:T(8,128)(2,1)S(1)}) custom-call(s32[4]{0:T(128)S(1)} %pad_add_fusion.where, bf16[4,96,768]{2,1,0:T(8,128)(2,1)S(1)} %pad_maximum_fusion.refs_0_.g0, bf16[4,96,768]{2,1,0:T(8,128)(2,1)} %collective-permute-done.5.refs_1_.g1, bf16[4,96,768]{2,1,0:T(8,128)(2,1)} %collective-permute-done.7.refs_2_.g2, ...), custom_call_target="tpu_custom_call" | custom-call | flops 1024 | bytes 1024 | tf_op jit(solution)/shard_map/act_grad/pallas_call | solution.py:134
  51.6 2.2 %collective-permute-start.13 = (bf16[192,1536]{1,0:T(8,128)(2,1)S(1)}, bf16[192,1536]{1,0:T(8,128)(2,1)S(1)}, u32[]{:S(2)}, u32[]{:S(2)}) collective-permute-start(bf16[192,1536]{1,0:T(8,128)(2,1)S(1)} %get-tuple-element.50), channel_id=1, source_target_pairs={{0,32},{1,33},{2,34},{3,35},{4,36},{5,37},{6,38},{7,39},{8,40},{9,... | collective-permute-start | bytes 1769480 | tf_op jit(solution)/shard_map/ppermute | solution.py:34
  53.8 1.6 %collective-permute-start.14 = (bf16[192,1536]{1,0:T(8,128)(2,1)S(1)}, bf16[192,1536]{1,0:T(8,128)(2,1)S(1)}, u32[]{:S(2)}, u32[]{:S(2)}) collective-permute-start(bf16[192,1536]{1,0:T(8,128)(2,1)S(1)} %get-tuple-element.51), channel_id=1, source_target_pairs={{0,96},{1,97},{2,98},{3,99},{4,100},{5,101},{6,102},{7,103},{8,104... | collective-permute-start | bytes 1769480 | tf_op jit(solution)/shard_map/ppermute | solution.py:34
  55.4 6.2 %act_grad.3 = (f32[192,1536]{1,0:T(8,128)S(1)}, f32[192,1536]{1,0:T(8,128)S(1)}) custom-call(s32[4]{0:T(128)S(1)} %pad_add_fusion.where, bf16[4,96,768]{2,1,0:T(8,128)(2,1)S(1)} %pad_maximum_fusion.refs_0_.g0, bf16[4,96,768]{2,1,0:T(8,128)(2,1)} %collective-permute-done.5.refs_1_.g1, bf16[4,96,768]{2,1,0:T(8,128)(2,1)} %collective-permute-done.7.refs_2_.g2, ...), custom_call_target="tpu_custom_call" | custom-call | flops 8000000000 | bytes 16777216 | tf_op jit(solution)/shard_map/act_grad/pallas_call | solution.py:134
  61.7 6.7 %collective-permute-done.14 = bf16[192,1536]{1,0:T(8,128)(2,1)S(1)} collective-permute-done((bf16[192,1536]{1,0:T(8,128)(2,1)S(1)}, bf16[192,1536]{1,0:T(8,128)(2,1)S(1)}, u32[]{:S(2)}, u32[]{:S(2)}) %collective-permute-start.14) | collective-permute-done | bytes 589856 | tf_op jit(solution)/shard_map/ppermute | solution.py:34
  68.4 0.1 collective-permute-done.13
  68.5 0.1 add_convert_fusion.1
  68.6 1.4 collective-permute-start.15
  70.1 1.3 collective-permute-start.16
  71.5 5.8 %collective-permute-done.15 = bf16[96,1536]{1,0:T(8,128)(2,1)S(1)} collective-permute-done((bf16[96,1536]{1,0:T(8,128)(2,1)S(1)}, bf16[96,1536]{1,0:T(8,128)(2,1)S(1)}, u32[]{:S(2)}, u32[]{:S(2)}) %collective-permute-start.15) | collective-permute-done | bytes 294944 | tf_op jit(solution)/shard_map/ppermute | solution.py:34
  77.3 0.2 convert_add_fusion.3
  77.5 0.1 multiply_convert_fusion.h0
  77.7 2.5 %collective-permute-start.18 = (bf16[4,48,1536]{2,1,0:T(8,128)(2,1)S(1)}, bf16[4,48,1536]{2,1,0:T(8,128)(2,1)S(1)}, u32[]{:S(2)}, u32[]{:S(2)}) collective-permute-start(bf16[4,48,1536]{2,1,0:T(8,128)(2,1)S(1)} %multiply_convert_fusion.h0), channel_id=1, source_target_pairs={{0,96},{1,97},{2,98},{3,99},{4,100},{5,101},{6,102},{7,103},{8,104... | collective-permute-start | bytes 1769480 | tf_op jit(solution)/shard_map/ppermute | solution.py:34
  80.1 10.0 %weight_out_grad.1 = f32[1536,768]{1,0:T(8,128)} custom-call(s32[4]{0:T(128)} %copy-done.3, bf16[1536,1536]{1,0:T(8,128)(2,1)} %all-gather.3.cloned.1.call-done.act, bf16[4,96,768]{2,1,0:T(8,128)(2,1)} %copy-done, bf16[4,96,768]{2,1,0:T(8,128)(2,1)} %collective-permute-done.5.refs_1_.g1, bf16[4,96,768]{2,1,0:T(8,128)(2,1)} %collective-permute-done.7.refs_2_.g2, ...), custom_call_target="tpu_custom_call" | custom-call | flops 8000000000 | bytes 16777216 | tf_op jit(solution)/shard_map/weight_out_grad/pallas_call | solution.py:247
  90.2 0.3 collective-permute-done.18.h1
  90.5 3.1 %collective-permute-done.17.h3 = bf16[4,48,1536]{2,1,0:T(8,128)(2,1)S(1)} collective-permute-done((bf16[4,48,1536]{2,1,0:T(8,128)(2,1)S(1)}, bf16[4,48,1536]{2,1,0:T(8,128)(2,1)S(1)}, u32[]{:S(2)}, u32[]{:S(2)}) %collective-permute-start.17) | collective-permute-done | bytes 589856 | tf_op jit(solution)/shard_map/ppermute | solution.py:34
  93.6 0.1 collective-permute-start.19
  93.7 2.7 %collective-permute-start.20 = (bf16[2,48,1536]{2,1,0:T(8,128)(2,1)S(1)}, bf16[2,48,1536]{2,1,0:T(8,128)(2,1)S(1)}, u32[]{:S(2)}, u32[]{:S(2)}) collective-permute-start(bf16[2,48,1536]{2,1,0:T(8,128)(2,1)S(1)} %slice.52), channel_id=1, source_target_pairs={{0,96},{1,97},{2,98},{3,99},{4,100},{5,101},{6,102},{7,103},{8,104... | collective-permute-start | bytes 884744 | tf_op jit(solution)/shard_map/ppermute | solution.py:34
  96.4 4.1 %collective-permute-done.19.h2a = bf16[2,48,1536]{2,1,0:T(8,128)(2,1)S(1)} collective-permute-done((bf16[2,48,1536]{2,1,0:T(8,128)(2,1)S(1)}, bf16[2,48,1536]{2,1,0:T(8,128)(2,1)S(1)}, u32[]{:S(2)}, u32[]{:S(2)}) %collective-permute-start.19) | collective-permute-done | bytes 294944 | tf_op jit(solution)/shard_map/ppermute | solution.py:34
  100.5 9.5 %input_grad.1 = (f32[4,48,1536]{2,1,0:T(8,128)}, bf16[4,48,1536]{2,1,0:T(8,128)(2,1)S(1)}, bf16[4,48,1536]{2,1,0:T(8,128)(2,1)S(1)}, bf16[4,48,1536]{2,1,0:T(8,128)(2,1)}, bf16[4,4,48,1536]{3,2,1,0:T(8,128)(2,1)}) custom-call(s32[4]{0:T(128)S(1)} %copy-done.4, bf16[4,48,1536]{2,1,0:T(8,128)(2,1)} %copy-done.7, bf16[4,48,1536]{2,1,0:T(8,128)(2,1)} %copy-done.8, ...), custom_call_target="tpu_custom_call" | custom-call | flops 1024 | bytes 1024 | tf_op jit(solution)/shard_map/input_grad/pallas_call | solution.py:202
  110.0 4.6 %collective-permute-start.24 = (bf16[4,4,48,1536]{3,2,1,0:T(8,128)(2,1)}, bf16[4,4,48,1536]{3,2,1,0:T(8,128)(2,1)}, u32[]{:S(2)}, u32[]{:S(2)}) collective-permute-start(bf16[4,4,48,1536]{3,2,1,0:T(8,128)(2,1)} %get-tuple-element.77), channel_id=1, source_target_pairs={{0,16},{1,17},{2,18},{3,19},{4,20},{5,21},{6,22},{7,23},{8,24},{9,... | collective-permute-start | bytes 7077896 | tf_op jit(solution)/shard_map/ppermute | solution.py:34
  114.6 2.0 %collective-permute-start.21 = (bf16[4,48,1536]{2,1,0:T(8,128)(2,1)S(1)}, bf16[4,48,1536]{2,1,0:T(8,128)(2,1)S(1)}, u32[]{:S(2)}, u32[]{:S(2)}) collective-permute-start(bf16[4,48,1536]{2,1,0:T(8,128)(2,1)S(1)} %get-tuple-element.73), channel_id=1, source_target_pairs={{0,4},{1,5},{2,6},{3,7},{4,8},{5,9},{6,10},{7,11},{8,12},{9,13},{1... | collective-permute-start | bytes 1769480 | tf_op jit(solution)/shard_map/ppermute | solution.py:34
  116.6 0.7 collective-permute-start.22
  117.2 2.0 %collective-permute-start.23 = (bf16[4,48,1536]{2,1,0:T(8,128)(2,1)S(1)}, bf16[4,48,1536]{2,1,0:T(8,128)(2,1)S(1)}, u32[]{:S(2)}, u32[]{:S(2)}) collective-permute-start(bf16[4,48,1536]{2,1,0:T(8,128)(2,1)S(1)} %get-tuple-element.75), channel_id=1, source_target_pairs={{0,8},{1,9},{2,10},{3,11},{4,12},{5,13},{6,14},{7,15},{8,0},{9,1},... | collective-permute-start | bytes 1769480 | tf_op jit(solution)/shard_map/ppermute | solution.py:34
  119.2 9.2 %weight_in_grad.1 = f32[768,1536]{1,0:T(8,128)} custom-call(s32[4]{0:T(128)} %copy-done.3, bf16[16,2,48,768]{3,2,1,0:T(8,128)(2,1)} %bitcast.43, bf16[768,1536]{1,0:T(8,128)(2,1)} %bitcast.44, bf16[768,1536]{1,0:T(8,128)(2,1)} %bitcast.14.hid_other), custom_call_target="tpu_custom_call" | custom-call | flops 8000000000 | bytes 16777216 | tf_op jit(solution)/shard_map/weight_in_grad/pallas_call | solution.py:282
  128.4 3.4 %collective-permute-done.23 = bf16[4,48,1536]{2,1,0:T(8,128)(2,1)S(1)} collective-permute-done((bf16[4,48,1536]{2,1,0:T(8,128)(2,1)S(1)}, bf16[4,48,1536]{2,1,0:T(8,128)(2,1)S(1)}, u32[]{:S(2)}, u32[]{:S(2)}) %collective-permute-start.23) | collective-permute-done | bytes 589856 | tf_op jit(solution)/shard_map/ppermute | solution.py:34
  131.8 0.4 fusion.16
  132.2 1.5 %collective-permute-start.25 = (bf16[48,1536]{1,0:T(8,128)(2,1)S(1)}, bf16[48,1536]{1,0:T(8,128)(2,1)S(1)}, u32[]{:S(2)}, u32[]{:S(2)}) collective-permute-start(bf16[48,1536]{1,0:T(8,128)(2,1)S(1)} %get-tuple-element.87), channel_id=1, source_target_pairs={{0,1},{1,2},{2,3},{3,0},{4,5},{5,6},{6,7},{7,4},{8,9},{9,10},{10,1... | collective-permute-start | bytes 442376 | tf_op jit(solution)/shard_map/ppermute | solution.py:34
  133.7 1.5 collective-permute-start.27
  135.2 1.9 %collective-permute-start.26 = (bf16[48,1536]{1,0:T(8,128)(2,1)S(1)}, bf16[48,1536]{1,0:T(8,128)(2,1)S(1)}, u32[]{:S(2)}, u32[]{:S(2)}) collective-permute-start(bf16[48,1536]{1,0:T(8,128)(2,1)S(1)} %get-tuple-element.89), channel_id=1, source_target_pairs={{0,3},{1,0},{2,1},{3,2},{4,7},{5,4},{6,5},{7,6},{8,11},{9,8},{10,9... | collective-permute-start | bytes 442376 | tf_op jit(solution)/shard_map/ppermute | solution.py:34
  137.1 0.7 collective-permute-done.25
  137.7 1.8 %collective-permute-done.27 = bf16[48,1536]{1,0:T(8,128)(2,1)S(1)} collective-permute-done((bf16[48,1536]{1,0:T(8,128)(2,1)S(1)}, bf16[48,1536]{1,0:T(8,128)(2,1)S(1)}, u32[]{:S(2)}, u32[]{:S(2)}) %collective-permute-start.27) | collective-permute-done | bytes 147488 | tf_op jit(solution)/shard_map/ppermute | solution.py:34
  139.6 0.3 collective-permute-done.26
  139.9 0.1 fusion.15
  140.0 2.0 %collective-permute-start.28 = (bf16[48,768]{1,0:T(8,128)(2,1)S(1)}, bf16[48,768]{1,0:T(8,128)(2,1)S(1)}, u32[]{:S(2)}, u32[]{:S(2)}) collective-permute-start(bf16[48,768]{1,0:T(8,128)(2,1)S(1)} %get-tuple-element.93), channel_id=1, source_target_pairs={{0,16},{1,17},{2,18},{3,19},{4,20},{5,21},{6,22},{7,23},{8,24},{9,... | collective-permute-start | bytes 221192 | tf_op jit(solution)/shard_map/ppermute | solution.py:34
  142.0 0.9 collective-permute-done.28
  143.0 0.7 maximum_select_fusion.1
  (46 shorter events, 0.3 us)
Async XLA Ops:
  7.2 4.1 %copy-start.11 = (bf16[96,768]{1,0:T(8,128)(2,1)S(1)}, bf16[96,768]{1,0:T(8,128)(2,1)}, u32[]{:S(2)}) copy-start(bf16[96,768]{1,0:T(8,128)(2,1)} %param.6) | copy-start | bytes 442372
  7.2 73.0 %all-gather.3.cloned.1.call-start = ((), (), s32[]{:S(2)}) async-start(), calls=%async_computation | async-start | bytes 5308416 | tf_op jit(solution)/shard_map/all_gather | solution.py:319
  9.6 109.6 %all-gather.5.cloned.1.call-start = ((), (), s32[]{:S(2)}) async-start(), calls=%async_computation.1 | async-start | bytes 2506752 | tf_op jit(solution)/shard_map/all_gather | solution.py:337
  9.7 10.2 %collective-permute-start.4 = (bf16[768,1536]{1,0:T(8,128)(2,1)}, bf16[768,1536]{1,0:T(8,128)(2,1)S(1)}, u32[]{:S(2)}, u32[]{:S(2)}) collective-permute-start(bf16[768,1536]{1,0:T(8,128)(2,1)} %w_own.1), channel_id=1, source_target_pairs={{0,16},{1,17},{2,18},{3,19},{4,20},{5,21},{6,22},{7,23},{8,24},{9,... | collective-permute-start | bytes 7077896 | tf_op jit(solution)/shard_map/ppermute | solution.py:34
  11.2 8.7 %collective-permute-start.3 = (bf16[1536,768]{1,0:T(8,128)(2,1)}, bf16[1536,768]{1,0:T(8,128)(2,1)}, u32[]{:S(2)}, u32[]{:S(2)}) collective-permute-start(bf16[1536,768]{1,0:T(8,128)(2,1)} %refs_8_.3), channel_id=1, source_target_pairs={{0,16},{1,17},{2,18},{3,19},{4,20},{5,21},{6,22},{7,23},{8,24},{9,... | collective-permute-start | bytes 7077896 | tf_op jit(solution)/shard_map/ppermute | solution.py:34
  11.3 5.6 %collective-permute-start.1 = (bf16[96,768]{1,0:T(8,128)(2,1)S(1)}, bf16[96,768]{1,0:T(8,128)(2,1)S(1)}, u32[]{:S(2)}, u32[]{:S(2)}) collective-permute-start(bf16[96,768]{1,0:T(8,128)(2,1)S(1)} %copy-done.11), channel_id=1, source_target_pairs={{0,4},{1,5},{2,6},{3,7},{4,8},{5,9},{6,10},{7,11},{8,12},{9,13},{1... | collective-permute-start | bytes 442376 | tf_op jit(solution)/shard_map/ppermute | solution.py:34
  12.6 4.3 %collective-permute-start = (bf16[96,768]{1,0:T(8,128)(2,1)S(1)}, bf16[96,768]{1,0:T(8,128)(2,1)S(1)}, u32[]{:S(2)}, u32[]{:S(2)}) collective-permute-start(bf16[96,768]{1,0:T(8,128)(2,1)S(1)} %copy-done.11), channel_id=1, source_target_pairs={{0,12},{1,13},{2,14},{3,15},{4,0},{5,1},{6,2},{7,3},{8,4},{9,5},{1... | collective-permute-start | bytes 442376 | tf_op jit(solution)/shard_map/ppermute | solution.py:34
  14.1 5.8 %collective-permute-start.2 = (bf16[96,768]{1,0:T(8,128)(2,1)S(1)}, bf16[96,768]{1,0:T(8,128)(2,1)S(1)}, u32[]{:S(2)}, u32[]{:S(2)}) collective-permute-start(bf16[96,768]{1,0:T(8,128)(2,1)S(1)} %copy-done.11), channel_id=1, source_target_pairs={{0,8},{1,9},{2,10},{3,11},{4,12},{5,13},{6,14},{7,15},{8,0},{9,1},... | collective-permute-start | bytes 442376 | tf_op jit(solution)/shard_map/ppermute | solution.py:34
  15.8 39.6 %copy-start.3 = (s32[4]{0:T(128)}, s32[4]{0:T(128)S(1)}, u32[]{:S(2)}) copy-start(s32[4]{0:T(128)S(1)} %pad_add_fusion.where) | copy-start | bytes 52
  19.9 1.4 copy-start.6
  21.4 34.0 %copy-start = (bf16[4,96,768]{2,1,0:T(8,128)(2,1)}, bf16[4,96,768]{2,1,0:T(8,128)(2,1)S(1)}, u32[]{:S(2)}) copy-start(bf16[4,96,768]{2,1,0:T(8,128)(2,1)S(1)} %pad_maximum_fusion.refs_0_.g0) | copy-start | bytes 1769476
  21.4 17.4 %collective-permute-start.8 = (bf16[4,96,768]{2,1,0:T(8,128)(2,1)S(1)}, bf16[4,96,768]{2,1,0:T(8,128)(2,1)S(1)}, u32[]{:S(2)}, u32[]{:S(2)}) collective-permute-start(bf16[4,96,768]{2,1,0:T(8,128)(2,1)S(1)} %pad_maximum_fusion.refs_0_.g0), channel_id=1, source_target_pairs={{0,1},{1,2},{2,3},{3,0},{4,5},{5,6},{6,7},{7,4},{8,9},{9,10},{10,1... | collective-permute-start | bytes 1769480 | tf_op jit(solution)/shard_map/ppermute | solution.py:34
  22.4 19.2 %collective-permute-start.7 = (bf16[4,96,768]{2,1,0:T(8,128)(2,1)S(1)}, bf16[4,96,768]{2,1,0:T(8,128)(2,1)}, u32[]{:S(2)}, u32[]{:S(2)}) collective-permute-start(bf16[4,96,768]{2,1,0:T(8,128)(2,1)S(1)} %pad_maximum_fusion.refs_0_.g0), channel_id=1, source_target_pairs={{0,2},{1,3},{2,0},{3,1},{4,6},{5,7},{6,4},{7,5},{8,10},{9,11},{10,... | collective-permute-start | bytes 1769480 | tf_op jit(solution)/shard_map/ppermute | solution.py:34
  25.1 13.6 %collective-permute-start.5 = (bf16[4,96,768]{2,1,0:T(8,128)(2,1)S(1)}, bf16[4,96,768]{2,1,0:T(8,128)(2,1)}, u32[]{:S(2)}, u32[]{:S(2)}) collective-permute-start(bf16[4,96,768]{2,1,0:T(8,128)(2,1)S(1)} %pad_maximum_fusion.refs_0_.g0), channel_id=1, source_target_pairs={{0,3},{1,0},{2,1},{3,2},{4,7},{5,4},{6,5},{7,6},{8,11},{9,8},{10,9... | collective-permute-start | bytes 1769480 | tf_op jit(solution)/shard_map/ppermute | solution.py:34
  26.0 19.5 %copy-start.1 = (bf16[1536,768]{1,0:T(8,128)(2,1)S(1)}, bf16[1536,768]{1,0:T(8,128)(2,1)}, u32[]{:S(2)}) copy-start(bf16[1536,768]{1,0:T(8,128)(2,1)} %refs_8_.3) | copy-start | bytes 7077892
  28.0 5.0 %collective-permute-start.6 = (bf16[2,48,1536]{2,1,0:T(8,128)(2,1)}, bf16[2,48,1536]{2,1,0:T(8,128)(2,1)}, u32[]{:S(2)}, u32[]{:S(2)}) collective-permute-start(bf16[2,48,1536]{2,1,0:T(8,128)(2,1)} %get-tuple-element.91), channel_id=1, source_target_pairs={{0,16},{1,17},{2,18},{3,19},{4,20},{5,21},{6,22},{7,23},{8,24},{9,... | collective-permute-start | bytes 884744 | tf_op jit(solution)/shard_map/ppermute | solution.py:34
  31.1 11.0 %collective-permute-start.9 = (bf16[4,96,768]{2,1,0:T(8,128)(2,1)S(1)}, bf16[4,96,768]{2,1,0:T(8,128)(2,1)S(1)}, u32[]{:S(2)}, u32[]{:S(2)}) collective-permute-start(bf16[4,96,768]{2,1,0:T(8,128)(2,1)S(1)} %pad_maximum_fusion.refs_0_.g0), channel_id=1, source_target_pairs={{0,16},{1,17},{2,18},{3,19},{4,20},{5,21},{6,22},{7,23},{8,24},{9,... | collective-permute-start | bytes 1769480 | tf_op jit(solution)/shard_map/ppermute | solution.py:34
  38.7 16.7 %copy-start.2 = (bf16[4,96,768]{2,1,0:T(8,128)(2,1)}, bf16[4,96,768]{2,1,0:T(8,128)(2,1)S(1)}, u32[]{:S(2)}) copy-start(bf16[4,96,768]{2,1,0:T(8,128)(2,1)S(1)} %collective-permute-done.8.refs_3_.g3) | copy-start | bytes 1769476
  38.7 4.6 %collective-permute-start.12 = (bf16[4,96,768]{2,1,0:T(8,128)(2,1)S(1)}, bf16[4,96,768]{2,1,0:T(8,128)(2,1)S(1)}, u32[]{:S(2)}, u32[]{:S(2)}) collective-permute-start(bf16[4,96,768]{2,1,0:T(8,128)(2,1)S(1)} %collective-permute-done.8.refs_3_.g3), channel_id=1, source_target_pairs={{0,16},{1,17},{2,18},{3,19},{4,20},{5,21},{6,22},{7,23},{8,24},{9,... | collective-permute-start | bytes 1769480 | tf_op jit(solution)/shard_map/ppermute | solution.py:34
  41.6 2.8 %collective-permute-start.11 = (bf16[4,96,768]{2,1,0:T(8,128)(2,1)}, bf16[4,96,768]{2,1,0:T(8,128)(2,1)S(1)}, u32[]{:S(2)}, u32[]{:S(2)}) collective-permute-start(bf16[4,96,768]{2,1,0:T(8,128)(2,1)} %collective-permute-done.7.refs_2_.g2), channel_id=1, source_target_pairs={{0,16},{1,17},{2,18},{3,19},{4,20},{5,21},{6,22},{7,23},{8,24},{9,... | collective-permute-start | bytes 1769480 | tf_op jit(solution)/shard_map/ppermute | solution.py:34
  42.0 3.5 %collective-permute-start.10 = (bf16[4,96,768]{2,1,0:T(8,128)(2,1)}, bf16[4,96,768]{2,1,0:T(8,128)(2,1)S(1)}, u32[]{:S(2)}, u32[]{:S(2)}) collective-permute-start(bf16[4,96,768]{2,1,0:T(8,128)(2,1)} %collective-permute-done.5.refs_1_.g1), channel_id=1, source_target_pairs={{0,16},{1,17},{2,18},{3,19},{4,20},{5,21},{6,22},{7,23},{8,24},{9,... | collective-permute-start | bytes 1769480 | tf_op jit(solution)/shard_map/ppermute | solution.py:34
  51.6 16.9 %collective-permute-start.13 = (bf16[192,1536]{1,0:T(8,128)(2,1)S(1)}, bf16[192,1536]{1,0:T(8,128)(2,1)S(1)}, u32[]{:S(2)}, u32[]{:S(2)}) collective-permute-start(bf16[192,1536]{1,0:T(8,128)(2,1)S(1)} %get-tuple-element.50), channel_id=1, source_target_pairs={{0,32},{1,33},{2,34},{3,35},{4,36},{5,37},{6,38},{7,39},{8,40},{9,... | collective-permute-start | bytes 1769480 | tf_op jit(solution)/shard_map/ppermute | solution.py:34
  53.8 14.6 %collective-permute-start.14 = (bf16[192,1536]{1,0:T(8,128)(2,1)S(1)}, bf16[192,1536]{1,0:T(8,128)(2,1)S(1)}, u32[]{:S(2)}, u32[]{:S(2)}) collective-permute-start(bf16[192,1536]{1,0:T(8,128)(2,1)S(1)} %get-tuple-element.51), channel_id=1, source_target_pairs={{0,96},{1,97},{2,98},{3,99},{4,100},{5,101},{6,102},{7,103},{8,104... | collective-permute-start | bytes 1769480 | tf_op jit(solution)/shard_map/ppermute | solution.py:34
  68.6 8.7 %collective-permute-start.15 = (bf16[96,1536]{1,0:T(8,128)(2,1)S(1)}, bf16[96,1536]{1,0:T(8,128)(2,1)S(1)}, u32[]{:S(2)}, u32[]{:S(2)}) collective-permute-start(bf16[96,1536]{1,0:T(8,128)(2,1)S(1)} %get-tuple-element.85), channel_id=1, source_target_pairs={{0,32},{1,33},{2,34},{3,35},{4,36},{5,37},{6,38},{7,39},{8,40},{9,... | collective-permute-start | bytes 884744 | tf_op jit(solution)/shard_map/ppermute | solution.py:34
  70.1 7.2 %collective-permute-start.16 = (bf16[96,1536]{1,0:T(8,128)(2,1)S(1)}, bf16[96,1536]{1,0:T(8,128)(2,1)S(1)}, u32[]{:S(2)}, u32[]{:S(2)}) collective-permute-start(bf16[96,1536]{1,0:T(8,128)(2,1)S(1)} %get-tuple-element.86), channel_id=1, source_target_pairs={{0,96},{1,97},{2,98},{3,99},{4,100},{5,101},{6,102},{7,103},{8,104... | collective-permute-start | bytes 884744 | tf_op jit(solution)/shard_map/ppermute | solution.py:34
  71.5 6.0 %copy-start.5 = (f32[4,48,1536]{2,1,0:T(8,128)S(1)}, f32[4,48,1536]{2,1,0:T(8,128)}, u32[]{:S(2)}) copy-start(f32[4,48,1536]{2,1,0:T(8,128)} %fusion.10) | copy-start | bytes 3538948
  77.7 12.5 %copy-start.7 = (bf16[4,48,1536]{2,1,0:T(8,128)(2,1)}, bf16[4,48,1536]{2,1,0:T(8,128)(2,1)S(1)}, u32[]{:S(2)}) copy-start(bf16[4,48,1536]{2,1,0:T(8,128)(2,1)S(1)} %multiply_convert_fusion.h0) | copy-start | bytes 1769476
  77.7 12.8 %collective-permute-start.18 = (bf16[4,48,1536]{2,1,0:T(8,128)(2,1)S(1)}, bf16[4,48,1536]{2,1,0:T(8,128)(2,1)S(1)}, u32[]{:S(2)}, u32[]{:S(2)}) collective-permute-start(bf16[4,48,1536]{2,1,0:T(8,128)(2,1)S(1)} %multiply_convert_fusion.h0), channel_id=1, source_target_pairs={{0,96},{1,97},{2,98},{3,99},{4,100},{5,101},{6,102},{7,103},{8,104... | collective-permute-start | bytes 1769480 | tf_op jit(solution)/shard_map/ppermute | solution.py:34
  80.1 13.4 %collective-permute-start.17 = (bf16[4,48,1536]{2,1,0:T(8,128)(2,1)S(1)}, bf16[4,48,1536]{2,1,0:T(8,128)(2,1)S(1)}, u32[]{:S(2)}, u32[]{:S(2)}) collective-permute-start(bf16[4,48,1536]{2,1,0:T(8,128)(2,1)S(1)} %multiply_convert_fusion.h0), channel_id=1, source_target_pairs={{0,32},{1,33},{2,34},{3,35},{4,36},{5,37},{6,38},{7,39},{8,40},{9,... | collective-permute-start | bytes 1769480 | tf_op jit(solution)/shard_map/ppermute | solution.py:34
  90.2 10.3 %copy-start.4 = (s32[4]{0:T(128)S(1)}, s32[4]{0:T(128)}, u32[]{:S(2)}) copy-start(s32[4]{0:T(128)} %copy-done.3) | copy-start | bytes 52
  90.5 10.0 %copy-start.8 = (bf16[4,48,1536]{2,1,0:T(8,128)(2,1)}, bf16[4,48,1536]{2,1,0:T(8,128)(2,1)S(1)}, u32[]{:S(2)}) copy-start(bf16[4,48,1536]{2,1,0:T(8,128)(2,1)S(1)} %collective-permute-done.18.h1) | copy-start | bytes 1769476
  93.6 6.9 %copy-start.9 = (bf16[4,48,1536]{2,1,0:T(8,128)(2,1)}, bf16[4,48,1536]{2,1,0:T(8,128)(2,1)S(1)}, u32[]{:S(2)}) copy-start(bf16[4,48,1536]{2,1,0:T(8,128)(2,1)S(1)} %collective-permute-done.17.h3) | copy-start | bytes 1769476
  93.6 6.9 %collective-permute-start.19 = (bf16[2,48,1536]{2,1,0:T(8,128)(2,1)S(1)}, bf16[2,48,1536]{2,1,0:T(8,128)(2,1)S(1)}, u32[]{:S(2)}, u32[]{:S(2)}) collective-permute-start(bf16[2,48,1536]{2,1,0:T(8,128)(2,1)S(1)} %slice.51), channel_id=1, source_target_pairs={{0,32},{1,33},{2,34},{3,35},{4,36},{5,37},{6,38},{7,39},{8,40},{9,... | collective-permute-start | bytes 884744 | tf_op jit(solution)/shard_map/ppermute | solution.py:34
  93.7 6.8 %collective-permute-start.20 = (bf16[2,48,1536]{2,1,0:T(8,128)(2,1)S(1)}, bf16[2,48,1536]{2,1,0:T(8,128)(2,1)S(1)}, u32[]{:S(2)}, u32[]{:S(2)}) collective-permute-start(bf16[2,48,1536]{2,1,0:T(8,128)(2,1)S(1)} %slice.52), channel_id=1, source_target_pairs={{0,96},{1,97},{2,98},{3,99},{4,100},{5,101},{6,102},{7,103},{8,104... | collective-permute-start | bytes 884744 | tf_op jit(solution)/shard_map/ppermute | solution.py:34
  110.0 9.3 %collective-permute-start.24 = (bf16[4,4,48,1536]{3,2,1,0:T(8,128)(2,1)}, bf16[4,4,48,1536]{3,2,1,0:T(8,128)(2,1)}, u32[]{:S(2)}, u32[]{:S(2)}) collective-permute-start(bf16[4,4,48,1536]{3,2,1,0:T(8,128)(2,1)} %get-tuple-element.77), channel_id=1, source_target_pairs={{0,16},{1,17},{2,18},{3,19},{4,20},{5,21},{6,22},{7,23},{8,24},{9,... | collective-permute-start | bytes 7077896 | tf_op jit(solution)/shard_map/ppermute | solution.py:34
  114.6 13.8 %collective-permute-start.21 = (bf16[4,48,1536]{2,1,0:T(8,128)(2,1)S(1)}, bf16[4,48,1536]{2,1,0:T(8,128)(2,1)S(1)}, u32[]{:S(2)}, u32[]{:S(2)}) collective-permute-start(bf16[4,48,1536]{2,1,0:T(8,128)(2,1)S(1)} %get-tuple-element.73), channel_id=1, source_target_pairs={{0,4},{1,5},{2,6},{3,7},{4,8},{5,9},{6,10},{7,11},{8,12},{9,13},{1... | collective-permute-start | bytes 1769480 | tf_op jit(solution)/shard_map/ppermute | solution.py:34
  116.6 11.8 %collective-permute-start.22 = (bf16[4,48,1536]{2,1,0:T(8,128)(2,1)}, bf16[4,48,1536]{2,1,0:T(8,128)(2,1)S(1)}, u32[]{:S(2)}, u32[]{:S(2)}) collective-permute-start(bf16[4,48,1536]{2,1,0:T(8,128)(2,1)} %get-tuple-element.74), channel_id=1, source_target_pairs={{0,12},{1,13},{2,14},{3,15},{4,0},{5,1},{6,2},{7,3},{8,4},{9,5},{1... | collective-permute-start | bytes 1769480 | tf_op jit(solution)/shard_map/ppermute | solution.py:34
  117.2 14.5 %collective-permute-start.23 = (bf16[4,48,1536]{2,1,0:T(8,128)(2,1)S(1)}, bf16[4,48,1536]{2,1,0:T(8,128)(2,1)S(1)}, u32[]{:S(2)}, u32[]{:S(2)}) collective-permute-start(bf16[4,48,1536]{2,1,0:T(8,128)(2,1)S(1)} %get-tuple-element.75), channel_id=1, source_target_pairs={{0,8},{1,9},{2,10},{3,11},{4,12},{5,13},{6,14},{7,15},{8,0},{9,1},... | collective-permute-start | bytes 1769480 | tf_op jit(solution)/shard_map/ppermute | solution.py:34
  119.2 12.5 %copy-start.10 = (f32[4,48,1536]{2,1,0:T(8,128)S(1)}, f32[4,48,1536]{2,1,0:T(8,128)}, u32[]{:S(2)}) copy-start(f32[4,48,1536]{2,1,0:T(8,128)} %get-tuple-element.72) | copy-start | bytes 3538948
  132.2 5.6 %collective-permute-start.25 = (bf16[48,1536]{1,0:T(8,128)(2,1)S(1)}, bf16[48,1536]{1,0:T(8,128)(2,1)S(1)}, u32[]{:S(2)}, u32[]{:S(2)}) collective-permute-start(bf16[48,1536]{1,0:T(8,128)(2,1)S(1)} %get-tuple-element.87), channel_id=1, source_target_pairs={{0,1},{1,2},{2,3},{3,0},{4,5},{5,6},{6,7},{7,4},{8,9},{9,10},{10,1... | collective-permute-start | bytes 442376 | tf_op jit(solution)/shard_map/ppermute | solution.py:34
  133.7 5.9 %collective-permute-start.27 = (bf16[48,1536]{1,0:T(8,128)(2,1)S(1)}, bf16[48,1536]{1,0:T(8,128)(2,1)S(1)}, u32[]{:S(2)}, u32[]{:S(2)}) collective-permute-start(bf16[48,1536]{1,0:T(8,128)(2,1)S(1)} %get-tuple-element.88), channel_id=1, source_target_pairs={{0,2},{1,3},{2,0},{3,1},{4,6},{5,7},{6,4},{7,5},{8,10},{9,11},{10,... | collective-permute-start | bytes 442376 | tf_op jit(solution)/shard_map/ppermute | solution.py:34
  135.2 4.7 %collective-permute-start.26 = (bf16[48,1536]{1,0:T(8,128)(2,1)S(1)}, bf16[48,1536]{1,0:T(8,128)(2,1)S(1)}, u32[]{:S(2)}, u32[]{:S(2)}) collective-permute-start(bf16[48,1536]{1,0:T(8,128)(2,1)S(1)} %get-tuple-element.89), channel_id=1, source_target_pairs={{0,3},{1,0},{2,1},{3,2},{4,7},{5,4},{6,5},{7,6},{8,11},{9,8},{10,9... | collective-permute-start | bytes 442376 | tf_op jit(solution)/shard_map/ppermute | solution.py:34
  140.0 2.9 %collective-permute-start.28 = (bf16[48,768]{1,0:T(8,128)(2,1)S(1)}, bf16[48,768]{1,0:T(8,128)(2,1)S(1)}, u32[]{:S(2)}, u32[]{:S(2)}) collective-permute-start(bf16[48,768]{1,0:T(8,128)(2,1)S(1)} %get-tuple-element.93), channel_id=1, source_target_pairs={{0,16},{1,17},{2,18},{3,19},{4,20},{5,21},{6,22},{7,23},{8,24},{9,... | collective-permute-start | bytes 221192 | tf_op jit(solution)/shard_map/ppermute | solution.py:34
Sparse Core Ops, SparseCore 0:
  9.7 38.1 all-gather.2
  71.5 45.0 all-gather.4

commit v5 on v4

--- a/solution.py
+++ b/solution.py
@@ -179,11 +179,13 @@
         copy.start()
     for copy in fills:
         copy.wait()
-    stores = [pltpu.make_async_copy(lhs, rows_out, out_sems.at[2, 0])]
-    stores[0].start()
+    rows_copy = pltpu.make_async_copy(lhs, rows_out, out_sems.at[2, 0])
+    stores = [rows_copy]
     for j in range(2):
         loads[j].wait()
         part = pl.ds(j * rows, rows)
+        if j == 1:
+            rows_copy.start()
         total = dot_nt(lhs[...].reshape(16 * n, -1), w[part]).reshape(N, N, n, -1)
         near[:, :, part] = total[0]
         for r in (1, 2, 3):

time: 151 us -> 151 us (level)
  no operation moved by 1% of the time
where the time goes in v5:
time: 151 us; the launch traced here: 150 us
  starting transfers between devices  45.1 us (30%)
  Pallas kernels  40.9 us (27%)
  waiting for transfers between devices  39.4 us (26%)
  between operations  14.3 us (9%)
  other arithmetic  7.14 us (5%)
  local copies, waits for them, and re-layouts  3.62 us (2%)
    ppermute x29, starting transfers between devices, permute(): return lax.ppermute(array, AXES, pairs)  45 us
    ppermute x29, waiting for transfers between devices, permute(): return lax.ppermute(array, AXES, pairs)  39.4 us
    pallas_call x2, Pallas kernels, act_grad_parts(): pl.pallas_call(functools.partial(act_grad_kernel, part), out_shape=[jax.S...  12.3 us
    pallas_call x1, Pallas kernels, weight_out_grad_of(): pl.pallas_call(weight_out_grad_kernel, out_shape=jax.ShapeDtypeStruct((hi...  10 us
    pallas_call x1, Pallas kernels, input_grad_parts(): pl.pallas_call(input_grad_kernel, out_shape=[jax.ShapeDtypeStruct((N, n,...  9.45 us
    pallas_call x1, Pallas kernels, weight_in_grad_of(): pl.pallas_call(weight_in_grad_kernel, out_shape=jax.ShapeDtypeStruct((wid...  9.15 us
    add x1, other arithmetic, gelu_parts(): 0.5 * (1.0 + tanh_value)  3.05 us
  transfers between devices with their start and end apart: 31, of which 18 were waited for; matrix products, arithmetic and copies ran while one was open for 4% of the time, Pallas kernels for 27%

profile of v5, /device:TPU:1, one launch (start us, length us, event | category | flops | bytes accessed | tf_op | source)
XLA Modules:
  0.0 150.5 jit_solution(2609121423702841540)
XLA Ops:
  7.2 0.0 all-gather.3.cloned.1.call-start
  7.2 2.4 %fusion.1 = bf16[192,1536]{1,0:T(8,128)(2,1)} fusion(bf16[192,1536]{1,0:T(8,128)(2,1)} %param.7), kind=kLoop, calls=%fused_computation.13 | loop fusion | flops 2949120 | bytes 1179648 | tf_op jit(solution)/shard_map/convert_element_type | solution.py:320
  9.6 0.0 all-gather.5.cloned.1.call-start
  9.7 1.5 collective-permute-start.4
  11.2 0.1 collective-permute-start.3
  11.3 1.4 collective-permute-start.1
  12.6 1.4 collective-permute-start
  14.1 1.6 %collective-permute-start.2 = (bf16[96,768]{1,0:T(8,128)(2,1)S(1)}, bf16[96,768]{1,0:T(8,128)(2,1)S(1)}, u32[]{:S(2)}, u32[]{:S(2)}) collective-permute-start(bf16[96,768]{1,0:T(8,128)(2,1)S(1)} %copy-done.11), channel_id=1, source_target_pairs={{0,8},{1,9},{2,10},{3,11},{4,12},{5,13},{6,14},{7,15},{8,0},{9,1},... | collective-permute-start | bytes 442376 | tf_op jit(solution)/shard_map/ppermute | solution.py:34
  15.7 0.1 pad_add_fusion.where
  15.8 1.1 collective-permute-done.1
  16.9 2.9 %collective-permute-done.2 = bf16[96,768]{1,0:T(8,128)(2,1)S(1)} collective-permute-done((bf16[96,768]{1,0:T(8,128)(2,1)S(1)}, bf16[96,768]{1,0:T(8,128)(2,1)S(1)}, u32[]{:S(2)}, u32[]{:S(2)}) %collective-permute-start.2) | collective-permute-done | bytes 147488 | tf_op jit(solution)/shard_map/ppermute | solution.py:34
  19.9 1.4 copy-done.6
  21.3 0.1 pad_maximum_fusion.refs_0_.g0
  21.4 1.0 collective-permute-start.8
  22.4 2.7 %collective-permute-start.7 = (bf16[4,96,768]{2,1,0:T(8,128)(2,1)S(1)}, bf16[4,96,768]{2,1,0:T(8,128)(2,1)}, u32[]{:S(2)}, u32[]{:S(2)}) collective-permute-start(bf16[4,96,768]{2,1,0:T(8,128)(2,1)S(1)} %pad_maximum_fusion.refs_0_.g0), channel_id=1, source_target_pairs={{0,2},{1,3},{2,0},{3,1},{4,6},{5,7},{6,4},{7,5},{8,10},{9,11},{10,... | collective-permute-start | bytes 1769480 | tf_op jit(solution)/shard_map/ppermute | solution.py:34
  25.1 0.9 collective-permute-start.5
  26.0 2.0 %dynamic-slice_bitcast_fusion.1 = (bf16[2,48,1536]{2,1,0:T(8,128)(2,1)}, bf16[2,48,1536]{2,1,0:T(8,128)(2,1)}) fusion(bf16[2,2,48,1536]{3,2,1,0:T(8,128)(2,1)} %bitcast.38, s32[]{:T(128)S(6)} %select_n.47, s32[]{:T(128)S(6)} %select_n.48), kind=kLoop, calls=%fused_computation.37 | loop fusion | bytes 1179656 | tf_op jit(solution)/shard_map/jit(dynamic_index_in_dim)/squeeze | solution.py:308
  28.0 3.1 %collective-permute-start.6 = (bf16[2,48,1536]{2,1,0:T(8,128)(2,1)}, bf16[2,48,1536]{2,1,0:T(8,128)(2,1)}, u32[]{:S(2)}, u32[]{:S(2)}) collective-permute-start(bf16[2,48,1536]{2,1,0:T(8,128)(2,1)} %get-tuple-element.91), channel_id=1, source_target_pairs={{0,16},{1,17},{2,18},{3,19},{4,20},{5,21},{6,22},{7,23},{8,24},{9,... | collective-permute-start | bytes 884744 | tf_op jit(solution)/shard_map/ppermute | solution.py:34
  31.1 1.9 %collective-permute-done.6 = bf16[2,48,1536]{2,1,0:T(8,128)(2,1)} collective-permute-done((bf16[2,48,1536]{2,1,0:T(8,128)(2,1)}, bf16[2,48,1536]{2,1,0:T(8,128)(2,1)}, u32[]{:S(2)}, u32[]{:S(2)}) %collective-permute-start.6) | collective-permute-done | bytes 294944 | tf_op jit(solution)/shard_map/ppermute | solution.py:34
  33.0 3.0 %fusion.10 = f32[4,48,1536]{2,1,0:T(8,128)} fusion(bf16[2,48,1536]{2,1,0:T(8,128)(2,1)} %collective-permute-done.6, bf16[2,48,1536]{2,1,0:T(8,128)(2,1)} %get-tuple-element.90, pred[]{:T(512)S(6)} %eq.7), kind=kLoop, calls=%fused_computation.22 | loop fusion | flops 6193152 | bytes 1769473 | tf_op jit(solution)/shard_map/add | solution.py:57
  36.1 2.6 %collective-permute-done.5.refs_1_.g1 = bf16[4,96,768]{2,1,0:T(8,128)(2,1)} collective-permute-done((bf16[4,96,768]{2,1,0:T(8,128)(2,1)S(1)}, bf16[4,96,768]{2,1,0:T(8,128)(2,1)}, u32[]{:S(2)}, u32[]{:S(2)}) %collective-permute-start.5) | collective-permute-done | bytes 589856 | tf_op jit(solution)/shard_map/ppermute | solution.py:34
  38.7 2.8 %collective-permute-start.12 = (bf16[4,96,768]{2,1,0:T(8,128)(2,1)S(1)}, bf16[4,96,768]{2,1,0:T(8,128)(2,1)S(1)}, u32[]{:S(2)}, u32[]{:S(2)}) collective-permute-start(bf16[4,96,768]{2,1,0:T(8,128)(2,1)S(1)} %collective-permute-done.8.refs_3_.g3), channel_id=1, source_target_pairs={{0,16},{1,17},{2,18},{3,19},{4,20},{5,21},{6,22},{7,23},{8,24},{9,... | collective-permute-start | bytes 1769480 | tf_op jit(solution)/shard_map/ppermute | solution.py:34
  41.6 0.4 collective-permute-start.11
  42.0 0.1 collective-permute-start.10
  42.1 1.3 collective-permute-done.12.refs_7_
  43.4 1.1 collective-permute-done.11.refs_6_
  44.4 1.1 collective-permute-done.10.refs_5_
  45.5 6.1 %act_grad.2 = (bf16[192,1536]{1,0:T(8,128)(2,1)S(1)}, bf16[192,1536]{1,0:T(8,128)(2,1)S(1)}) custom-call(s32[4]{0:T(128)S(1)} %pad_add_fusion.where, bf16[4,96,768]{2,1,0:T(8,128)(2,1)S(1)} %pad_maximum_fusion.refs_0_.g0, bf16[4,96,768]{2,1,0:T(8,128)(2,1)} %collective-permute-done.5.refs_1_.g1, bf16[4,96,768]{2,1,0:T(8,128)(2,1)} %collective-permute-done.7.refs_2_.g2, ...), custom_call_target="tpu_custom_call" | custom-call | flops 1024 | bytes 1024 | tf_op jit(solution)/shard_map/act_grad/pallas_call | solution.py:134
  51.6 2.2 %collective-permute-start.13 = (bf16[192,1536]{1,0:T(8,128)(2,1)S(1)}, bf16[192,1536]{1,0:T(8,128)(2,1)S(1)}, u32[]{:S(2)}, u32[]{:S(2)}) collective-permute-start(bf16[192,1536]{1,0:T(8,128)(2,1)S(1)} %get-tuple-element.50), channel_id=1, source_target_pairs={{0,32},{1,33},{2,34},{3,35},{4,36},{5,37},{6,38},{7,39},{8,40},{9,... | collective-permute-start | bytes 1769480 | tf_op jit(solution)/shard_map/ppermute | solution.py:34
  53.8 1.6 %collective-permute-start.14 = (bf16[192,1536]{1,0:T(8,128)(2,1)S(1)}, bf16[192,1536]{1,0:T(8,128)(2,1)S(1)}, u32[]{:S(2)}, u32[]{:S(2)}) collective-permute-start(bf16[192,1536]{1,0:T(8,128)(2,1)S(1)} %get-tuple-element.51), channel_id=1, source_target_pairs={{0,96},{1,97},{2,98},{3,99},{4,100},{5,101},{6,102},{7,103},{8,104... | collective-permute-start | bytes 1769480 | tf_op jit(solution)/shard_map/ppermute | solution.py:34
  55.4 6.2 %act_grad.3 = (f32[192,1536]{1,0:T(8,128)S(1)}, f32[192,1536]{1,0:T(8,128)S(1)}) custom-call(s32[4]{0:T(128)S(1)} %pad_add_fusion.where, bf16[4,96,768]{2,1,0:T(8,128)(2,1)S(1)} %pad_maximum_fusion.refs_0_.g0, bf16[4,96,768]{2,1,0:T(8,128)(2,1)} %collective-permute-done.5.refs_1_.g1, bf16[4,96,768]{2,1,0:T(8,128)(2,1)} %collective-permute-done.7.refs_2_.g2, ...), custom_call_target="tpu_custom_call" | custom-call | flops 8000000000 | bytes 16777216 | tf_op jit(solution)/shard_map/act_grad/pallas_call | solution.py:134
  61.7 6.7 %collective-permute-done.14 = bf16[192,1536]{1,0:T(8,128)(2,1)S(1)} collective-permute-done((bf16[192,1536]{1,0:T(8,128)(2,1)S(1)}, bf16[192,1536]{1,0:T(8,128)(2,1)S(1)}, u32[]{:S(2)}, u32[]{:S(2)}) %collective-permute-start.14) | collective-permute-done | bytes 589856 | tf_op jit(solution)/shard_map/ppermute | solution.py:34
  68.4 0.1 collective-permute-done.13
  68.5 0.1 add_convert_fusion.1
  68.6 1.4 collective-permute-start.15
  70.1 1.3 collective-permute-start.16
  71.5 5.8 %collective-permute-done.15 = bf16[96,1536]{1,0:T(8,128)(2,1)S(1)} collective-permute-done((bf16[96,1536]{1,0:T(8,128)(2,1)S(1)}, bf16[96,1536]{1,0:T(8,128)(2,1)S(1)}, u32[]{:S(2)}, u32[]{:S(2)}) %collective-permute-start.15) | collective-permute-done | bytes 294944 | tf_op jit(solution)/shard_map/ppermute | solution.py:34
  77.3 0.2 convert_add_fusion.3
  77.5 0.1 multiply_convert_fusion.h0
  77.7 2.5 %collective-permute-start.18 = (bf16[4,48,1536]{2,1,0:T(8,128)(2,1)S(1)}, bf16[4,48,1536]{2,1,0:T(8,128)(2,1)S(1)}, u32[]{:S(2)}, u32[]{:S(2)}) collective-permute-start(bf16[4,48,1536]{2,1,0:T(8,128)(2,1)S(1)} %multiply_convert_fusion.h0), channel_id=1, source_target_pairs={{0,96},{1,97},{2,98},{3,99},{4,100},{5,101},{6,102},{7,103},{8,104... | collective-permute-start | bytes 1769480 | tf_op jit(solution)/shard_map/ppermute | solution.py:34
  80.1 10.0 %weight_out_grad.1 = f32[1536,768]{1,0:T(8,128)} custom-call(s32[4]{0:T(128)} %copy-done.3, bf16[1536,1536]{1,0:T(8,128)(2,1)} %all-gather.3.cloned.1.call-done.act, bf16[4,96,768]{2,1,0:T(8,128)(2,1)} %copy-done, bf16[4,96,768]{2,1,0:T(8,128)(2,1)} %collective-permute-done.5.refs_1_.g1, bf16[4,96,768]{2,1,0:T(8,128)(2,1)} %collective-permute-done.7.refs_2_.g2, ...), custom_call_target="tpu_custom_call" | custom-call | flops 8000000000 | bytes 16777216 | tf_op jit(solution)/shard_map/weight_out_grad/pallas_call | solution.py:249
  90.2 0.3 collective-permute-done.18.h1
  90.5 3.1 %collective-permute-done.17.h3 = bf16[4,48,1536]{2,1,0:T(8,128)(2,1)S(1)} collective-permute-done((bf16[4,48,1536]{2,1,0:T(8,128)(2,1)S(1)}, bf16[4,48,1536]{2,1,0:T(8,128)(2,1)S(1)}, u32[]{:S(2)}, u32[]{:S(2)}) %collective-permute-start.17) | collective-permute-done | bytes 589856 | tf_op jit(solution)/shard_map/ppermute | solution.py:34
  93.6 0.1 collective-permute-start.19
  93.7 2.7 %collective-permute-start.20 = (bf16[2,48,1536]{2,1,0:T(8,128)(2,1)S(1)}, bf16[2,48,1536]{2,1,0:T(8,128)(2,1)S(1)}, u32[]{:S(2)}, u32[]{:S(2)}) collective-permute-start(bf16[2,48,1536]{2,1,0:T(8,128)(2,1)S(1)} %slice.52), channel_id=1, source_target_pairs={{0,96},{1,97},{2,98},{3,99},{4,100},{5,101},{6,102},{7,103},{8,104... | collective-permute-start | bytes 884744 | tf_op jit(solution)/shard_map/ppermute | solution.py:34
  96.4 4.1 %collective-permute-done.19.h2a = bf16[2,48,1536]{2,1,0:T(8,128)(2,1)S(1)} collective-permute-done((bf16[2,48,1536]{2,1,0:T(8,128)(2,1)S(1)}, bf16[2,48,1536]{2,1,0:T(8,128)(2,1)S(1)}, u32[]{:S(2)}, u32[]{:S(2)}) %collective-permute-start.19) | collective-permute-done | bytes 294944 | tf_op jit(solution)/shard_map/ppermute | solution.py:34
  100.5 9.5 %input_grad.1 = (f32[4,48,1536]{2,1,0:T(8,128)}, bf16[4,48,1536]{2,1,0:T(8,128)(2,1)S(1)}, bf16[4,48,1536]{2,1,0:T(8,128)(2,1)S(1)}, bf16[4,48,1536]{2,1,0:T(8,128)(2,1)}, bf16[4,4,48,1536]{3,2,1,0:T(8,128)(2,1)}) custom-call(s32[4]{0:T(128)S(1)} %copy-done.4, bf16[4,48,1536]{2,1,0:T(8,128)(2,1)} %copy-done.7, bf16[4,48,1536]{2,1,0:T(8,128)(2,1)} %copy-done.8, ...), custom_call_target="tpu_custom_call" | custom-call | flops 1024 | bytes 1024 | tf_op jit(solution)/shard_map/input_grad/pallas_call | solution.py:204
  110.0 4.6 %collective-permute-start.24 = (bf16[4,4,48,1536]{3,2,1,0:T(8,128)(2,1)}, bf16[4,4,48,1536]{3,2,1,0:T(8,128)(2,1)}, u32[]{:S(2)}, u32[]{:S(2)}) collective-permute-start(bf16[4,4,48,1536]{3,2,1,0:T(8,128)(2,1)} %get-tuple-element.77), channel_id=1, source_target_pairs={{0,16},{1,17},{2,18},{3,19},{4,20},{5,21},{6,22},{7,23},{8,24},{9,... | collective-permute-start | bytes 7077896 | tf_op jit(solution)/shard_map/ppermute | solution.py:34
  114.6 2.0 %collective-permute-start.21 = (bf16[4,48,1536]{2,1,0:T(8,128)(2,1)S(1)}, bf16[4,48,1536]{2,1,0:T(8,128)(2,1)S(1)}, u32[]{:S(2)}, u32[]{:S(2)}) collective-permute-start(bf16[4,48,1536]{2,1,0:T(8,128)(2,1)S(1)} %get-tuple-element.73), channel_id=1, source_target_pairs={{0,4},{1,5},{2,6},{3,7},{4,8},{5,9},{6,10},{7,11},{8,12},{9,13},{1... | collective-permute-start | bytes 1769480 | tf_op jit(solution)/shard_map/ppermute | solution.py:34
  116.6 0.7 collective-permute-start.22
  117.2 2.0 %collective-permute-start.23 = (bf16[4,48,1536]{2,1,0:T(8,128)(2,1)S(1)}, bf16[4,48,1536]{2,1,0:T(8,128)(2,1)S(1)}, u32[]{:S(2)}, u32[]{:S(2)}) collective-permute-start(bf16[4,48,1536]{2,1,0:T(8,128)(2,1)S(1)} %get-tuple-element.75), channel_id=1, source_target_pairs={{0,8},{1,9},{2,10},{3,11},{4,12},{5,13},{6,14},{7,15},{8,0},{9,1},... | collective-permute-start | bytes 1769480 | tf_op jit(solution)/shard_map/ppermute | solution.py:34
  119.2 9.2 %weight_in_grad.1 = f32[768,1536]{1,0:T(8,128)} custom-call(s32[4]{0:T(128)} %copy-done.3, bf16[16,2,48,768]{3,2,1,0:T(8,128)(2,1)} %bitcast.43, bf16[768,1536]{1,0:T(8,128)(2,1)} %bitcast.44, bf16[768,1536]{1,0:T(8,128)(2,1)} %bitcast.14.hid_other), custom_call_target="tpu_custom_call" | custom-call | flops 8000000000 | bytes 16777216 | tf_op jit(solution)/shard_map/weight_in_grad/pallas_call | solution.py:284
  128.4 3.4 %collective-permute-done.23 = bf16[4,48,1536]{2,1,0:T(8,128)(2,1)S(1)} collective-permute-done((bf16[4,48,1536]{2,1,0:T(8,128)(2,1)S(1)}, bf16[4,48,1536]{2,1,0:T(8,128)(2,1)S(1)}, u32[]{:S(2)}, u32[]{:S(2)}) %collective-permute-start.23) | collective-permute-done | bytes 589856 | tf_op jit(solution)/shard_map/ppermute | solution.py:34
  131.8 0.4 fusion.16
  132.2 1.5 %collective-permute-start.25 = (bf16[48,1536]{1,0:T(8,128)(2,1)S(1)}, bf16[48,1536]{1,0:T(8,128)(2,1)S(1)}, u32[]{:S(2)}, u32[]{:S(2)}) collective-permute-start(bf16[48,1536]{1,0:T(8,128)(2,1)S(1)} %get-tuple-element.87), channel_id=1, source_target_pairs={{0,1},{1,2},{2,3},{3,0},{4,5},{5,6},{6,7},{7,4},{8,9},{9,10},{10,1... | collective-permute-start | bytes 442376 | tf_op jit(solution)/shard_map/ppermute | solution.py:34
  133.7 1.5 collective-permute-start.27
  135.2 1.9 %collective-permute-start.26 = (bf16[48,1536]{1,0:T(8,128)(2,1)S(1)}, bf16[48,1536]{1,0:T(8,128)(2,1)S(1)}, u32[]{:S(2)}, u32[]{:S(2)}) collective-permute-start(bf16[48,1536]{1,0:T(8,128)(2,1)S(1)} %get-tuple-element.89), channel_id=1, source_target_pairs={{0,3},{1,0},{2,1},{3,2},{4,7},{5,4},{6,5},{7,6},{8,11},{9,8},{10,9... | collective-permute-start | bytes 442376 | tf_op jit(solution)/shard_map/ppermute | solution.py:34
  137.1 0.7 collective-permute-done.25
  137.7 1.8 %collective-permute-done.27 = bf16[48,1536]{1,0:T(8,128)(2,1)S(1)} collective-permute-done((bf16[48,1536]{1,0:T(8,128)(2,1)S(1)}, bf16[48,1536]{1,0:T(8,128)(2,1)S(1)}, u32[]{:S(2)}, u32[]{:S(2)}) %collective-permute-start.27) | collective-permute-done | bytes 147488 | tf_op jit(solution)/shard_map/ppermute | solution.py:34
  139.6 0.3 collective-permute-done.26
  139.9 0.1 fusion.15
  140.0 2.0 %collective-permute-start.28 = (bf16[48,768]{1,0:T(8,128)(2,1)S(1)}, bf16[48,768]{1,0:T(8,128)(2,1)S(1)}, u32[]{:S(2)}, u32[]{:S(2)}) collective-permute-start(bf16[48,768]{1,0:T(8,128)(2,1)S(1)} %get-tuple-element.93), channel_id=1, source_target_pairs={{0,16},{1,17},{2,18},{3,19},{4,20},{5,21},{6,22},{7,23},{8,24},{9,... | collective-permute-start | bytes 221192 | tf_op jit(solution)/shard_map/ppermute | solution.py:34
  142.0 0.9 collective-permute-done.28
  143.0 0.7 maximum_select_fusion.1
  (46 shorter events, 0.3 us)
Async XLA Ops:
  7.2 4.1 %copy-start.11 = (bf16[96,768]{1,0:T(8,128)(2,1)S(1)}, bf16[96,768]{1,0:T(8,128)(2,1)}, u32[]{:S(2)}) copy-start(bf16[96,768]{1,0:T(8,128)(2,1)} %param.6) | copy-start | bytes 442372
  7.2 73.0 %all-gather.3.cloned.1.call-start = ((), (), s32[]{:S(2)}) async-start(), calls=%async_computation | async-start | bytes 5308416 | tf_op jit(solution)/shard_map/all_gather | solution.py:321
  9.6 109.6 %all-gather.5.cloned.1.call-start = ((), (), s32[]{:S(2)}) async-start(), calls=%async_computation.1 | async-start | bytes 2506752 | tf_op jit(solution)/shard_map/all_gather | solution.py:339
  9.7 10.2 %collective-permute-start.4 = (bf16[768,1536]{1,0:T(8,128)(2,1)}, bf16[768,1536]{1,0:T(8,128)(2,1)S(1)}, u32[]{:S(2)}, u32[]{:S(2)}) collective-permute-start(bf16[768,1536]{1,0:T(8,128)(2,1)} %w_own.1), channel_id=1, source_target_pairs={{0,16},{1,17},{2,18},{3,19},{4,20},{5,21},{6,22},{7,23},{8,24},{9,... | collective-permute-start | bytes 7077896 | tf_op jit(solution)/shard_map/ppermute | solution.py:34
  11.2 8.7 %collective-permute-start.3 = (bf16[1536,768]{1,0:T(8,128)(2,1)}, bf16[1536,768]{1,0:T(8,128)(2,1)}, u32[]{:S(2)}, u32[]{:S(2)}) collective-permute-start(bf16[1536,768]{1,0:T(8,128)(2,1)} %refs_8_.3), channel_id=1, source_target_pairs={{0,16},{1,17},{2,18},{3,19},{4,20},{5,21},{6,22},{7,23},{8,24},{9,... | collective-permute-start | bytes 7077896 | tf_op jit(solution)/shard_map/ppermute | solution.py:34
  11.3 5.6 %collective-permute-start.1 = (bf16[96,768]{1,0:T(8,128)(2,1)S(1)}, bf16[96,768]{1,0:T(8,128)(2,1)S(1)}, u32[]{:S(2)}, u32[]{:S(2)}) collective-permute-start(bf16[96,768]{1,0:T(8,128)(2,1)S(1)} %copy-done.11), channel_id=1, source_target_pairs={{0,4},{1,5},{2,6},{3,7},{4,8},{5,9},{6,10},{7,11},{8,12},{9,13},{1... | collective-permute-start | bytes 442376 | tf_op jit(solution)/shard_map/ppermute | solution.py:34
  12.6 4.3 %collective-permute-start = (bf16[96,768]{1,0:T(8,128)(2,1)S(1)}, bf16[96,768]{1,0:T(8,128)(2,1)S(1)}, u32[]{:S(2)}, u32[]{:S(2)}) collective-permute-start(bf16[96,768]{1,0:T(8,128)(2,1)S(1)} %copy-done.11), channel_id=1, source_target_pairs={{0,12},{1,13},{2,14},{3,15},{4,0},{5,1},{6,2},{7,3},{8,4},{9,5},{1... | collective-permute-start | bytes 442376 | tf_op jit(solution)/shard_map/ppermute | solution.py:34
  14.1 5.8 %collective-permute-start.2 = (bf16[96,768]{1,0:T(8,128)(2,1)S(1)}, bf16[96,768]{1,0:T(8,128)(2,1)S(1)}, u32[]{:S(2)}, u32[]{:S(2)}) collective-permute-start(bf16[96,768]{1,0:T(8,128)(2,1)S(1)} %copy-done.11), channel_id=1, source_target_pairs={{0,8},{1,9},{2,10},{3,11},{4,12},{5,13},{6,14},{7,15},{8,0},{9,1},... | collective-permute-start | bytes 442376 | tf_op jit(solution)/shard_map/ppermute | solution.py:34
  15.8 39.6 %copy-start.3 = (s32[4]{0:T(128)}, s32[4]{0:T(128)S(1)}, u32[]{:S(2)}) copy-start(s32[4]{0:T(128)S(1)} %pad_add_fusion.where) | copy-start | bytes 52
  19.9 1.4 copy-start.6
  21.4 34.0 %copy-start = (bf16[4,96,768]{2,1,0:T(8,128)(2,1)}, bf16[4,96,768]{2,1,0:T(8,128)(2,1)S(1)}, u32[]{:S(2)}) copy-start(bf16[4,96,768]{2,1,0:T(8,128)(2,1)S(1)} %pad_maximum_fusion.refs_0_.g0) | copy-start | bytes 1769476
  21.4 17.4 %collective-permute-start.8 = (bf16[4,96,768]{2,1,0:T(8,128)(2,1)S(1)}, bf16[4,96,768]{2,1,0:T(8,128)(2,1)S(1)}, u32[]{:S(2)}, u32[]{:S(2)}) collective-permute-start(bf16[4,96,768]{2,1,0:T(8,128)(2,1)S(1)} %pad_maximum_fusion.refs_0_.g0), channel_id=1, source_target_pairs={{0,1},{1,2},{2,3},{3,0},{4,5},{5,6},{6,7},{7,4},{8,9},{9,10},{10,1... | collective-permute-start | bytes 1769480 | tf_op jit(solution)/shard_map/ppermute | solution.py:34
  22.4 19.2 %collective-permute-start.7 = (bf16[4,96,768]{2,1,0:T(8,128)(2,1)S(1)}, bf16[4,96,768]{2,1,0:T(8,128)(2,1)}, u32[]{:S(2)}, u32[]{:S(2)}) collective-permute-start(bf16[4,96,768]{2,1,0:T(8,128)(2,1)S(1)} %pad_maximum_fusion.refs_0_.g0), channel_id=1, source_target_pairs={{0,2},{1,3},{2,0},{3,1},{4,6},{5,7},{6,4},{7,5},{8,10},{9,11},{10,... | collective-permute-start | bytes 1769480 | tf_op jit(solution)/shard_map/ppermute | solution.py:34
  25.1 13.6 %collective-permute-start.5 = (bf16[4,96,768]{2,1,0:T(8,128)(2,1)S(1)}, bf16[4,96,768]{2,1,0:T(8,128)(2,1)}, u32[]{:S(2)}, u32[]{:S(2)}) collective-permute-start(bf16[4,96,768]{2,1,0:T(8,128)(2,1)S(1)} %pad_maximum_fusion.refs_0_.g0), channel_id=1, source_target_pairs={{0,3},{1,0},{2,1},{3,2},{4,7},{5,4},{6,5},{7,6},{8,11},{9,8},{10,9... | collective-permute-start | bytes 1769480 | tf_op jit(solution)/shard_map/ppermute | solution.py:34
  26.0 19.5 %copy-start.1 = (bf16[1536,768]{1,0:T(8,128)(2,1)S(1)}, bf16[1536,768]{1,0:T(8,128)(2,1)}, u32[]{:S(2)}) copy-start(bf16[1536,768]{1,0:T(8,128)(2,1)} %refs_8_.3) | copy-start | bytes 7077892
  28.0 5.0 %collective-permute-start.6 = (bf16[2,48,1536]{2,1,0:T(8,128)(2,1)}, bf16[2,48,1536]{2,1,0:T(8,128)(2,1)}, u32[]{:S(2)}, u32[]{:S(2)}) collective-permute-start(bf16[2,48,1536]{2,1,0:T(8,128)(2,1)} %get-tuple-element.91), channel_id=1, source_target_pairs={{0,16},{1,17},{2,18},{3,19},{4,20},{5,21},{6,22},{7,23},{8,24},{9,... | collective-permute-start | bytes 884744 | tf_op jit(solution)/shard_map/ppermute | solution.py:34
  31.1 11.0 %collective-permute-start.9 = (bf16[4,96,768]{2,1,0:T(8,128)(2,1)S(1)}, bf16[4,96,768]{2,1,0:T(8,128)(2,1)S(1)}, u32[]{:S(2)}, u32[]{:S(2)}) collective-permute-start(bf16[4,96,768]{2,1,0:T(8,128)(2,1)S(1)} %pad_maximum_fusion.refs_0_.g0), channel_id=1, source_target_pairs={{0,16},{1,17},{2,18},{3,19},{4,20},{5,21},{6,22},{7,23},{8,24},{9,... | collective-permute-start | bytes 1769480 | tf_op jit(solution)/shard_map/ppermute | solution.py:34
  38.7 16.7 %copy-start.2 = (bf16[4,96,768]{2,1,0:T(8,128)(2,1)}, bf16[4,96,768]{2,1,0:T(8,128)(2,1)S(1)}, u32[]{:S(2)}) copy-start(bf16[4,96,768]{2,1,0:T(8,128)(2,1)S(1)} %collective-permute-done.8.refs_3_.g3) | copy-start | bytes 1769476
  38.7 4.6 %collective-permute-start.12 = (bf16[4,96,768]{2,1,0:T(8,128)(2,1)S(1)}, bf16[4,96,768]{2,1,0:T(8,128)(2,1)S(1)}, u32[]{:S(2)}, u32[]{:S(2)}) collective-permute-start(bf16[4,96,768]{2,1,0:T(8,128)(2,1)S(1)} %collective-permute-done.8.refs_3_.g3), channel_id=1, source_target_pairs={{0,16},{1,17},{2,18},{3,19},{4,20},{5,21},{6,22},{7,23},{8,24},{9,... | collective-permute-start | bytes 1769480 | tf_op jit(solution)/shard_map/ppermute | solution.py:34
  41.6 2.8 %collective-permute-start.11 = (bf16[4,96,768]{2,1,0:T(8,128)(2,1)}, bf16[4,96,768]{2,1,0:T(8,128)(2,1)S(1)}, u32[]{:S(2)}, u32[]{:S(2)}) collective-permute-start(bf16[4,96,768]{2,1,0:T(8,128)(2,1)} %collective-permute-done.7.refs_2_.g2), channel_id=1, source_target_pairs={{0,16},{1,17},{2,18},{3,19},{4,20},{5,21},{6,22},{7,23},{8,24},{9,... | collective-permute-start | bytes 1769480 | tf_op jit(solution)/shard_map/ppermute | solution.py:34
  42.0 3.5 %collective-permute-start.10 = (bf16[4,96,768]{2,1,0:T(8,128)(2,1)}, bf16[4,96,768]{2,1,0:T(8,128)(2,1)S(1)}, u32[]{:S(2)}, u32[]{:S(2)}) collective-permute-start(bf16[4,96,768]{2,1,0:T(8,128)(2,1)} %collective-permute-done.5.refs_1_.g1), channel_id=1, source_target_pairs={{0,16},{1,17},{2,18},{3,19},{4,20},{5,21},{6,22},{7,23},{8,24},{9,... | collective-permute-start | bytes 1769480 | tf_op jit(solution)/shard_map/ppermute | solution.py:34
  51.6 16.9 %collective-permute-start.13 = (bf16[192,1536]{1,0:T(8,128)(2,1)S(1)}, bf16[192,1536]{1,0:T(8,128)(2,1)S(1)}, u32[]{:S(2)}, u32[]{:S(2)}) collective-permute-start(bf16[192,1536]{1,0:T(8,128)(2,1)S(1)} %get-tuple-element.50), channel_id=1, source_target_pairs={{0,32},{1,33},{2,34},{3,35},{4,36},{5,37},{6,38},{7,39},{8,40},{9,... | collective-permute-start | bytes 1769480 | tf_op jit(solution)/shard_map/ppermute | solution.py:34
  53.8 14.6 %collective-permute-start.14 = (bf16[192,1536]{1,0:T(8,128)(2,1)S(1)}, bf16[192,1536]{1,0:T(8,128)(2,1)S(1)}, u32[]{:S(2)}, u32[]{:S(2)}) collective-permute-start(bf16[192,1536]{1,0:T(8,128)(2,1)S(1)} %get-tuple-element.51), channel_id=1, source_target_pairs={{0,96},{1,97},{2,98},{3,99},{4,100},{5,101},{6,102},{7,103},{8,104... | collective-permute-start | bytes 1769480 | tf_op jit(solution)/shard_map/ppermute | solution.py:34
  68.6 8.7 %collective-permute-start.15 = (bf16[96,1536]{1,0:T(8,128)(2,1)S(1)}, bf16[96,1536]{1,0:T(8,128)(2,1)S(1)}, u32[]{:S(2)}, u32[]{:S(2)}) collective-permute-start(bf16[96,1536]{1,0:T(8,128)(2,1)S(1)} %get-tuple-element.85), channel_id=1, source_target_pairs={{0,32},{1,33},{2,34},{3,35},{4,36},{5,37},{6,38},{7,39},{8,40},{9,... | collective-permute-start | bytes 884744 | tf_op jit(solution)/shard_map/ppermute | solution.py:34
  70.1 7.2 %collective-permute-start.16 = (bf16[96,1536]{1,0:T(8,128)(2,1)S(1)}, bf16[96,1536]{1,0:T(8,128)(2,1)S(1)}, u32[]{:S(2)}, u32[]{:S(2)}) collective-permute-start(bf16[96,1536]{1,0:T(8,128)(2,1)S(1)} %get-tuple-element.86), channel_id=1, source_target_pairs={{0,96},{1,97},{2,98},{3,99},{4,100},{5,101},{6,102},{7,103},{8,104... | collective-permute-start | bytes 884744 | tf_op jit(solution)/shard_map/ppermute | solution.py:34
  71.5 6.0 %copy-start.5 = (f32[4,48,1536]{2,1,0:T(8,128)S(1)}, f32[4,48,1536]{2,1,0:T(8,128)}, u32[]{:S(2)}) copy-start(f32[4,48,1536]{2,1,0:T(8,128)} %fusion.10) | copy-start | bytes 3538948
  77.7 12.5 %copy-start.7 = (bf16[4,48,1536]{2,1,0:T(8,128)(2,1)}, bf16[4,48,1536]{2,1,0:T(8,128)(2,1)S(1)}, u32[]{:S(2)}) copy-start(bf16[4,48,1536]{2,1,0:T(8,128)(2,1)S(1)} %multiply_convert_fusion.h0) | copy-start | bytes 1769476
  77.7 12.8 %collective-permute-start.18 = (bf16[4,48,1536]{2,1,0:T(8,128)(2,1)S(1)}, bf16[4,48,1536]{2,1,0:T(8,128)(2,1)S(1)}, u32[]{:S(2)}, u32[]{:S(2)}) collective-permute-start(bf16[4,48,1536]{2,1,0:T(8,128)(2,1)S(1)} %multiply_convert_fusion.h0), channel_id=1, source_target_pairs={{0,96},{1,97},{2,98},{3,99},{4,100},{5,101},{6,102},{7,103},{8,104... | collective-permute-start | bytes 1769480 | tf_op jit(solution)/shard_map/ppermute | solution.py:34
  80.1 13.4 %collective-permute-start.17 = (bf16[4,48,1536]{2,1,0:T(8,128)(2,1)S(1)}, bf16[4,48,1536]{2,1,0:T(8,128)(2,1)S(1)}, u32[]{:S(2)}, u32[]{:S(2)}) collective-permute-start(bf16[4,48,1536]{2,1,0:T(8,128)(2,1)S(1)} %multiply_convert_fusion.h0), channel_id=1, source_target_pairs={{0,32},{1,33},{2,34},{3,35},{4,36},{5,37},{6,38},{7,39},{8,40},{9,... | collective-permute-start | bytes 1769480 | tf_op jit(solution)/shard_map/ppermute | solution.py:34
  90.2 10.3 %copy-start.4 = (s32[4]{0:T(128)S(1)}, s32[4]{0:T(128)}, u32[]{:S(2)}) copy-start(s32[4]{0:T(128)} %copy-done.3) | copy-start | bytes 52
  90.5 10.0 %copy-start.8 = (bf16[4,48,1536]{2,1,0:T(8,128)(2,1)}, bf16[4,48,1536]{2,1,0:T(8,128)(2,1)S(1)}, u32[]{:S(2)}) copy-start(bf16[4,48,1536]{2,1,0:T(8,128)(2,1)S(1)} %collective-permute-done.18.h1) | copy-start | bytes 1769476
  93.6 6.9 %copy-start.9 = (bf16[4,48,1536]{2,1,0:T(8,128)(2,1)}, bf16[4,48,1536]{2,1,0:T(8,128)(2,1)S(1)}, u32[]{:S(2)}) copy-start(bf16[4,48,1536]{2,1,0:T(8,128)(2,1)S(1)} %collective-permute-done.17.h3) | copy-start | bytes 1769476
  93.6 6.9 %collective-permute-start.19 = (bf16[2,48,1536]{2,1,0:T(8,128)(2,1)S(1)}, bf16[2,48,1536]{2,1,0:T(8,128)(2,1)S(1)}, u32[]{:S(2)}, u32[]{:S(2)}) collective-permute-start(bf16[2,48,1536]{2,1,0:T(8,128)(2,1)S(1)} %slice.51), channel_id=1, source_target_pairs={{0,32},{1,33},{2,34},{3,35},{4,36},{5,37},{6,38},{7,39},{8,40},{9,... | collective-permute-start | bytes 884744 | tf_op jit(solution)/shard_map/ppermute | solution.py:34
  93.7 6.8 %collective-permute-start.20 = (bf16[2,48,1536]{2,1,0:T(8,128)(2,1)S(1)}, bf16[2,48,1536]{2,1,0:T(8,128)(2,1)S(1)}, u32[]{:S(2)}, u32[]{:S(2)}) collective-permute-start(bf16[2,48,1536]{2,1,0:T(8,128)(2,1)S(1)} %slice.52), channel_id=1, source_target_pairs={{0,96},{1,97},{2,98},{3,99},{4,100},{5,101},{6,102},{7,103},{8,104... | collective-permute-start | bytes 884744 | tf_op jit(solution)/shard_map/ppermute | solution.py:34
  110.0 9.3 %collective-permute-start.24 = (bf16[4,4,48,1536]{3,2,1,0:T(8,128)(2,1)}, bf16[4,4,48,1536]{3,2,1,0:T(8,128)(2,1)}, u32[]{:S(2)}, u32[]{:S(2)}) collective-permute-start(bf16[4,4,48,1536]{3,2,1,0:T(8,128)(2,1)} %get-tuple-element.77), channel_id=1, source_target_pairs={{0,16},{1,17},{2,18},{3,19},{4,20},{5,21},{6,22},{7,23},{8,24},{9,... | collective-permute-start | bytes 7077896 | tf_op jit(solution)/shard_map/ppermute | solution.py:34
  114.6 13.8 %collective-permute-start.21 = (bf16[4,48,1536]{2,1,0:T(8,128)(2,1)S(1)}, bf16[4,48,1536]{2,1,0:T(8,128)(2,1)S(1)}, u32[]{:S(2)}, u32[]{:S(2)}) collective-permute-start(bf16[4,48,1536]{2,1,0:T(8,128)(2,1)S(1)} %get-tuple-element.73), channel_id=1, source_target_pairs={{0,4},{1,5},{2,6},{3,7},{4,8},{5,9},{6,10},{7,11},{8,12},{9,13},{1... | collective-permute-start | bytes 1769480 | tf_op jit(solution)/shard_map/ppermute | solution.py:34
  116.6 11.8 %collective-permute-start.22 = (bf16[4,48,1536]{2,1,0:T(8,128)(2,1)}, bf16[4,48,1536]{2,1,0:T(8,128)(2,1)S(1)}, u32[]{:S(2)}, u32[]{:S(2)}) collective-permute-start(bf16[4,48,1536]{2,1,0:T(8,128)(2,1)} %get-tuple-element.74), channel_id=1, source_target_pairs={{0,12},{1,13},{2,14},{3,15},{4,0},{5,1},{6,2},{7,3},{8,4},{9,5},{1... | collective-permute-start | bytes 1769480 | tf_op jit(solution)/shard_map/ppermute | solution.py:34
  117.2 14.5 %collective-permute-start.23 = (bf16[4,48,1536]{2,1,0:T(8,128)(2,1)S(1)}, bf16[4,48,1536]{2,1,0:T(8,128)(2,1)S(1)}, u32[]{:S(2)}, u32[]{:S(2)}) collective-permute-start(bf16[4,48,1536]{2,1,0:T(8,128)(2,1)S(1)} %get-tuple-element.75), channel_id=1, source_target_pairs={{0,8},{1,9},{2,10},{3,11},{4,12},{5,13},{6,14},{7,15},{8,0},{9,1},... | collective-permute-start | bytes 1769480 | tf_op jit(solution)/shard_map/ppermute | solution.py:34
  119.2 12.5 %copy-start.10 = (f32[4,48,1536]{2,1,0:T(8,128)S(1)}, f32[4,48,1536]{2,1,0:T(8,128)}, u32[]{:S(2)}) copy-start(f32[4,48,1536]{2,1,0:T(8,128)} %get-tuple-element.72) | copy-start | bytes 3538948
  132.2 5.6 %collective-permute-start.25 = (bf16[48,1536]{1,0:T(8,128)(2,1)S(1)}, bf16[48,1536]{1,0:T(8,128)(2,1)S(1)}, u32[]{:S(2)}, u32[]{:S(2)}) collective-permute-start(bf16[48,1536]{1,0:T(8,128)(2,1)S(1)} %get-tuple-element.87), channel_id=1, source_target_pairs={{0,1},{1,2},{2,3},{3,0},{4,5},{5,6},{6,7},{7,4},{8,9},{9,10},{10,1... | collective-permute-start | bytes 442376 | tf_op jit(solution)/shard_map/ppermute | solution.py:34
  133.7 5.9 %collective-permute-start.27 = (bf16[48,1536]{1,0:T(8,128)(2,1)S(1)}, bf16[48,1536]{1,0:T(8,128)(2,1)S(1)}, u32[]{:S(2)}, u32[]{:S(2)}) collective-permute-start(bf16[48,1536]{1,0:T(8,128)(2,1)S(1)} %get-tuple-element.88), channel_id=1, source_target_pairs={{0,2},{1,3},{2,0},{3,1},{4,6},{5,7},{6,4},{7,5},{8,10},{9,11},{10,... | collective-permute-start | bytes 442376 | tf_op jit(solution)/shard_map/ppermute | solution.py:34
  135.2 4.7 %collective-permute-start.26 = (bf16[48,1536]{1,0:T(8,128)(2,1)S(1)}, bf16[48,1536]{1,0:T(8,128)(2,1)S(1)}, u32[]{:S(2)}, u32[]{:S(2)}) collective-permute-start(bf16[48,1536]{1,0:T(8,128)(2,1)S(1)} %get-tuple-element.89), channel_id=1, source_target_pairs={{0,3},{1,0},{2,1},{3,2},{4,7},{5,4},{6,5},{7,6},{8,11},{9,8},{10,9... | collective-permute-start | bytes 442376 | tf_op jit(solution)/shard_map/ppermute | solution.py:34
  140.0 2.9 %collective-permute-start.28 = (bf16[48,768]{1,0:T(8,128)(2,1)S(1)}, bf16[48,768]{1,0:T(8,128)(2,1)S(1)}, u32[]{:S(2)}, u32[]{:S(2)}) collective-permute-start(bf16[48,768]{1,0:T(8,128)(2,1)S(1)} %get-tuple-element.93), channel_id=1, source_target_pairs={{0,16},{1,17},{2,18},{3,19},{4,20},{5,21},{6,22},{7,23},{8,24},{9,... | collective-permute-start | bytes 221192 | tf_op jit(solution)/shard_map/ppermute | solution.py:34
Sparse Core Ops, SparseCore 0:
  9.7 38.1 all-gather.2
  71.5 45.0 all-gather.4
